TPU v7x, 32 devices: a whole 2x2x4 slice. The times are simulated.
32 devices in a mesh: nodes: 16 (over z, y, x), heads: 2 (over core).
Axes of the slice: x: 2, y: 2, z: 4, core: 2. Of those that a mesh axis runs over, the one named last changes fastest.
Arguments:
- inputs: bfloat16 [14336, 512], P('nodes', 'heads'), may hold values from -6 to 6
- w_query: bfloat16 [512, 512], P(None, 'heads'), may hold values from -0.375 to 0.375
- w_key: bfloat16 [512, 512], P(None, 'heads'), may hold values from -0.375 to 0.375
- w_value: bfloat16 [512, 512], P(None, 'heads'), may hold values from -0.25 to 0.25
- w_out: bfloat16 [512, 512], P('heads'), may hold values from -1 to 1
- w_up: bfloat16 [512, 2048], P(None, 'heads'), may hold values from -0.25 to 0.25
- w_down: bfloat16 [2048, 512], P('heads'), may hold values from -0.125 to 0.125
- mod_table: float32 [4, 16, 512], replicated, may hold values from -2.5 to 2.5
- level_ids: int32 [14336], P('nodes'), may hold values from 0 to 15
- neighbours: int32 [14336, 16], P('nodes'), may hold values from 0 to 14335, as said below
- cotangent: bfloat16 [14336, 512], P('nodes', 'heads'), may hold values from -6 to 6
Outputs:
- output: bfloat16 [14336, 512], P('nodes', 'heads')
- grad_inputs: float32 [14336, 512], P('nodes', 'heads')
- grad_query: float32 [512, 512], P(None, 'heads')
- grad_key: float32 [512, 512], P(None, 'heads')
- grad_value: float32 [512, 512], P(None, 'heads')
- grad_out: float32 [512, 512], P('heads')
- grad_up: float32 [512, 2048], P(None, 'heads')
- grad_down: float32 [2048, 512], P('heads')
- grad_table: float32 [4, 16, 512], P(None, None, 'heads')
Inputs may be any that keep to these rules, and one draw needn't show every extreme that they name: `neighbours`: each row holds 16 distinct node indices, none equal to the row's own node, each within 896 of it in the cyclic order of all 14336 nodes.
All inputs are finite; a program needn't handle non-finite values.
Results may differ from a plain program's by a relative error of at most 0.015.
Values may be sent and summed in bfloat16 or wider, within the bound.
No kernel may reach another device: no remote copies, remote signals or barrier semaphores. Data moves between devices by JAX's collectives and lax.ppermute only.
A program may use at most 128 MiB of HBM per device.

v0:
```python
import math

import jax
import jax.numpy as jnp
from jax import lax
from jax.sharding import PartitionSpec as P

HD = 128
K = 16
SPAN = 896


epsilon = 1e-05
highest = lax.Precision.HIGHEST


def extended(block, sides, width):
    for axis, dim in sides:
        count = lax.axis_size(axis)
        forward = [(i, i + 1) for i in range(count - 1)]
        forward.append((count - 1, 0))
        backward = [(target, source) for source, target in forward]
        low = lax.ppermute(
            lax.slice_in_dim(block, block.shape[dim] - width, None, axis=dim), axis, forward
        )
        high = lax.ppermute(lax.slice_in_dim(block, 0, width, axis=dim), axis, backward)
        block = jnp.concatenate([low, block, high], axis=dim)
    return block


def passed_along(block, axis, distance):
    devices = range(lax.axis_size(axis))
    route = [((i - distance) % len(devices), i) for i in devices]
    return lax.ppermute(block, axis, route)


def contract_rows(left, right, precision=None):
    return lax.dot_general(
        left,
        right,
        (((0,), (0,)), ((), ())),
        precision=precision,
        preferred_element_type=jnp.float32,
    )


def contract_cols(left, right):
    return lax.dot_general(
        left, right, (((1,), (1,)), ((), ())), preferred_element_type=jnp.float32
    )


def norm_full(values):
    row_mean = jnp.mean(values, axis=1, keepdims=True)
    centred = values - row_mean
    variance = jnp.mean(centred * centred, axis=1, keepdims=True)
    inverse = lax.rsqrt(variance + epsilon)
    return (centred * inverse, inverse)


def body(
    inputs,
    w_query,
    w_key,
    w_value,
    w_out,
    w_up,
    w_down,
    mod_table,
    level_ids,
    neighbours,
    cotangent,
):
    node_rows = inputs.shape[0]
    half = inputs.shape[1]
    width = half * lax.axis_size("heads")
    local_width = w_query.shape[1]
    head_count = local_width // HD
    column_first = lax.axis_index("heads") * half
    factor = 1.0 / math.sqrt(HD)
    onehot = (
        level_ids[:, None] == jnp.arange(mod_table.shape[1], dtype=jnp.int32)[None, :]
    ).astype(jnp.float32)

    def level_rows(which):
        return jnp.dot(onehot, mod_table[which], precision=highest)

    full_in = lax.all_gather(inputs, "heads", axis=1, tiled=True).astype(jnp.float32)
    normed1, inverse1 = norm_full(full_in)
    normed_one = (normed1 * (1.0 + level_rows(0)) + level_rows(1)).astype(jnp.bfloat16)
    queries = jnp.dot(normed_one, w_query, preferred_element_type=jnp.float32).astype(jnp.bfloat16)
    keys = jnp.dot(normed_one, w_key, preferred_element_type=jnp.float32).astype(jnp.bfloat16)
    values = jnp.dot(normed_one, w_value, preferred_element_type=jnp.float32).astype(jnp.bfloat16)
    key_value = jnp.concatenate([keys, values], axis=1)
    padded = extended(key_value, (("nodes", 0),), SPAN)
    node_count = node_rows * lax.axis_size("nodes")
    first_node = lax.axis_index("nodes") * node_rows
    local_index = jnp.mod(neighbours - first_node + SPAN, node_count)
    block_rows = math.gcd(node_rows, 128)
    block_count = node_rows // block_rows
    window_rows = block_rows + 2 * SPAN
    window_iota = jnp.arange(window_rows, dtype=jnp.int32)
    query_blocks = queries.reshape(block_count, block_rows, head_count, HD)
    index_blocks = local_index.reshape(block_count, block_rows, K)
    block_starts = jnp.arange(block_count, dtype=jnp.int32) * block_rows

    def selector(index_block, start):
        return index_block.reshape(block_rows * K, 1) - start == window_iota[None, :]

    def fetch(index_block, start):
        window = lax.dynamic_slice_in_dim(padded, start, window_rows, 0)
        picks = selector(index_block, start).astype(jnp.bfloat16)
        fetched = jnp.dot(picks, window, preferred_element_type=jnp.float32).astype(jnp.bfloat16)
        fetched = fetched.reshape(block_rows, K, 2 * local_width)
        key_block = fetched[:, :, :local_width].reshape(block_rows, K, head_count, HD)
        value_block = fetched[:, :, local_width:].reshape(block_rows, K, head_count, HD)
        return (key_block, value_block)

    def attend(operands):
        query_block, index_block, start = operands
        key_block, value_block = fetch(index_block, start)
        scores = (
            jnp.einsum("bhd,bkhd->bkh", query_block, key_block, preferred_element_type=jnp.float32)
            * factor
        )
        top_score = jnp.max(scores, axis=1, keepdims=True)
        weights = jnp.exp(scores - top_score)
        total = jnp.sum(weights, axis=1, keepdims=True)
        probs = weights / total
        mixed_block = jnp.einsum(
            "bkh,bkhd->bhd", probs, value_block.astype(jnp.float32), precision=highest
        )
        return (
            mixed_block.reshape(block_rows, local_width).astype(jnp.bfloat16),
            (top_score + jnp.log(total))[:, 0, :],
        )

    mixed_blocks, log_totals = lax.map(attend, (query_blocks, index_blocks, block_starts))
    mixed = mixed_blocks.reshape(node_rows, local_width)
    attn_share = lax.psum_scatter(
        jnp.dot(mixed, w_out, preferred_element_type=jnp.float32).astype(jnp.bfloat16),
        "heads",
        scatter_dimension=1,
        tiled=True,
    ).astype(jnp.float32)
    middle = inputs.astype(jnp.float32) + attn_share
    full_mid = lax.all_gather(middle.astype(jnp.bfloat16), "heads", axis=1, tiled=True).astype(
        middle.dtype
    )
    normed2, inverse2 = norm_full(full_mid)
    normed_two = (normed2 * (1.0 + level_rows(2)) + level_rows(3)).astype(jnp.bfloat16)
    pre_act = jnp.dot(normed_two, w_up, preferred_element_type=jnp.float32)
    activated = jax.nn.silu(pre_act).astype(jnp.bfloat16)
    mlp_share = lax.psum_scatter(
        jnp.dot(activated, w_down, preferred_element_type=jnp.float32).astype(jnp.bfloat16),
        "heads",
        scatter_dimension=1,
        tiled=True,
    ).astype(jnp.float32)
    output = (middle + mlp_share).astype(jnp.bfloat16)

    def norm_back(grad_share, normed_whole, inverse, which):
        normed_share = lax.dynamic_slice_in_dim(normed_whole, column_first, half, 1)
        scale_table = lax.dynamic_slice_in_dim(mod_table[2 * which], column_first, half, 1)
        scale_share = jnp.dot(onehot, scale_table, precision=highest)
        gained = grad_share * (1.0 + scale_share)
        sum_gain, sum_cross = lax.psum(
            (jnp.sum(gained, axis=1), jnp.sum(gained * normed_share, axis=1)), "heads"
        )
        grad_in = inverse * (
            gained - sum_gain[:, None] / width - normed_share * sum_cross[:, None] / width
        )
        grad_scale = contract_rows(onehot, grad_share * normed_share, highest)
        grad_shift = contract_rows(onehot, grad_share, highest)
        return (grad_in, grad_scale, grad_shift)

    full_cot = lax.all_gather(cotangent, "heads", axis=1, tiled=True)
    grad_down = contract_rows(activated, full_cot)
    grad_act = contract_cols(full_cot, w_down)
    sigma = jax.nn.sigmoid(pre_act)
    grad_pre = (grad_act * sigma * (1.0 + pre_act * (1.0 - sigma))).astype(jnp.bfloat16)
    grad_up = contract_rows(normed_two, grad_pre)
    grad_two = lax.psum_scatter(
        contract_cols(grad_pre, w_up).astype(jnp.bfloat16), "heads", scatter_dimension=1, tiled=True
    ).astype(jnp.float32)
    grad_in2, scale_two, shift_two = norm_back(grad_two, normed2, inverse2, 1)
    grad_mid = cotangent.astype(jnp.float32) + grad_in2
    grad_branch = lax.all_gather(grad_mid.astype(jnp.bfloat16), "heads", axis=1, tiled=True)
    grad_out = contract_rows(mixed, grad_branch)
    grad_mixed = contract_cols(grad_branch, w_out)

    def attend_back(carry, operands):
        query_block, index_block, grad_block, log_block, start = operands
        key_block, value_block = fetch(index_block, start)
        scores = (
            jnp.einsum("bhd,bkhd->bkh", query_block, key_block, preferred_element_type=jnp.float32)
            * factor
        )
        probs = jnp.exp(scores - log_block[:, None, :])
        grad_heads = grad_block.reshape(block_rows, head_count, HD)
        grad_probs = jnp.einsum(
            "bhd,bkhd->bkh", grad_heads, value_block.astype(jnp.float32), precision=highest
        )
        grad_scores = probs * (grad_probs - jnp.sum(probs * grad_probs, axis=1, keepdims=True))
        grad_query_block = (
            jnp.einsum(
                "bkh,bkhd->bhd", grad_scores, key_block.astype(jnp.float32), precision=highest
            )
            * factor
        )
        grad_key_block = (
            jnp.einsum(
                "bkh,bhd->bkhd", grad_scores, query_block.astype(jnp.float32), precision=highest
            )
            * factor
        )
        grad_value_block = jnp.einsum("bkh,bhd->bkhd", probs, grad_heads, precision=highest)
        joined = jnp.concatenate(
            [
                grad_key_block.reshape(block_rows, K, local_width),
                grad_value_block.reshape(block_rows, K, local_width),
            ],
            axis=2,
        )
        picks = selector(index_block, start).astype(jnp.float32)
        spread = contract_rows(picks, joined.reshape(block_rows * K, 2 * local_width), highest)
        current = lax.dynamic_slice_in_dim(carry, start, window_rows, 0)
        carry = lax.dynamic_update_slice_in_dim(carry, current + spread, start, 0)
        return (carry, grad_query_block.reshape(block_rows, local_width))

    start_pad = jnp.zeros((node_rows + 2 * SPAN, 2 * local_width), jnp.float32)
    grad_pad, grad_query_blocks = lax.scan(
        attend_back,
        start_pad,
        (
            query_blocks,
            index_blocks,
            grad_mixed.reshape(block_count, block_rows, local_width),
            log_totals,
            block_starts,
        ),
    )
    from_above = passed_along(grad_pad[:SPAN].astype(jnp.bfloat16), "nodes", -1).astype(jnp.float32)
    from_below = passed_along(grad_pad[node_rows + SPAN :].astype(jnp.bfloat16), "nodes", 1).astype(
        jnp.float32
    )
    grad_centre = grad_pad[SPAN : SPAN + node_rows]
    grad_centre = grad_centre.at[:SPAN].add(from_below)
    grad_centre = grad_centre.at[node_rows - SPAN :].add(from_above)
    grad_keys = grad_centre[:, :local_width].astype(jnp.bfloat16)
    grad_values = grad_centre[:, local_width:].astype(jnp.bfloat16)
    grad_queries = grad_query_blocks.reshape(node_rows, local_width).astype(jnp.bfloat16)
    grad_query = contract_rows(normed_one, grad_queries)
    grad_key = contract_rows(normed_one, grad_keys)
    grad_value = contract_rows(normed_one, grad_values)
    grad_joined = jnp.concatenate([grad_queries, grad_keys, grad_values], axis=1)
    weights_joined = jnp.concatenate([w_query, w_key, w_value], axis=1)
    grad_one = lax.psum_scatter(
        contract_cols(grad_joined, weights_joined).astype(jnp.bfloat16),
        "heads",
        scatter_dimension=1,
        tiled=True,
    ).astype(jnp.float32)
    grad_in1, scale_one, shift_one = norm_back(grad_one, normed1, inverse1, 0)
    grad_inputs = grad_mid + grad_in1
    grad_table = jnp.stack([scale_one, shift_one, scale_two, shift_two])
    up_total, down_total, query_total, key_total, value_total, out_total, table_total = lax.psum(
        (grad_up, grad_down, grad_query, grad_key, grad_value, grad_out, grad_table), "nodes"
    )
    return (
        output,
        grad_inputs,
        query_total,
        key_total,
        value_total,
        out_total,
        up_total,
        down_total,
        table_total,
    )


def solution(mesh):
    return jax.shard_map(
        body,
        mesh=mesh,
        in_specs=(
            P("nodes", "heads"),
            P(None, "heads"),
            P(None, "heads"),
            P(None, "heads"),
            P("heads", None),
            P(None, "heads"),
            P("heads", None),
            P(),
            P("nodes"),
            P("nodes", None),
            P("nodes", "heads"),
        ),
        out_specs=(
            P("nodes", "heads"),
            P("nodes", "heads"),
            P(None, "heads"),
            P(None, "heads"),
            P(None, "heads"),
            P("heads", None),
            P(None, "heads"),
            P("heads", None),
            P(None, None, "heads"),
        ),
        check_vma=False,
    )
```

profile of v0, /device:TPU:0, one launch (start us, length us, event | category | flops | bytes accessed | tf_op | source)
XLA Modules:
  0.0 920.6 jit_solution(9868743078367835547)
XLA Ops:
  15.5 6.8 collective-permute-start.1
  26.9 15.7 %collective-permute-done.1 = bf16[896,512]{0,1:T(8,128)(2,1)} collective-permute-done((bf16[896,512]{0,1:T(8,128)(2,1)}, bf16[896,512]{0,1:T(8,128)(2,1)}, u32[]{:S(2)}, u32[]{:S(2)}) %collective-permute-start.1) | collective-permute-done | bytes 917536 | tf_op jit(solution)/shard_map/ppermute | solution.py:26
  42.5 17.5 %collective-permute-done = bf16[896,512]{0,1:T(8,128)(2,1)} collective-permute-done((bf16[896,512]{0,1:T(8,128)(2,1)}, bf16[896,512]{0,1:T(8,128)(2,1)}, u32[]{:S(2)}, u32[]{:S(2)}) %collective-permute-start) | collective-permute-done | bytes 917536 | tf_op jit(solution)/shard_map/ppermute | solution.py:23
  60.1 9.0 pad_maximum_fusion
  73.7 90.9 %while.30 = (s32[]{:T(128)}, bf16[7,128,256]{2,1,0:T(8,128)(2,1)S(1)}, f32[7,128,2]{1,2,0:T(2,128)S(1)}, s32[7,128,16]{2,1,0:T(8,128)S(1)}, s32[7]{0:T(128)S(1)}...) while((s32[]{:T(128)}, ...), condition=%wide.region_5.6_spmd.clone, body=%wide.region_2.5_spmd.clone.sunk | while | flops 4038919936 | bytes 11354291 | solution.py:138
  77.9 6.4 fusion.173
  90.9 6.4 fusion.173
  129.8 6.4 fusion.173
  142.8 6.4 fusion.173
  192.9 7.5 reduce-scatter.9.cloned.1.call-done
  213.4 391.9 %while.31 = (s32[]{:T(128)}, f32[2688,512]{1,0:T(8,128)}, bf16[7,128,256]{2,1,0:T(8,128)(2,1)}, s32[7]{0:T(128)S(1)}, s32[7,128,16]{2,1,0:T(8,128)S(1)}, /*index...) while((s32[]{:T(128)}, f32[2688,512]{1,0:T(8,128)}, ...), condition=%wide.region_17.18_spmd.clone, body=%wide.region_15.17_spmd.clone.sunk | while | flops 28211992576 | bytes 74831536 | solution.py:232
  218.2 6.4 fusion.185
  242.6 15.5 %dynamic-slice_add_fusion.2 = f32[1920,512]{1,0:T(8,128)} fusion(f32[2688,512]{1,0:T(8,128)S(1)} %bitcast.243, s32[]{:T(128)S(6)} %select_n.29, f32[2048,256]{1,0:T(8,128)S(1)} %get-tuple-element.410, f32[2048,256]{1,0:T(8,128)S(1)} %get-tuple-element.411, s32[2048]{0:T(1024)S(1)} %sub.215), kind=kOutput, calls=%fused_computation.36.clone.1 | convolution fusion | flops 24165154816 | bytes 12066820 | tf_op jit(solution)/shard_map/while/body/eval_jaxpr/dot_general | solution.py:38
  258.1 11.4 %dynamic_update_slice.29 = f32[2688,512]{1,0:T(8,128)} dynamic-update-slice(f32[2688,512]{1,0:T(8,128)} %get-tuple-element.455, f32[1920,512]{1,0:T(8,128)} %dynamic-slice_add_fusion.2, s32[]{:T(128)S(6)} %select_n.29, s32[]{:T(128)} %constant.159.clone.1..sunk.1) | dynamic-update-slice | bytes 7864324 | tf_op jit(solution)/shard_map/while/body/eval_jaxpr/dynamic_update_slice | solution.py:228
  274.2 6.4 fusion.185
  298.6 15.5 %dynamic-slice_add_fusion.2 = f32[1920,512]{1,0:T(8,128)} fusion(f32[2688,512]{1,0:T(8,128)S(1)} %bitcast.243, s32[]{:T(128)S(6)} %select_n.29, f32[2048,256]{1,0:T(8,128)S(1)} %get-tuple-element.410, f32[2048,256]{1,0:T(8,128)S(1)} %get-tuple-element.411, s32[2048]{0:T(1024)S(1)} %sub.215), kind=kOutput, calls=%fused_computation.36.clone.1 | convolution fusion | flops 24165154816 | bytes 12066820 | tf_op jit(solution)/shard_map/while/body/eval_jaxpr/dot_general | solution.py:38
  314.1 11.4 %dynamic_update_slice.29 = f32[2688,512]{1,0:T(8,128)} dynamic-update-slice(f32[2688,512]{1,0:T(8,128)} %get-tuple-element.455, f32[1920,512]{1,0:T(8,128)} %dynamic-slice_add_fusion.2, s32[]{:T(128)S(6)} %select_n.29, s32[]{:T(128)} %constant.159.clone.1..sunk.1) | dynamic-update-slice | bytes 7864324 | tf_op jit(solution)/shard_map/while/body/eval_jaxpr/dynamic_update_slice | solution.py:228
  354.6 15.5 %dynamic-slice_add_fusion.2 = f32[1920,512]{1,0:T(8,128)} fusion(f32[2688,512]{1,0:T(8,128)S(1)} %bitcast.243, s32[]{:T(128)S(6)} %select_n.29, f32[2048,256]{1,0:T(8,128)S(1)} %get-tuple-element.410, f32[2048,256]{1,0:T(8,128)S(1)} %get-tuple-element.411, s32[2048]{0:T(1024)S(1)} %sub.215), kind=kOutput, calls=%fused_computation.36.clone.1 | convolution fusion | flops 24165154816 | bytes 12066820 | tf_op jit(solution)/shard_map/while/body/eval_jaxpr/dot_general | solution.py:38
  370.1 11.4 %dynamic_update_slice.29 = f32[2688,512]{1,0:T(8,128)} dynamic-update-slice(f32[2688,512]{1,0:T(8,128)} %get-tuple-element.455, f32[1920,512]{1,0:T(8,128)} %dynamic-slice_add_fusion.2, s32[]{:T(128)S(6)} %select_n.29, s32[]{:T(128)} %constant.159.clone.1..sunk.1) | dynamic-update-slice | bytes 7864324 | tf_op jit(solution)/shard_map/while/body/eval_jaxpr/dynamic_update_slice | solution.py:228
  386.2 6.4 fusion.185
  410.6 15.5 %dynamic-slice_add_fusion.2 = f32[1920,512]{1,0:T(8,128)} fusion(f32[2688,512]{1,0:T(8,128)S(1)} %bitcast.243, s32[]{:T(128)S(6)} %select_n.29, f32[2048,256]{1,0:T(8,128)S(1)} %get-tuple-element.410, f32[2048,256]{1,0:T(8,128)S(1)} %get-tuple-element.411, s32[2048]{0:T(1024)S(1)} %sub.215), kind=kOutput, calls=%fused_computation.36.clone.1 | convolution fusion | flops 24165154816 | bytes 12066820 | tf_op jit(solution)/shard_map/while/body/eval_jaxpr/dot_general | solution.py:38
  426.1 11.4 %dynamic_update_slice.29 = f32[2688,512]{1,0:T(8,128)} dynamic-update-slice(f32[2688,512]{1,0:T(8,128)} %get-tuple-element.455, f32[1920,512]{1,0:T(8,128)} %dynamic-slice_add_fusion.2, s32[]{:T(128)S(6)} %select_n.29, s32[]{:T(128)} %constant.159.clone.1..sunk.1) | dynamic-update-slice | bytes 7864324 | tf_op jit(solution)/shard_map/while/body/eval_jaxpr/dynamic_update_slice | solution.py:228
  442.2 6.4 fusion.185
  466.7 15.5 %dynamic-slice_add_fusion.2 = f32[1920,512]{1,0:T(8,128)} fusion(f32[2688,512]{1,0:T(8,128)S(1)} %bitcast.243, s32[]{:T(128)S(6)} %select_n.29, f32[2048,256]{1,0:T(8,128)S(1)} %get-tuple-element.410, f32[2048,256]{1,0:T(8,128)S(1)} %get-tuple-element.411, s32[2048]{0:T(1024)S(1)} %sub.215), kind=kOutput, calls=%fused_computation.36.clone.1 | convolution fusion | flops 24165154816 | bytes 12066820 | tf_op jit(solution)/shard_map/while/body/eval_jaxpr/dot_general | solution.py:38
  482.1 11.4 %dynamic_update_slice.29 = f32[2688,512]{1,0:T(8,128)} dynamic-update-slice(f32[2688,512]{1,0:T(8,128)} %get-tuple-element.455, f32[1920,512]{1,0:T(8,128)} %dynamic-slice_add_fusion.2, s32[]{:T(128)S(6)} %select_n.29, s32[]{:T(128)} %constant.159.clone.1..sunk.1) | dynamic-update-slice | bytes 7864324 | tf_op jit(solution)/shard_map/while/body/eval_jaxpr/dynamic_update_slice | solution.py:228
  498.2 6.4 fusion.185
  522.7 15.5 %dynamic-slice_add_fusion.2 = f32[1920,512]{1,0:T(8,128)} fusion(f32[2688,512]{1,0:T(8,128)S(1)} %bitcast.243, s32[]{:T(128)S(6)} %select_n.29, f32[2048,256]{1,0:T(8,128)S(1)} %get-tuple-element.410, f32[2048,256]{1,0:T(8,128)S(1)} %get-tuple-element.411, s32[2048]{0:T(1024)S(1)} %sub.215), kind=kOutput, calls=%fused_computation.36.clone.1 | convolution fusion | flops 24165154816 | bytes 12066820 | tf_op jit(solution)/shard_map/while/body/eval_jaxpr/dot_general | solution.py:38
  538.1 11.4 %dynamic_update_slice.29 = f32[2688,512]{1,0:T(8,128)} dynamic-update-slice(f32[2688,512]{1,0:T(8,128)} %get-tuple-element.455, f32[1920,512]{1,0:T(8,128)} %dynamic-slice_add_fusion.2, s32[]{:T(128)S(6)} %select_n.29, s32[]{:T(128)} %constant.159.clone.1..sunk.1) | dynamic-update-slice | bytes 7864324 | tf_op jit(solution)/shard_map/while/body/eval_jaxpr/dynamic_update_slice | solution.py:228
  578.6 15.5 %dynamic-slice_add_fusion.2 = f32[1920,512]{1,0:T(8,128)} fusion(f32[2688,512]{1,0:T(8,128)S(1)} %bitcast.243, s32[]{:T(128)S(6)} %select_n.29, f32[2048,256]{1,0:T(8,128)S(1)} %get-tuple-element.410, f32[2048,256]{1,0:T(8,128)S(1)} %get-tuple-element.411, s32[2048]{0:T(1024)S(1)} %sub.215), kind=kOutput, calls=%fused_computation.36.clone.1 | convolution fusion | flops 24165154816 | bytes 12066820 | tf_op jit(solution)/shard_map/while/body/eval_jaxpr/dot_general | solution.py:38
  594.1 10.9 %dynamic_update_slice.29 = f32[2688,512]{1,0:T(8,128)} dynamic-update-slice(f32[2688,512]{1,0:T(8,128)} %get-tuple-element.455, f32[1920,512]{1,0:T(8,128)} %dynamic-slice_add_fusion.2, s32[]{:T(128)S(6)} %select_n.29, s32[]{:T(128)} %constant.159.clone.1..sunk.1) | dynamic-update-slice | bytes 7864324 | tf_op jit(solution)/shard_map/while/body/eval_jaxpr/dynamic_update_slice | solution.py:228
  614.0 35.9 %collective-permute-done.2 = bf16[896,512]{1,0:T(8,128)(2,1)S(1)} collective-permute-done((bf16[896,512]{1,0:T(8,128)(2,1)S(1)}, bf16[896,512]{1,0:T(8,128)(2,1)S(1)}, u32[]{:S(2)}, u32[]{:S(2)}) %collective-permute-start.2) | collective-permute-done | bytes 917536 | tf_op jit(solution)/shard_map/ppermute | solution.py:34
  689.5 214.4 %all-reduce.5.cloned.1.call-done = (f32[512,256]{1,0:T(8,128)}, f32[512,256]{1,0:T(8,128)}, f32[512,256]{1,0:T(8,128)}, f32[256,512]{1,0:T(8,128)}, f32[512,1024...) async-done(((f32[512,256]{1,0:T(8,128)}, f32[512,256]{1,0:T(8,128)}, f32[512,256]{1,0:T(8,128)}, f32[256,512]{1,0:T(8,128)}, f32[512,1024]{1,0:T(8,128)}, ...) | async-done | bytes 6357008 | tf_op jit(solution)/shard_map/psum | solution.py:267
  (607 shorter events, 324.6 us)
Async XLA Ops:
  7.2 175.5 %copy-start = (bf16[512,1024]{1,0:T(8,128)(2,1)S(1)}, bf16[512,1024]{1,0:T(8,128)(2,1)}, u32[]{:S(2)}) copy-start(bf16[512,1024]{1,0:T(8,128)(2,1)} %param.28) | copy-start | bytes 3145732
  7.2 169.0 %reduce-scatter.5.cloned.1.call-start = ((), (), s32[]{:S(2)}) async-start(), calls=%async_computation.4 | async-start | bytes 1376256 | tf_op jit(solution)/shard_map/reduce_scatter | solution.py:140
  15.5 27.1 %collective-permute-start.1 = (bf16[896,512]{0,1:T(8,128)(2,1)}, bf16[896,512]{0,1:T(8,128)(2,1)}, u32[]{:S(2)}, u32[]{:S(2)}) collective-permute-start(bf16[896,512]{0,1:T(8,128)(2,1)} %pad_maximum_fusion.1), channel_id=1, source_target_pairs={{2,0},{4,2},{6,4},{8,6},{10,8},{12,10},{14,12},{16,14},{18,16},{20... | collective-permute-start | bytes 2752520 | tf_op jit(solution)/shard_map/ppermute | solution.py:26
  22.3 37.7 %collective-permute-start = (bf16[896,512]{0,1:T(8,128)(2,1)}, bf16[896,512]{0,1:T(8,128)(2,1)}, u32[]{:S(2)}, u32[]{:S(2)}) collective-permute-start(bf16[896,512]{0,1:T(8,128)(2,1)} %pad_maximum_fusion.1), channel_id=1, source_target_pairs={{0,2},{2,4},{4,6},{6,8},{8,10},{10,12},{12,14},{14,16},{16,18},{18... | collective-permute-start | bytes 2752520 | tf_op jit(solution)/shard_map/ppermute | solution.py:23
  167.1 33.2 %reduce-scatter.9.cloned.1.call-start = ((), (), s32[]{:S(2)}) async-start(), calls=%async_computation.6 | async-start | bytes 1376256 | tf_op jit(solution)/shard_map/reduce_scatter | solution.py:183
  190.7 485.0 %reduce-scatter.11.cloned.1.call-start = ((), (), s32[]{:S(2)}) async-start(), calls=%async_computation.7 | async-start | bytes 1376256 | tf_op jit(solution)/shard_map/reduce_scatter | solution.py:258
  192.9 12.0 %copy-start.7 = (f32[896,512]{1,0:T(8,128)S(1)}, f32[896,512]{1,0:T(8,128)}, u32[]{:S(2)}) copy-start(f32[896,512]{1,0:T(8,128)} %fusion.51) | copy-start | bytes 5505028
  258.1 11.4 %copy-start.20 = (s32[7,128,16]{2,1,0:T(8,128)S(1)}, s32[7,128,16]{2,1,0:T(8,128)}, u32[]{:S(2)}) copy-start(s32[7,128,16]{2,1,0:T(8,128)} %copy-done.19) | copy-start | bytes 172036 | tf_op jit(solution)/shard_map/while
  258.1 11.4 %copy-start.22 = (f32[7,128,256]{2,1,0:T(8,128)S(1)}, f32[7,128,256]{2,1,0:T(8,128)}, u32[]{:S(2)}) copy-start(f32[7,128,256]{2,1,0:T(8,128)} %copy-done.21) | copy-start | bytes 2752516 | tf_op jit(solution)/shard_map/while
  258.1 11.4 %copy-start.57 = (s32[7]{0:T(128)S(1)}, s32[7]{0:T(128)}, u32[]{:S(2)}) copy-start(s32[7]{0:T(128)} %copy-done.56) | copy-start | bytes 88 | tf_op jit(solution)/shard_map/while
  314.1 11.4 %copy-start.20 = (s32[7,128,16]{2,1,0:T(8,128)S(1)}, s32[7,128,16]{2,1,0:T(8,128)}, u32[]{:S(2)}) copy-start(s32[7,128,16]{2,1,0:T(8,128)} %copy-done.19) | copy-start | bytes 172036 | tf_op jit(solution)/shard_map/while
  314.1 11.4 %copy-start.22 = (f32[7,128,256]{2,1,0:T(8,128)S(1)}, f32[7,128,256]{2,1,0:T(8,128)}, u32[]{:S(2)}) copy-start(f32[7,128,256]{2,1,0:T(8,128)} %copy-done.21) | copy-start | bytes 2752516 | tf_op jit(solution)/shard_map/while
  314.1 11.4 %copy-start.57 = (s32[7]{0:T(128)S(1)}, s32[7]{0:T(128)}, u32[]{:S(2)}) copy-start(s32[7]{0:T(128)} %copy-done.56) | copy-start | bytes 88 | tf_op jit(solution)/shard_map/while
  370.1 11.4 %copy-start.22 = (f32[7,128,256]{2,1,0:T(8,128)S(1)}, f32[7,128,256]{2,1,0:T(8,128)}, u32[]{:S(2)}) copy-start(f32[7,128,256]{2,1,0:T(8,128)} %copy-done.21) | copy-start | bytes 2752516 | tf_op jit(solution)/shard_map/while
  370.1 11.4 %copy-start.57 = (s32[7]{0:T(128)S(1)}, s32[7]{0:T(128)}, u32[]{:S(2)}) copy-start(s32[7]{0:T(128)} %copy-done.56) | copy-start | bytes 88 | tf_op jit(solution)/shard_map/while
  426.1 11.4 %copy-start.20 = (s32[7,128,16]{2,1,0:T(8,128)S(1)}, s32[7,128,16]{2,1,0:T(8,128)}, u32[]{:S(2)}) copy-start(s32[7,128,16]{2,1,0:T(8,128)} %copy-done.19) | copy-start | bytes 172036 | tf_op jit(solution)/shard_map/while
  426.1 11.4 %copy-start.22 = (f32[7,128,256]{2,1,0:T(8,128)S(1)}, f32[7,128,256]{2,1,0:T(8,128)}, u32[]{:S(2)}) copy-start(f32[7,128,256]{2,1,0:T(8,128)} %copy-done.21) | copy-start | bytes 2752516 | tf_op jit(solution)/shard_map/while
  426.1 11.4 %copy-start.57 = (s32[7]{0:T(128)S(1)}, s32[7]{0:T(128)}, u32[]{:S(2)}) copy-start(s32[7]{0:T(128)} %copy-done.56) | copy-start | bytes 88 | tf_op jit(solution)/shard_map/while
  482.1 11.4 %copy-start.20 = (s32[7,128,16]{2,1,0:T(8,128)S(1)}, s32[7,128,16]{2,1,0:T(8,128)}, u32[]{:S(2)}) copy-start(s32[7,128,16]{2,1,0:T(8,128)} %copy-done.19) | copy-start | bytes 172036 | tf_op jit(solution)/shard_map/while
  482.1 11.4 %copy-start.22 = (f32[7,128,256]{2,1,0:T(8,128)S(1)}, f32[7,128,256]{2,1,0:T(8,128)}, u32[]{:S(2)}) copy-start(f32[7,128,256]{2,1,0:T(8,128)} %copy-done.21) | copy-start | bytes 2752516 | tf_op jit(solution)/shard_map/while
  482.1 11.4 %copy-start.57 = (s32[7]{0:T(128)S(1)}, s32[7]{0:T(128)}, u32[]{:S(2)}) copy-start(s32[7]{0:T(128)} %copy-done.56) | copy-start | bytes 88 | tf_op jit(solution)/shard_map/while
  538.1 11.4 %copy-start.20 = (s32[7,128,16]{2,1,0:T(8,128)S(1)}, s32[7,128,16]{2,1,0:T(8,128)}, u32[]{:S(2)}) copy-start(s32[7,128,16]{2,1,0:T(8,128)} %copy-done.19) | copy-start | bytes 172036 | tf_op jit(solution)/shard_map/while
  538.1 11.4 %copy-start.22 = (f32[7,128,256]{2,1,0:T(8,128)S(1)}, f32[7,128,256]{2,1,0:T(8,128)}, u32[]{:S(2)}) copy-start(f32[7,128,256]{2,1,0:T(8,128)} %copy-done.21) | copy-start | bytes 2752516 | tf_op jit(solution)/shard_map/while
  538.1 11.4 %copy-start.57 = (s32[7]{0:T(128)S(1)}, s32[7]{0:T(128)}, u32[]{:S(2)}) copy-start(s32[7]{0:T(128)} %copy-done.56) | copy-start | bytes 88 | tf_op jit(solution)/shard_map/while
  608.3 41.6 %collective-permute-start.2 = (bf16[896,512]{1,0:T(8,128)(2,1)S(1)}, bf16[896,512]{1,0:T(8,128)(2,1)S(1)}, u32[]{:S(2)}, u32[]{:S(2)}) collective-permute-start(bf16[896,512]{1,0:T(8,128)(2,1)S(1)} %get-tuple-element.290), channel_id=1, source_target_pairs={{30,0},{0,2},{2,4},{4,6},{6,8},{8,10},{10,12},{12,14},{14,16},{16,... | collective-permute-start | bytes 2752520 | tf_op jit(solution)/shard_map/ppermute | solution.py:34
  610.1 44.5 %copy-start.42 = (bf16[512,256]{1,0:T(8,128)(2,1)S(1)}, bf16[512,256]{1,0:T(8,128)(2,1)}, u32[]{:S(2)}) copy-start(bf16[512,256]{1,0:T(8,128)(2,1)} %param.26) | copy-start | bytes 786436
  610.1 44.5 %copy-start.44 = (bf16[512,256]{1,0:T(8,128)(2,1)S(1)}, bf16[512,256]{1,0:T(8,128)(2,1)}, u32[]{:S(2)}) copy-start(bf16[512,256]{1,0:T(8,128)(2,1)} %param.25) | copy-start | bytes 786436
  610.1 44.5 %copy-start.45 = (bf16[512,256]{1,0:T(8,128)(2,1)S(1)}, bf16[512,256]{1,0:T(8,128)(2,1)}, u32[]{:S(2)}) copy-start(bf16[512,256]{1,0:T(8,128)(2,1)} %param.24) | copy-start | bytes 786436
  610.1 44.5 %copy-start.54 = (bf16[7,128,256]{2,1,0:T(8,128)(2,1)S(1)}, bf16[7,128,256]{2,1,0:T(8,128)(2,1)}, u32[]{:S(2)}) copy-start(bf16[7,128,256]{2,1,0:T(8,128)(2,1)} %get-tuple-element.147) | copy-start | bytes 1376260
  610.1 41.7 %collective-permute-start.3 = (bf16[896,512]{1,0:T(8,128)(2,1)S(1)}, bf16[896,512]{1,0:T(8,128)(2,1)S(1)}, u32[]{:S(2)}, u32[]{:S(2)}) collective-permute-start(bf16[896,512]{1,0:T(8,128)(2,1)S(1)} %get-tuple-element.291), channel_id=1, source_target_pairs={{2,0},{4,2},{6,4},{8,6},{10,8},{12,10},{14,12},{16,14},{18,16},{20... | collective-permute-start | bytes 2752520 | tf_op jit(solution)/shard_map/ppermute | solution.py:34
  656.6 23.0 %reduce-scatter.7.cloned.1.call-start = ((), (), s32[]{:S(2)}) async-start(), calls=%async_computation.5 | async-start | bytes 1376256 | tf_op jit(solution)/shard_map/reduce_scatter | solution.py:154
  664.9 239.1 %all-reduce.5.cloned.1.call-start = ((), (), s32[]{:S(2)}) async-start(), calls=%async_computation.8 | async-start | bytes 12713984 | tf_op jit(solution)/shard_map/psum | solution.py:267
  (91 other events, 439.7 us)
Sparse Core Ops, SparseCore 0:
  167.3 8.8 reduce-scatter.4
  190.8 9.5 reduce-scatter.8
  656.7 8.3 reduce-scatter.10
  667.8 9.5 reduce-scatter.6
  684.9 218.9 all-reduce.4
where the time goes:
time: 928 us; the launch traced here: 921 us
  waiting for transfers between devices  297 us (32%)
  matrix products  286 us (31%)
  local copies, waits for them, and re-layouts  159 us (17%)
  other arithmetic  105 us (11%)
  loops' own time  29.8 us (3%)
  blocking collectives  15.9 us (2%)
  between operations  14.8 us (2%)
  starting transfers between devices  13 us (1%)
    psum x1, waiting for transfers between devices, body(): lax.psum((grad_up, grad_down, grad_query, grad_key, grad_value, grad_out,...  214 us
    dot_general x17, matrix products, contract_rows(): lax.dot_general(left, right, (((0,), (0,)), ((), ())), precision=precisio...  125 us
    dot_general x14, matrix products, fetch(): jnp.dot(picks, window, preferred_element_type=jnp.float32)  89.1 us
    dynamic_update_slice x7, local copies, waits for them, and re-layouts, attend_back(): carry = lax.dynamic_update_slice_in_dim(carry, current + spread, start, 0)  79.2 us
    ppermute x2, waiting for transfers between devices, passed_along(): return lax.ppermute(block, axis, route)  37.8 us
    mul x7, other arithmetic, attend_back(): jnp.einsum('bkh,bhd->bkhd', grad_scores, query_block.astype(jnp.float32),...  21.6 us
    sub x7, other arithmetic, attend_back(): grad_probs - jnp.sum(probs * grad_probs, axis=1, keepdims=True)  19.2 us
  transfers between devices with their start and end apart: 9, of which 7 were waited for; matrix products, arithmetic and copies ran while one was open for 4% of the time, Pallas kernels for 0%

commit v1 on v0

--- a/solution.py
+++ b/solution.py
@@ -3,15 +3,179 @@
 import jax
 import jax.numpy as jnp
 from jax import lax
+from jax.experimental import pallas as pl
+from jax.experimental.pallas import tpu as pltpu
 from jax.sharding import PartitionSpec as P
 
 HD = 128
 K = 16
 SPAN = 896
-
-
+ROWS = 128
+WORD = 64
 epsilon = 1e-05
 highest = lax.Precision.HIGHEST
+HUGE = -1e30
+VMEM = 56 * 1024 * 1024
+
+
+def dot(left, right, left_dim, right_dim):
+    return lax.dot_general(
+        left,
+        right,
+        (((left_dim,), (right_dim,)), ((), ())),
+        preferred_element_type=jnp.float32,
+    )
+
+
+def two_blocks(first, second):
+    zero = jnp.zeros_like(first)
+    return jnp.concatenate(
+        [jnp.concatenate([first, zero], 1), jnp.concatenate([zero, second], 1)], 0
+    )
+
+
+def forward_kernel(nbr_ref, q_ref, k_ref, vt_ref, e_ref, mixed_ref, inv_ref):
+    block = pl.program_id(0)
+    start = pl.multiple_of(block * ROWS, ROWS)
+    window = e_ref.shape[1]
+    factor = 1.0 / math.sqrt(HD)
+    scale = factor * math.log2(math.e)
+    place = nbr_ref[:, pl.ds(start, ROWS)] - start
+    bit = jnp.left_shift(1, jnp.right_shift(place, 6))
+    low = jnp.bitwise_and(place, WORD - 1)
+    lane_low = lax.broadcasted_iota(jnp.int32, (WORD, ROWS), 0)
+    words = jnp.zeros((WORD, ROWS), jnp.int32)
+    for j in range(K):
+        words = words | jnp.where(lane_low == low[j : j + 1, :], bit[j : j + 1, :], 0)
+    words = jnp.concatenate([words, words], 1)
+    queries = q_ref[pl.ds(start, ROWS), :]
+    both = two_blocks(queries[:, :HD], queries[:, HD:])
+    scores = dot(k_ref[pl.ds(start, window), :], both, 1, 1)
+    masked = []
+    for t in range(window // WORD):
+        keep = (words & (1 << t)) != 0
+        masked.append(jnp.where(keep, scores[t * WORD : (t + 1) * WORD, :], HUGE))
+    top = masked[0]
+    for part in masked[1:]:
+        top = jnp.maximum(top, part)
+    top = jnp.max(top, axis=0, keepdims=True) * scale
+    total = jnp.zeros((WORD, 2 * ROWS), jnp.float32)
+    weights = []
+    for part in masked:
+        weight = jnp.exp2(part * scale - top)
+        total = total + weight
+        weights.append(weight.astype(jnp.bfloat16))
+    inverse = 1.0 / jnp.sum(total, axis=0, keepdims=True)
+    weights = jnp.concatenate(weights, 0)
+    e_ref[0] = weights
+    inv_ref[0] = jnp.broadcast_to(inverse, inv_ref.shape[1:])
+    mixed = dot(vt_ref[:, pl.ds(start, window)], weights, 1, 0) * inverse
+    mixed_ref[:, :HD] = mixed[:HD, :ROWS].T.astype(jnp.bfloat16)
+    mixed_ref[:, HD:] = mixed[HD:, ROWS:].T.astype(jnp.bfloat16)
+
+
+def attend(places, queries, keys, values_t):
+    rows = queries.shape[0]
+    wide = 2 * HD
+    blocks = rows // ROWS
+    window = ROWS + 2 * SPAN
+    return pl.pallas_call(
+        forward_kernel,
+        grid=(blocks,),
+        in_specs=[
+            pl.BlockSpec(places.shape, lambda b: (0, 0)),
+            pl.BlockSpec(queries.shape, lambda b: (0, 0)),
+            pl.BlockSpec(keys.shape, lambda b: (0, 0)),
+            pl.BlockSpec(values_t.shape, lambda b: (0, 0)),
+        ],
+        out_specs=[
+            pl.BlockSpec((1, window, wide), lambda b: (b, 0, 0)),
+            pl.BlockSpec((ROWS, wide), lambda b: (b, 0)),
+            pl.BlockSpec((1, 8, wide), lambda b: (b, 0, 0)),
+        ],
+        out_shape=[
+            jax.ShapeDtypeStruct((blocks, window, wide), jnp.bfloat16),
+            jax.ShapeDtypeStruct((rows, wide), jnp.bfloat16),
+            jax.ShapeDtypeStruct((blocks, 8, wide), jnp.float32),
+        ],
+        compiler_params=pltpu.CompilerParams(vmem_limit_bytes=VMEM),
+        name="attend_forward",
+    )(places, queries, keys, values_t)
+
+
+def backward_kernel(
+    e_ref, inv_ref, q_ref, kt_ref, v_ref, gt_ref, dq_ref, dk_ref, dv_ref, dk_sum, dv_sum
+):
+    block = pl.program_id(0)
+    start = pl.multiple_of(block * ROWS, ROWS)
+    window = e_ref.shape[1]
+    factor = 1.0 / math.sqrt(HD)
+
+    @pl.when(block == 0)
+    def _():
+        dk_sum[...] = jnp.zeros_like(dk_sum)
+        dv_sum[...] = jnp.zeros_like(dv_sum)
+
+    inverse = inv_ref[0][:1, :]
+    queries = q_ref[pl.ds(start, ROWS), :]
+    both = two_blocks(queries[:, :HD], queries[:, HD:])
+    grad = gt_ref[:, pl.ds(start, ROWS)]
+    grad_both = two_blocks(
+        (grad[:HD, :] * inverse[:, :ROWS]).astype(jnp.bfloat16),
+        (grad[HD:, :] * inverse[:, ROWS:]).astype(jnp.bfloat16),
+    )
+    weights = e_ref[0]
+    spots = pl.ds(start, window)
+    grad_probs = dot(v_ref[spots, :], grad_both, 1, 0)
+    wide = weights.astype(jnp.float32)
+    cross = jnp.sum(grad_probs * wide, axis=0, keepdims=True) * inverse
+    grad_scores = (wide * (grad_probs - cross)).astype(jnp.bfloat16)
+    dv_sum[spots, :] += dot(weights, grad_both, 1, 1)
+    dk_sum[spots, :] += dot(grad_scores, both, 1, 0)
+    grad_query = dot(kt_ref[:, spots], grad_scores, 1, 0) * factor
+    dq_ref[:, :HD] = grad_query[:HD, :ROWS].T.astype(jnp.bfloat16)
+    dq_ref[:, HD:] = grad_query[HD:, ROWS:].T.astype(jnp.bfloat16)
+
+    @pl.when(block == pl.num_programs(0) - 1)
+    def _():
+        dk_ref[...] = (dk_sum[...] * factor).astype(dk_ref.dtype)
+        dv_ref[...] = dv_sum[...].astype(dv_ref.dtype)
+
+
+def attend_back(weights, inverse, queries, keys_t, values, grad_t):
+    rows = queries.shape[0]
+    wide = 2 * HD
+    blocks, window, _ = weights.shape
+    span_rows = values.shape[0]
+    whole = lambda array: pl.BlockSpec(array.shape, lambda b: (0, 0))
+    return pl.pallas_call(
+        backward_kernel,
+        grid=(blocks,),
+        in_specs=[
+            pl.BlockSpec((1, window, wide), lambda b: (b, 0, 0)),
+            pl.BlockSpec((1, 8, wide), lambda b: (b, 0, 0)),
+            whole(queries),
+            whole(keys_t),
+            whole(values),
+            whole(grad_t),
+        ],
+        out_specs=[
+            pl.BlockSpec((ROWS, wide), lambda b: (b, 0)),
+            pl.BlockSpec((span_rows, wide), lambda b: (0, 0)),
+            pl.BlockSpec((span_rows, wide), lambda b: (0, 0)),
+        ],
+        out_shape=[
+            jax.ShapeDtypeStruct((rows, wide), jnp.bfloat16),
+            jax.ShapeDtypeStruct((span_rows, wide), jnp.float32),
+            jax.ShapeDtypeStruct((span_rows, wide), jnp.float32),
+        ],
+        scratch_shapes=[
+            pltpu.VMEM((span_rows, wide), jnp.float32),
+            pltpu.VMEM((span_rows, wide), jnp.float32),
+        ],
+        compiler_params=pltpu.CompilerParams(vmem_limit_bytes=VMEM),
+        name="attend_backward",
+    )(weights, inverse, queries, keys_t, values, grad_t)
 
 
 def extended(block, sides, width):
@@ -96,47 +260,8 @@
     node_count = node_rows * lax.axis_size("nodes")
     first_node = lax.axis_index("nodes") * node_rows
     local_index = jnp.mod(neighbours - first_node + SPAN, node_count)
-    block_rows = math.gcd(node_rows, 128)
-    block_count = node_rows // block_rows
-    window_rows = block_rows + 2 * SPAN
-    window_iota = jnp.arange(window_rows, dtype=jnp.int32)
-    query_blocks = queries.reshape(block_count, block_rows, head_count, HD)
-    index_blocks = local_index.reshape(block_count, block_rows, K)
-    block_starts = jnp.arange(block_count, dtype=jnp.int32) * block_rows
-
-    def selector(index_block, start):
-        return index_block.reshape(block_rows * K, 1) - start == window_iota[None, :]
-
-    def fetch(index_block, start):
-        window = lax.dynamic_slice_in_dim(padded, start, window_rows, 0)
-        picks = selector(index_block, start).astype(jnp.bfloat16)
-        fetched = jnp.dot(picks, window, preferred_element_type=jnp.float32).astype(jnp.bfloat16)
-        fetched = fetched.reshape(block_rows, K, 2 * local_width)
-        key_block = fetched[:, :, :local_width].reshape(block_rows, K, head_count, HD)
-        value_block = fetched[:, :, local_width:].reshape(block_rows, K, head_count, HD)
-        return (key_block, value_block)
-
-    def attend(operands):
-        query_block, index_block, start = operands
-        key_block, value_block = fetch(index_block, start)
-        scores = (
-            jnp.einsum("bhd,bkhd->bkh", query_block, key_block, preferred_element_type=jnp.float32)
-            * factor
-        )
-        top_score = jnp.max(scores, axis=1, keepdims=True)
-        weights = jnp.exp(scores - top_score)
-        total = jnp.sum(weights, axis=1, keepdims=True)
-        probs = weights / total
-        mixed_block = jnp.einsum(
-            "bkh,bkhd->bhd", probs, value_block.astype(jnp.float32), precision=highest
-        )
-        return (
-            mixed_block.reshape(block_rows, local_width).astype(jnp.bfloat16),
-            (top_score + jnp.log(total))[:, 0, :],
-        )
-
-    mixed_blocks, log_totals = lax.map(attend, (query_blocks, index_blocks, block_starts))
-    mixed = mixed_blocks.reshape(node_rows, local_width)
+    places = local_index.T
+    weights, mixed, inverse_sum = attend(places, queries, padded[:, :local_width], padded[:, local_width:].T)
     attn_share = lax.psum_scatter(
         jnp.dot(mixed, w_out, preferred_element_type=jnp.float32).astype(jnp.bfloat16),
         "heads",
@@ -187,59 +312,11 @@
     grad_mid = cotangent.astype(jnp.float32) + grad_in2
     grad_branch = lax.all_gather(grad_mid.astype(jnp.bfloat16), "heads", axis=1, tiled=True)
     grad_out = contract_rows(mixed, grad_branch)
-    grad_mixed = contract_cols(grad_branch, w_out)
-
-    def attend_back(carry, operands):
-        query_block, index_block, grad_block, log_block, start = operands
-        key_block, value_block = fetch(index_block, start)
-        scores = (
-            jnp.einsum("bhd,bkhd->bkh", query_block, key_block, preferred_element_type=jnp.float32)
-            * factor
-        )
-        probs = jnp.exp(scores - log_block[:, None, :])
-        grad_heads = grad_block.reshape(block_rows, head_count, HD)
-        grad_probs = jnp.einsum(
-            "bhd,bkhd->bkh", grad_heads, value_block.astype(jnp.float32), precision=highest
-        )
-        grad_scores = probs * (grad_probs - jnp.sum(probs * grad_probs, axis=1, keepdims=True))
-        grad_query_block = (
-            jnp.einsum(
-                "bkh,bkhd->bhd", grad_scores, key_block.astype(jnp.float32), precision=highest
-            )
-            * factor
-        )
-        grad_key_block = (
-            jnp.einsum(
-                "bkh,bhd->bkhd", grad_scores, query_block.astype(jnp.float32), precision=highest
-            )
-            * factor
-        )
-        grad_value_block = jnp.einsum("bkh,bhd->bkhd", probs, grad_heads, precision=highest)
-        joined = jnp.concatenate(
-            [
-                grad_key_block.reshape(block_rows, K, local_width),
-                grad_value_block.reshape(block_rows, K, local_width),
-            ],
-            axis=2,
-        )
-        picks = selector(index_block, start).astype(jnp.float32)
-        spread = contract_rows(picks, joined.reshape(block_rows * K, 2 * local_width), highest)
-        current = lax.dynamic_slice_in_dim(carry, start, window_rows, 0)
-        carry = lax.dynamic_update_slice_in_dim(carry, current + spread, start, 0)
-        return (carry, grad_query_block.reshape(block_rows, local_width))
-
-    start_pad = jnp.zeros((node_rows + 2 * SPAN, 2 * local_width), jnp.float32)
-    grad_pad, grad_query_blocks = lax.scan(
-        attend_back,
-        start_pad,
-        (
-            query_blocks,
-            index_blocks,
-            grad_mixed.reshape(block_count, block_rows, local_width),
-            log_totals,
-            block_starts,
-        ),
-    )
+    grad_t = dot(w_out, grad_branch, 1, 1)
+    grad_queries, grad_key_pad, grad_value_pad = attend_back(
+        weights, inverse_sum, queries, padded[:, :local_width].T, padded[:, local_width:], grad_t
+    )
+    grad_pad = jnp.concatenate([grad_key_pad, grad_value_pad], axis=1)
     from_above = passed_along(grad_pad[:SPAN].astype(jnp.bfloat16), "nodes", -1).astype(jnp.float32)
     from_below = passed_along(grad_pad[node_rows + SPAN :].astype(jnp.bfloat16), "nodes", 1).astype(
         jnp.float32
@@ -249,7 +326,6 @@
     grad_centre = grad_centre.at[node_rows - SPAN :].add(from_above)
     grad_keys = grad_centre[:, :local_width].astype(jnp.bfloat16)
     grad_values = grad_centre[:, local_width:].astype(jnp.bfloat16)
-    grad_queries = grad_query_blocks.reshape(node_rows, local_width).astype(jnp.bfloat16)
     grad_query = contract_rows(normed_one, grad_queries)
     grad_key = contract_rows(normed_one, grad_keys)
     grad_value = contract_rows(normed_one, grad_values)

time: 928 us -> 461 us (0.50)
  matrix products: 286 us -> 46.6 us
  local copies, waits for them, and re-layouts: 159 us -> 23.7 us
  other arithmetic: 105 us -> 18.8 us
  Pallas kernels: 0 us -> 33.9 us
  loops' own time: 29.8 us -> 0 us
    dot_general x49 -> x1, matrix products: 133 us -> 1.41 us  [dot(): lax.dot_general(left, right, (((left_dim,), (right_dim,)), ((), ())), pre...]
    dot_general x17 -> x10, matrix products: 125 us -> 18.2 us  [contract_rows(): lax.dot_general(left, right, (((0,), (0,)), ((), ())), precision=precisio...]
    dynamic_update_slice x21 -> x0, local copies, waits for them, and re-layouts: 83.7 us -> none  [the longest x7 79.2 us: attend_back(): carry = lax.dynamic_update_slice_in_dim(carry, current + spread, start, 0)]
    pallas_call x0 -> x2, Pallas kernels: none -> 33.9 us  [the longest x1 18.1 us: attend_back(): pl.pallas_call(backward_kernel, grid=(blocks,), in_specs=[pl.BlockSpec((1...]
    another operation x2 -> x0, loops' own time: 29.8 us -> none  [the longest x1 15.5 us: body(): lax.scan(attend_back, start_pad, (query_blocks, index_blocks, grad_mixed....]
    sub x21 -> x0, other arithmetic: 28.4 us -> none  [the longest x7 19.2 us: attend_back(): grad_probs - jnp.sum(probs * grad_probs, axis=1, keepdims=True)]
    mul x15 -> x0, other arithmetic: 22.1 us -> none  [the longest x7 21.6 us: attend_back(): jnp.einsum('bkh,bhd->bkhd', grad_scores, query_block.astype(jnp.float32),...]
    dot_general x7 -> x0, other arithmetic: 17.2 us -> none  [attend_back(): jnp.einsum('bkh,bhd->bkhd', probs, grad_heads, precision=highest)]
  transfers between devices with their start and end apart: 9 -> 9, of which waited for: 7 -> 7; matrix products, arithmetic and copies ran while one was open for 4% -> 9% of each run, Pallas kernels for 0% -> 0%
where the time goes in v1:
time: 461 us
  waiting for transfers between devices  295 us (64%)
  matrix products  46.6 us (10%)
  Pallas kernels  33.9 us (7%)
  local copies, waits for them, and re-layouts  23.7 us (5%)
  other arithmetic  18.8 us (4%)
  blocking collectives  15.8 us (3%)
  between operations  14.2 us (3%)
  starting transfers between devices  13 us (3%)
    psum x1, waiting for transfers between devices, body(): lax.psum((grad_up, grad_down, grad_query, grad_key, grad_value, grad_out,...  213 us
    ppermute x2, waiting for transfers between devices, passed_along(): return lax.ppermute(block, axis, route)  37.5 us
    dot_general x10, matrix products, contract_rows(): lax.dot_general(left, right, (((0,), (0,)), ((), ())), precision=precisio...  18.2 us
    pallas_call x1, Pallas kernels, attend_back(): pl.pallas_call(backward_kernel, grid=(blocks,), in_specs=[pl.BlockSpec((1...  18.1 us
    ppermute x1, waiting for transfers between devices, extended(): lax.ppermute(lax.slice_in_dim(block, block.shape[dim] - width, None, axis...  17.5 us
    unnamed x94, local copies, waits for them, and re-layouts  16.9 us
    ppermute x1, waiting for transfers between devices, extended(): lax.ppermute(lax.slice_in_dim(block, 0, width, axis=dim), axis, backward)  16.6 us
    pallas_call x1, Pallas kernels, attend(): pl.pallas_call(forward_kernel, grid=(blocks,), in_specs=[pl.BlockSpec(pla...  15.8 us
  transfers between devices with their start and end apart: 9, of which 7 were waited for; matrix products, arithmetic and copies ran while one was open for 9% of the time, Pallas kernels for 0%

profile of v1, /device:TPU:0, one launch (start us, length us, event | category | flops | bytes accessed | tf_op | source)
XLA Modules:
  0.0 460.7 jit_solution(12244002854089593905)
XLA Ops:
  7.3 2.9 all_gather.12
  16.0 6.9 %collective-permute-start.1 = (bf16[896,512]{1,0:T(8,128)(2,1)}, bf16[896,512]{1,0:T(8,128)(2,1)}, u32[]{:S(2)}, u32[]{:S(2)}) collective-permute-start(bf16[896,512]{1,0:T(8,128)(2,1)} %pad_maximum_fusion.1), channel_id=1, source_target_pairs={{2,0},{4,2},{6,4},{8,6},{10,8},{12,10},{14,12},{16,14},{18,16},{20... | collective-permute-start | bytes 2752520 | tf_op jit(solution)/shard_map/ppermute | solution.py:190
  24.4 2.1 convolution_convert_fusion.6.q_ref
  26.5 16.6 %collective-permute-done.1 = bf16[896,512]{1,0:T(8,128)(2,1)} collective-permute-done((bf16[896,512]{1,0:T(8,128)(2,1)}, bf16[896,512]{1,0:T(8,128)(2,1)}, u32[]{:S(2)}, u32[]{:S(2)}) %collective-permute-start.1) | collective-permute-done | bytes 917536 | tf_op jit(solution)/shard_map/ppermute | solution.py:190
  43.1 17.5 %collective-permute-done = bf16[896,512]{1,0:T(8,128)(2,1)} collective-permute-done((bf16[896,512]{1,0:T(8,128)(2,1)}, bf16[896,512]{1,0:T(8,128)(2,1)}, u32[]{:S(2)}, u32[]{:S(2)}) %collective-permute-start) | collective-permute-done | bytes 917536 | tf_op jit(solution)/shard_map/ppermute | solution.py:187
  60.6 2.0 pad_maximum_fusion
  62.6 2.2 fusion.59
  66.5 15.8 %attend_forward.1 = (bf16[7,1920,256]{2,1,0:T(8,128)(2,1)}, bf16[896,256]{1,0:T(8,128)(2,1)}, f32[7,8,256]{2,1,0:T(8,128)}) custom-call(s32[16,896]{1,0:T(8,128)} %fusion.37.nbr_ref, bf16[896,256]{1,0:T(8,128)(2,1)} %convolution_convert_fusion.6.q_ref, bf16[2688,256]{1,0:T(8,128)(2,1)} %get-tuple-element.83.k_ref, bf16[256,2688]{1,0:T(8,128)(2,1)} %copy.22.vt_ref), custom_call_target="tpu_custom_call" | custom-call | tf_op jit(solution)/shard_map/attend_forward/pallas_call | solution.py:82
  82.3 2.4 convolution_convert_fusion.3
  84.8 2.7 all_gather.14
  87.5 2.2 fusion.25
  89.7 3.9 reduce-scatter.5.cloned.1.call-done
  94.7 2.8 all_gather.13
  99.8 2.8 multiply_convert_fusion.1
  105.7 2.1 convolution_convert_fusion.1
  107.9 2.5 copy.25.kt_ref
  111.9 5.6 %reduce-scatter.9.cloned.1.call-done = bf16[896,256]{1,0:T(8,128)(2,1)} async-done(((bf16[896,512]{1,0:T(8,128)(2,1)}), bf16[896,256]{1,0:T(8,128)(2,1)}) %reduce-scatter.9.cloned.1.call-update) | async-done | bytes 458768 | tf_op jit(solution)/shard_map/reduce_scatter | solution.py:308
  119.5 2.5 all-reduce.2
  122.1 2.6 fusion.57
  124.7 2.4 all_gather.15
  128.5 18.1 %attend_backward.1 = (bf16[896,256]{1,0:T(8,128)(2,1)}, f32[2688,256]{1,0:T(8,128)}, f32[2688,256]{1,0:T(8,128)}) custom-call(bf16[7,1920,256]{2,1,0:T(8,128)(2,1)} %get-tuple-element.56.e_ref, f32[7,8,256]{2,1,0:T(8,128)} %get-tuple-element.57.inv_ref, bf16[896,256]{1,0:T(8,128)(2,1)} %convolution_convert_fusion.6.q_ref, bf16[256,2688]{1,0:T(8,128)(2,1)} %copy.25.kt_ref, ...), custom_call_target="tpu_custom_call" | custom-call | tf_op jit(solution)/shard_map/attend_backward/pallas_call | solution.py:151
  146.7 2.3 constant_dynamic-update-slice_fusion.1
  151.9 4.2 collective-permute-start.3
  156.1 35.6 %collective-permute-done.2 = bf16[896,512]{1,0:T(8,128)(2,1)S(1)} collective-permute-done((bf16[896,512]{1,0:T(8,128)(2,1)S(1)}, bf16[896,512]{1,0:T(8,128)(2,1)S(1)}, u32[]{:S(2)}, u32[]{:S(2)}) %collective-permute-start.2) | collective-permute-done | bytes 917536 | tf_op jit(solution)/shard_map/ppermute | solution.py:198
  199.0 3.4 convolution_convert_fusion.2
  202.3 4.2 fusion.63
  206.7 4.2 fusion.64
  218.6 2.1 convolution_bitcast_fusion.2
  225.9 2.5 all-reduce.1
  228.3 2.5 multiply_add_fusion
  230.9 213.4 %all-reduce.5.cloned.1.call-done = (f32[512,256]{1,0:T(8,128)}, f32[512,256]{1,0:T(8,128)}, f32[512,256]{1,0:T(8,128)}, f32[256,512]{1,0:T(8,128)}, f32[512,1024...) async-done(((f32[512,256]{1,0:T(8,128)}, f32[512,256]{1,0:T(8,128)}, f32[512,256]{1,0:T(8,128)}, f32[256,512]{1,0:T(8,128)}, f32[512,1024]{1,0:T(8,128)}, ...) | async-done | bytes 6357008 | tf_op jit(solution)/shard_map/psum | solution.py:343
  446.2 2.0 copy.41
  (147 shorter events, 51.6 us)
Async XLA Ops:
  7.2 92.6 %copy-start = (bf16[512,1024]{1,0:T(8,128)(2,1)S(1)}, bf16[512,1024]{1,0:T(8,128)(2,1)}, u32[]{:S(2)}) copy-start(bf16[512,1024]{1,0:T(8,128)(2,1)} %param.24) | copy-start | bytes 3145732
  7.2 3.6 copy-start.31
  7.2 3.6 copy-start.32
  7.2 86.4 %reduce-scatter.5.cloned.1.call-start = ((), (), s32[]{:S(2)}) async-start(), calls=%async_computation.4 | async-start | bytes 1376256 | tf_op jit(solution)/shard_map/reduce_scatter | solution.py:265
  13.4 11.0 %copy-start.2 = (bf16[896,512]{1,0:T(8,128)(2,1)}, bf16[896,512]{1,0:T(8,128)(2,1)S(1)}, u32[]{:S(2)}) copy-start(bf16[896,512]{1,0:T(8,128)(2,1)S(1)} %add_convert_fusion.1) | copy-start | bytes 2752516
  16.0 27.1 %collective-permute-start.1 = (bf16[896,512]{1,0:T(8,128)(2,1)}, bf16[896,512]{1,0:T(8,128)(2,1)}, u32[]{:S(2)}, u32[]{:S(2)}) collective-permute-start(bf16[896,512]{1,0:T(8,128)(2,1)} %pad_maximum_fusion.1), channel_id=1, source_target_pairs={{2,0},{4,2},{6,4},{8,6},{10,8},{12,10},{14,12},{16,14},{18,16},{20... | collective-permute-start | bytes 2752520 | tf_op jit(solution)/shard_map/ppermute | solution.py:190
  22.9 37.7 %collective-permute-start = (bf16[896,512]{1,0:T(8,128)(2,1)}, bf16[896,512]{1,0:T(8,128)(2,1)}, u32[]{:S(2)}, u32[]{:S(2)}) collective-permute-start(bf16[896,512]{1,0:T(8,128)(2,1)} %pad_maximum_fusion.1), channel_id=1, source_target_pairs={{0,2},{2,4},{4,6},{6,8},{8,10},{10,12},{12,14},{14,16},{16,18},{18... | collective-permute-start | bytes 2752520 | tf_op jit(solution)/shard_map/ppermute | solution.py:187
  22.9 37.7 %copy-start.8 = (bf16[896,256]{1,0:T(8,128)(2,1)S(1)}, bf16[896,256]{1,0:T(8,128)(2,1)}, u32[]{:S(2)}) copy-start(bf16[896,256]{1,0:T(8,128)(2,1)} %copy-done.7) | copy-start | bytes 1376260
  66.5 15.8 %copy-start.23 = (bf16[256,512]{1,0:T(8,128)(2,1)S(1)}, bf16[256,512]{1,0:T(8,128)(2,1)}, u32[]{:S(2)}) copy-start(bf16[256,512]{1,0:T(8,128)(2,1)} %param.23) | copy-start | bytes 786436
  84.7 8.9 %copy-start.9 = (bf16[896,256]{1,0:T(8,128)(2,1)S(1)}, bf16[896,256]{1,0:T(8,128)(2,1)}, u32[]{:S(2)}) copy-start(bf16[896,256]{1,0:T(8,128)(2,1)} %param.19) | copy-start | bytes 1376260
  84.7 32.8 %reduce-scatter.9.cloned.1.call-start = ((), (), s32[]{:S(2)}) async-start(), calls=%async_computation.6 | async-start | bytes 1376256 | tf_op jit(solution)/shard_map/reduce_scatter | solution.py:308
  94.7 3.5 copy-start.6
  107.8 109.4 %reduce-scatter.11.cloned.1.call-start = ((), (), s32[]{:S(2)}) async-start(), calls=%async_computation.7 | async-start | bytes 1376256 | tf_op jit(solution)/shard_map/reduce_scatter | solution.py:334
  111.9 10.1 %copy-start.20 = (bf16[896,256]{1,0:T(8,128)(2,1)S(1)}, bf16[896,256]{1,0:T(8,128)(2,1)}, u32[]{:S(2)}) copy-start(bf16[896,256]{1,0:T(8,128)(2,1)} %param.29) | copy-start | bytes 1376260
  122.1 5.1 %copy-start.24 = (bf16[256,512]{1,0:T(8,128)(2,1)S(1)}, bf16[256,512]{1,0:T(8,128)(2,1)}, u32[]{:S(2)}) copy-start(bf16[256,512]{1,0:T(8,128)(2,1)} %param.23) | copy-start | bytes 786436
  150.1 41.5 %collective-permute-start.2 = (bf16[896,512]{1,0:T(8,128)(2,1)S(1)}, bf16[896,512]{1,0:T(8,128)(2,1)S(1)}, u32[]{:S(2)}, u32[]{:S(2)}) collective-permute-start(bf16[896,512]{1,0:T(8,128)(2,1)S(1)} %get-tuple-element.78), channel_id=1, source_target_pairs={{30,0},{0,2},{2,4},{4,6},{6,8},{8,10},{10,12},{12,14},{14,16},{16,... | collective-permute-start | bytes 2752520 | tf_op jit(solution)/shard_map/ppermute | solution.py:198
  151.9 43.1 %copy-start.33 = (bf16[512,256]{1,0:T(8,128)(2,1)S(1)}, bf16[512,256]{1,0:T(8,128)(2,1)}, u32[]{:S(2)}) copy-start(bf16[512,256]{1,0:T(8,128)(2,1)} %param.20) | copy-start | bytes 786436
  151.9 43.1 %copy-start.35 = (bf16[512,256]{1,0:T(8,128)(2,1)S(1)}, bf16[512,256]{1,0:T(8,128)(2,1)}, u32[]{:S(2)}) copy-start(bf16[512,256]{1,0:T(8,128)(2,1)} %param.22) | copy-start | bytes 786436
  151.9 43.1 %copy-start.37 = (bf16[512,256]{1,0:T(8,128)(2,1)S(1)}, bf16[512,256]{1,0:T(8,128)(2,1)}, u32[]{:S(2)}) copy-start(bf16[512,256]{1,0:T(8,128)(2,1)} %param.21) | copy-start | bytes 786436
  151.9 43.1 %copy-start.40 = (bf16[896,256]{1,0:T(8,128)(2,1)S(1)}, bf16[896,256]{1,0:T(8,128)(2,1)}, u32[]{:S(2)}) copy-start(bf16[896,256]{1,0:T(8,128)(2,1)} %get-tuple-element.58) | copy-start | bytes 1376260
  151.9 41.7 %collective-permute-start.3 = (bf16[896,512]{1,0:T(8,128)(2,1)S(1)}, bf16[896,512]{1,0:T(8,128)(2,1)S(1)}, u32[]{:S(2)}, u32[]{:S(2)}) collective-permute-start(bf16[896,512]{1,0:T(8,128)(2,1)S(1)} %get-tuple-element.79), channel_id=1, source_target_pairs={{2,0},{4,2},{6,4},{8,6},{10,8},{12,10},{14,12},{16,14},{18,16},{20... | collective-permute-start | bytes 2752520 | tf_op jit(solution)/shard_map/ppermute | solution.py:198
  196.9 24.5 %reduce-scatter.7.cloned.1.call-start = ((), (), s32[]{:S(2)}) async-start(), calls=%async_computation.5 | async-start | bytes 1376256 | tf_op jit(solution)/shard_map/reduce_scatter | solution.py:279
  199.0 3.4 copy-start.13
  202.3 4.3 copy-start.26
  206.6 4.3 copy-start.10
  206.6 237.7 %all-reduce.5.cloned.1.call-start = ((), (), s32[]{:S(2)}) async-start(), calls=%async_computation.8 | async-start | bytes 12713984 | tf_op jit(solution)/shard_map/psum | solution.py:343
  206.7 4.7 %copy-start.4 = (f32[896,512]{1,0:T(8,128)S(1)}, f32[896,512]{1,0:T(8,128)}, u32[]{:S(2)}) copy-start(f32[896,512]{1,0:T(8,128)} %fusion.2) | copy-start | bytes 5505028
  224.3 4.0 copy-start.14
  444.3 4.0 copy-start.30
  444.3 4.8 %copy-start.29 = (f32[256,512]{1,0:T(8,128)S(1)}, f32[256,512]{1,0:T(8,128)}, u32[]{:S(2)}) copy-start(f32[256,512]{1,0:T(8,128)} %get-tuple-element.95) | copy-start | bytes 1572868
  446.2 3.6 copy-start.17
  449.9 4.3 copy-start.1
  (20 other events, 41.2 us)
Sparse Core Ops, SparseCore 0:
  84.8 8.7 reduce-scatter.4
  107.9 9.5 reduce-scatter.8
  197.0 8.4 reduce-scatter.10
  208.2 9.5 reduce-scatter.6
  225.3 218.9 all-reduce.4

commit v2 on v1

--- a/solution.py
+++ b/solution.py
@@ -178,40 +178,50 @@
     )(weights, inverse, queries, keys_t, values, grad_t)
 
 
-def extended(block, sides, width):
-    for axis, dim in sides:
-        count = lax.axis_size(axis)
-        forward = [(i, i + 1) for i in range(count - 1)]
-        forward.append((count - 1, 0))
-        backward = [(target, source) for source, target in forward]
-        low = lax.ppermute(
-            lax.slice_in_dim(block, block.shape[dim] - width, None, axis=dim), axis, forward
-        )
-        high = lax.ppermute(lax.slice_in_dim(block, 0, width, axis=dim), axis, backward)
-        block = jnp.concatenate([low, block, high], axis=dim)
-    return block
-
-
 def passed_along(block, axis, distance):
     devices = range(lax.axis_size(axis))
     route = [((i - distance) % len(devices), i) for i in devices]
     return lax.ppermute(block, axis, route)
 
 
-def contract_rows(left, right, precision=None):
-    return lax.dot_general(
-        left,
-        right,
-        (((0,), (0,)), ((), ())),
-        precision=precision,
-        preferred_element_type=jnp.float32,
-    )
-
-
-def contract_cols(left, right):
-    return lax.dot_general(
-        left, right, (((1,), (1,)), ((), ())), preferred_element_type=jnp.float32
-    )
+def swapped(block, axis, bit):
+    devices = range(lax.axis_size(axis))
+    return lax.ppermute(block, axis, [(i, i ^ bit) for i in devices])
+
+
+def bits_of(axis, swap):
+    bits = [1 << k for k in range(lax.axis_size(axis).bit_length() - 1)]
+    if swap:
+        bits[0], bits[1] = bits[1], bits[0]
+    return bits
+
+
+def scatter_sum(block, axis, bits):
+    place = lax.axis_index(axis)
+    for bit in bits:
+        half = block.shape[0] // 2
+        upper = (place & bit) != 0
+        send = jnp.where(upper, block[:half], block[half:])
+        keep = jnp.where(upper, block[half:], block[:half])
+        got = swapped(send, axis, bit)
+        block = (keep.astype(jnp.float32) + got.astype(jnp.float32)).astype(jnp.bfloat16)
+    return block
+
+
+def gathered(block, axis, bits):
+    place = lax.axis_index(axis)
+    for bit in reversed(bits):
+        upper = (place & bit) != 0
+        got = swapped(block, axis, bit)
+        block = jnp.where(
+            upper, jnp.concatenate([got, block]), jnp.concatenate([block, got])
+        )
+    return block
+
+
+def total_of(block, axis, swap):
+    bits = bits_of(axis, swap)
+    return gathered(scatter_sum(block.astype(jnp.bfloat16), axis, bits), axis, bits)
 
 
 def norm_full(values):
@@ -220,6 +230,13 @@
     variance = jnp.mean(centred * centred, axis=1, keepdims=True)
     inverse = lax.rsqrt(variance + epsilon)
     return (centred * inverse, inverse)
+
+
+def in_three(table):
+    first = lax.reduce_precision(table, 8, 7)
+    rest = table - first
+    second = lax.reduce_precision(rest, 8, 7)
+    return jnp.concatenate([first, second, rest - second], axis=0).astype(jnp.bfloat16)
 
 
 def body(
@@ -235,124 +252,148 @@
     neighbours,
     cotangent,
 ):
-    node_rows = inputs.shape[0]
-    half = inputs.shape[1]
+    rows, half = inputs.shape
     width = half * lax.axis_size("heads")
     local_width = w_query.shape[1]
-    head_count = local_width // HD
-    column_first = lax.axis_index("heads") * half
-    factor = 1.0 / math.sqrt(HD)
-    onehot = (
-        level_ids[:, None] == jnp.arange(mod_table.shape[1], dtype=jnp.int32)[None, :]
-    ).astype(jnp.float32)
-
-    def level_rows(which):
-        return jnp.dot(onehot, mod_table[which], precision=highest)
-
-    full_in = lax.all_gather(inputs, "heads", axis=1, tiled=True).astype(jnp.float32)
-    normed1, inverse1 = norm_full(full_in)
-    normed_one = (normed1 * (1.0 + level_rows(0)) + level_rows(1)).astype(jnp.bfloat16)
-    queries = jnp.dot(normed_one, w_query, preferred_element_type=jnp.float32).astype(jnp.bfloat16)
-    keys = jnp.dot(normed_one, w_key, preferred_element_type=jnp.float32).astype(jnp.bfloat16)
-    values = jnp.dot(normed_one, w_value, preferred_element_type=jnp.float32).astype(jnp.bfloat16)
-    key_value = jnp.concatenate([keys, values], axis=1)
-    padded = extended(key_value, (("nodes", 0),), SPAN)
-    node_count = node_rows * lax.axis_size("nodes")
-    first_node = lax.axis_index("nodes") * node_rows
-    local_index = jnp.mod(neighbours - first_node + SPAN, node_count)
-    places = local_index.T
-    weights, mixed, inverse_sum = attend(places, queries, padded[:, :local_width], padded[:, local_width:].T)
-    attn_share = lax.psum_scatter(
-        jnp.dot(mixed, w_out, preferred_element_type=jnp.float32).astype(jnp.bfloat16),
-        "heads",
-        scatter_dimension=1,
-        tiled=True,
-    ).astype(jnp.float32)
-    middle = inputs.astype(jnp.float32) + attn_share
-    full_mid = lax.all_gather(middle.astype(jnp.bfloat16), "heads", axis=1, tiled=True).astype(
-        middle.dtype
-    )
-    normed2, inverse2 = norm_full(full_mid)
-    normed_two = (normed2 * (1.0 + level_rows(2)) + level_rows(3)).astype(jnp.bfloat16)
-    pre_act = jnp.dot(normed_two, w_up, preferred_element_type=jnp.float32)
-    activated = jax.nn.silu(pre_act).astype(jnp.bfloat16)
-    mlp_share = lax.psum_scatter(
-        jnp.dot(activated, w_down, preferred_element_type=jnp.float32).astype(jnp.bfloat16),
-        "heads",
-        scatter_dimension=1,
-        tiled=True,
-    ).astype(jnp.float32)
-    output = (middle + mlp_share).astype(jnp.bfloat16)
-
-    def norm_back(grad_share, normed_whole, inverse, which):
-        normed_share = lax.dynamic_slice_in_dim(normed_whole, column_first, half, 1)
-        scale_table = lax.dynamic_slice_in_dim(mod_table[2 * which], column_first, half, 1)
-        scale_share = jnp.dot(onehot, scale_table, precision=highest)
-        gained = grad_share * (1.0 + scale_share)
-        sum_gain, sum_cross = lax.psum(
-            (jnp.sum(gained, axis=1), jnp.sum(gained * normed_share, axis=1)), "heads"
-        )
-        grad_in = inverse * (
-            gained - sum_gain[:, None] / width - normed_share * sum_cross[:, None] / width
-        )
-        grad_scale = contract_rows(onehot, grad_share * normed_share, highest)
-        grad_shift = contract_rows(onehot, grad_share, highest)
-        return (grad_in, grad_scale, grad_shift)
-
-    full_cot = lax.all_gather(cotangent, "heads", axis=1, tiled=True)
-    grad_down = contract_rows(activated, full_cot)
-    grad_act = contract_cols(full_cot, w_down)
+    levels = mod_table.shape[1]
+    first_head = lax.axis_index("heads") == 0
+    bf16 = jnp.bfloat16
+    f32 = jnp.float32
+
+    def mine(block):
+        return jnp.where(first_head, block[:, :half], block[:, half:])
+
+    def theirs(block):
+        return jnp.where(first_head, block[:, half:], block[:, :half])
+
+    def whole(block):
+        return lax.all_gather(block, "heads", axis=1, tiled=True)
+
+    before = passed_along(inputs, "nodes", 1)
+    after = passed_along(inputs, "nodes", -1)
+    levels_before = passed_along(level_ids, "nodes", 1)
+    levels_after = passed_along(level_ids, "nodes", -1)
+    full_in = whole(inputs)
+    full_cot = whole(cotangent)
+    full_around = whole(jnp.concatenate([before, after], axis=0))
+    rows_in = jnp.concatenate([full_around[:rows], full_in, full_around[rows:]], axis=0)
+    levels_all = jnp.concatenate([levels_before, level_ids, levels_after])
+
+    def onehot_of(ids):
+        return (ids[:, None] == jnp.arange(levels, dtype=jnp.int32)[None, :]).astype(bf16)
+
+    onehot_all = onehot_of(levels_all)
+    onehot = onehot_of(level_ids)
+    tables = [in_three(mod_table[which]) for which in range(4)]
+
+    def level_rows(chosen, which):
+        return dot(jnp.concatenate([chosen] * 3, axis=1), tables[which], 1, 0)
+
+    normed1, inverse1 = norm_full(rows_in.astype(f32))
+    normed_all = (
+        normed1 * (1.0 + level_rows(onehot_all, 0)) + level_rows(onehot_all, 1)
+    ).astype(bf16)
+    normed_one = normed_all[rows : 2 * rows]
+    queries = dot(normed_one, w_query, 1, 0).astype(bf16)
+    keys = dot(normed_all, w_key, 1, 0).astype(bf16)
+    values_t = dot(w_value, normed_all, 0, 1).astype(bf16)
+    keys_t = dot(w_key, normed_all, 0, 1).astype(bf16)
+    values = dot(normed_all, w_value, 1, 0).astype(bf16)
+    node_count = rows * lax.axis_size("nodes")
+    first_node = lax.axis_index("nodes") * rows
+    places = jnp.mod(neighbours.T - first_node + SPAN, node_count)
+    weights, mixed, inverse_sum = attend(places, queries, keys, values_t)
+
+    attn_part = dot(mixed, w_out, 1, 0).astype(bf16)
+    attn_other = swapped(attn_part, "heads", 1)
+    middle = full_in.astype(f32) + (attn_part.astype(f32) + attn_other.astype(f32))
+    normed2, inverse2 = norm_full(middle)
+    gain2 = 1.0 + level_rows(onehot, 2)
+    normed_two = (normed2 * gain2 + level_rows(onehot, 3)).astype(bf16)
+    pre_act = dot(normed_two, w_up, 1, 0)
     sigma = jax.nn.sigmoid(pre_act)
-    grad_pre = (grad_act * sigma * (1.0 + pre_act * (1.0 - sigma))).astype(jnp.bfloat16)
-    grad_up = contract_rows(normed_two, grad_pre)
-    grad_two = lax.psum_scatter(
-        contract_cols(grad_pre, w_up).astype(jnp.bfloat16), "heads", scatter_dimension=1, tiled=True
-    ).astype(jnp.float32)
-    grad_in2, scale_two, shift_two = norm_back(grad_two, normed2, inverse2, 1)
-    grad_mid = cotangent.astype(jnp.float32) + grad_in2
-    grad_branch = lax.all_gather(grad_mid.astype(jnp.bfloat16), "heads", axis=1, tiled=True)
-    grad_out = contract_rows(mixed, grad_branch)
+    activated = (pre_act * sigma).astype(bf16)
+    grad_act = dot(full_cot, w_down, 1, 1)
+    grad_pre = (grad_act * sigma * (1.0 + pre_act * (1.0 - sigma))).astype(bf16)
+    two_part = dot(grad_pre, w_up, 1, 1).astype(bf16)
+    two_other = swapped(two_part, "heads", 1)
+    mlp_part = dot(activated, w_down, 1, 0)
+    mlp_other = swapped(theirs(mlp_part).astype(bf16), "heads", 1)
+    output = (mine(middle) + (mine(mlp_part) + mlp_other.astype(f32))).astype(bf16)
+    grad_up = dot(normed_two, grad_pre, 0, 0)
+    grad_down = dot(activated, full_cot, 0, 0)
+    up_total = total_of(grad_up, "nodes", False).astype(f32)
+    down_total = total_of(grad_down, "nodes", True).astype(f32)
+
+    grad_two = two_part.astype(f32) + two_other.astype(f32)
+    gained = grad_two * gain2
+    grad_mid = full_cot.astype(f32) + inverse2 * (
+        gained
+        - jnp.mean(gained, axis=1, keepdims=True)
+        - normed2 * jnp.mean(gained * normed2, axis=1, keepdims=True)
+    )
+    scale_two = dot(onehot, mine(grad_two * normed2).astype(bf16), 0, 0)
+    shift_two = dot(onehot, mine(grad_two).astype(bf16), 0, 0)
+    grad_branch = grad_mid.astype(bf16)
+    grad_out = dot(mixed, grad_branch, 0, 0)
     grad_t = dot(w_out, grad_branch, 1, 1)
-    grad_queries, grad_key_pad, grad_value_pad = attend_back(
-        weights, inverse_sum, queries, padded[:, :local_width].T, padded[:, local_width:], grad_t
-    )
-    grad_pad = jnp.concatenate([grad_key_pad, grad_value_pad], axis=1)
-    from_above = passed_along(grad_pad[:SPAN].astype(jnp.bfloat16), "nodes", -1).astype(jnp.float32)
-    from_below = passed_along(grad_pad[node_rows + SPAN :].astype(jnp.bfloat16), "nodes", 1).astype(
-        jnp.float32
-    )
-    grad_centre = grad_pad[SPAN : SPAN + node_rows]
-    grad_centre = grad_centre.at[:SPAN].add(from_below)
-    grad_centre = grad_centre.at[node_rows - SPAN :].add(from_above)
-    grad_keys = grad_centre[:, :local_width].astype(jnp.bfloat16)
-    grad_values = grad_centre[:, local_width:].astype(jnp.bfloat16)
-    grad_query = contract_rows(normed_one, grad_queries)
-    grad_key = contract_rows(normed_one, grad_keys)
-    grad_value = contract_rows(normed_one, grad_values)
-    grad_joined = jnp.concatenate([grad_queries, grad_keys, grad_values], axis=1)
-    weights_joined = jnp.concatenate([w_query, w_key, w_value], axis=1)
-    grad_one = lax.psum_scatter(
-        contract_cols(grad_joined, weights_joined).astype(jnp.bfloat16),
-        "heads",
-        scatter_dimension=1,
-        tiled=True,
-    ).astype(jnp.float32)
-    grad_in1, scale_one, shift_one = norm_back(grad_one, normed1, inverse1, 0)
-    grad_inputs = grad_mid + grad_in1
-    grad_table = jnp.stack([scale_one, shift_one, scale_two, shift_two])
-    up_total, down_total, query_total, key_total, value_total, out_total, table_total = lax.psum(
-        (grad_up, grad_down, grad_query, grad_key, grad_value, grad_out, grad_table), "nodes"
-    )
+    grad_queries, grad_keys, grad_values = attend_back(
+        weights, inverse_sum, queries, keys_t, values, grad_t
+    )
+    grad_keys = grad_keys.astype(bf16)
+    grad_values = grad_values.astype(bf16)
+    grad_query = dot(normed_one, grad_queries, 0, 0)
+    grad_key = dot(normed_all, grad_keys, 0, 0)
+    grad_value = dot(normed_all, grad_values, 0, 0)
+    one_part = dot(
+        jnp.concatenate([grad_keys, grad_values], axis=1),
+        jnp.concatenate([w_key, w_value], axis=1),
+        1,
+        1,
+    )
+    one_part = one_part.at[rows : 2 * rows].add(dot(grad_queries, w_query, 1, 1))
+    one_other = swapped(theirs(one_part).astype(bf16), "heads", 1)
+    one_all = mine(one_part) + one_other.astype(f32)
+    to_before = passed_along(one_all[:rows].astype(bf16), "nodes", -1)
+    to_after = passed_along(one_all[2 * rows :].astype(bf16), "nodes", 1)
+    normed1_mine = mine(normed1)
+    scale_one = dot(onehot_all, (one_all * normed1_mine).astype(bf16), 0, 0)
+    shift_one = dot(onehot_all, one_all.astype(bf16), 0, 0)
+    first_set = jnp.concatenate([grad_query, grad_key], axis=0)
+    table = jnp.concatenate([scale_one, shift_one, scale_two, shift_two], axis=0)
+    second_set = jnp.concatenate(
+        [grad_value, grad_out[:, :half], grad_out[:, half:], table, jnp.zeros_like(table)], axis=0
+    )
+    first_total = total_of(first_set, "nodes", False).astype(f32)
+    second_total = total_of(second_set, "nodes", True).astype(f32)
+
+    grad_one = (
+        one_all[rows : 2 * rows] + to_before.astype(f32) + to_after.astype(f32)
+    )
+    normed_mine = normed1_mine[rows : 2 * rows]
+    scale_mine = dot(
+        jnp.concatenate([onehot] * 3, axis=1), mine(tables[0]), 1, 0
+    )
+    gained = grad_one * (1.0 + scale_mine)
+    sum_gain, sum_cross = lax.psum(
+        (jnp.sum(gained, axis=1), jnp.sum(gained * normed_mine, axis=1)), "heads"
+    )
+    grad_inputs = mine(grad_mid) + inverse1[rows : 2 * rows] * (
+        gained - sum_gain[:, None] / width - normed_mine * sum_cross[:, None] / width
+    )
+    depth = w_query.shape[0]
+    out_rows = w_out.shape[0]
+    spots = [depth, depth + out_rows, depth + 2 * out_rows]
     return (
         output,
         grad_inputs,
-        query_total,
-        key_total,
-        value_total,
-        out_total,
+        first_total[:depth],
+        first_total[depth:],
+        second_total[:depth],
+        jnp.concatenate([second_total[spots[0] : spots[1]], second_total[spots[1] : spots[2]]], 1),
         up_total,
         down_total,
-        table_total,
+        second_total[spots[2] : spots[2] + 4 * levels].reshape(4, levels, half),
     )
 
 

time: 461 us -> 281 us (0.61)
  waiting for transfers between devices: 295 us -> 70.9 us
  starting transfers between devices: 13 us -> 61.3 us
  other arithmetic: 18.8 us -> 38.3 us
  matrix products: 46.6 us -> 34.1 us
  local copies, waits for them, and re-layouts: 23.7 us -> 13.4 us
  blocking collectives: 15.8 us -> 9.4 us
    psum x1 -> x0, waiting for transfers between devices: 213 us -> none  [body(): lax.psum((grad_up, grad_down, grad_query, grad_key, grad_value, grad_out,...]
    dot_general x25 -> x0, matrix products: 45.2 us -> none  [the longest x10 18.2 us: contract_rows(): lax.dot_general(left, right, (((0,), (0,)), ((), ())), precision=precisio...]
    ppermute x2 -> x36, starting transfers between devices: 6.86 us -> 46.6 us  [swapped(): return lax.ppermute(block, axis, [(i, i ^ bit) for i in devices])]
    dot_general x1 -> x26, matrix products: 1.41 us -> 34.1 us  [dot(): lax.dot_general(left, right, (((left_dim,), (right_dim,)), ((), ())), pre...]
    ppermute x2 -> x6, waiting for transfers between devices: 37.5 us -> 8.8 us  [passed_along(): return lax.ppermute(block, axis, route)]
    ppermute x2 -> x36, waiting for transfers between devices: 34.1 us -> 59 us  [swapped(): return lax.ppermute(block, axis, [(i, i ^ bit) for i in devices])]
    unnamed x94 -> x65, local copies, waits for them, and re-layouts: 16.9 us -> 3.38 us
    reduce_scatter x4 -> x0, waiting for transfers between devices: 9.55 us -> none  [the longest x1 5.6 us: body(): lax.psum_scatter(contract_cols(grad_pre, w_up).astype(jnp.bfloat16), 'hea...]
  transfers between devices with their start and end apart: 9 -> 43, of which waited for: 7 -> 25; matrix products, arithmetic and copies ran while one was open for 9% -> 17% of each run, Pallas kernels for 0% -> 7%
where the time goes in v2:
time: 281 us; the launch traced here: 277 us
  waiting for transfers between devices  70.9 us (25%)
  starting transfers between devices  61.3 us (22%)
  other arithmetic  38.3 us (14%)
  Pallas kernels  34.2 us (12%)
  matrix products  34.1 us (12%)
  between operations  15.1 us (5%)
  local copies, waits for them, and re-layouts  13.4 us (5%)
  blocking collectives  9.4 us (3%)
    ppermute x36, waiting for transfers between devices, swapped(): return lax.ppermute(block, axis, [(i, i ^ bit) for i in devices])  59 us
    ppermute x36, starting transfers between devices, swapped(): return lax.ppermute(block, axis, [(i, i ^ bit) for i in devices])  46.6 us
    dot_general x26, matrix products, dot(): lax.dot_general(left, right, (((left_dim,), (right_dim,)), ((), ())), pre...  34.1 us
    pallas_call x1, Pallas kernels, attend_back(): pl.pallas_call(backward_kernel, grid=(blocks,), in_specs=[pl.BlockSpec((1...  18.3 us
    pallas_call x1, Pallas kernels, attend(): pl.pallas_call(forward_kernel, grid=(blocks,), in_specs=[pl.BlockSpec(pla...  16 us
    ppermute x6, starting transfers between devices, passed_along(): return lax.ppermute(block, axis, route)  14.7 us
    ppermute x6, waiting for transfers between devices, passed_along(): return lax.ppermute(block, axis, route)  8.8 us
    all_gather x2, blocking collectives, whole(): return lax.all_gather(block, 'heads', axis=1, tiled=True)  6.94 us
  transfers between devices with their start and end apart: 43, of which 25 were waited for; matrix products, arithmetic and copies ran while one was open for 17% of the time, Pallas kernels for 7%

profile of v2, /device:TPU:0, one launch (start us, length us, event | category | flops | bytes accessed | tf_op | source)
XLA Modules:
  0.0 276.7 jit_solution(10925170767722691636)
XLA Ops:
  7.2 7.0 %collective-permute-start.3 = (s32[896]{0:T(1024)}, s32[896]{0:T(1024)S(1)}, u32[]{:S(2)}, u32[]{:S(2)}) collective-permute-start(s32[896]{0:T(1024)} %param.21), channel_id=1, source_target_pairs={{2,0},{4,2},{6,4},{8,6},{10,8},{12,10},{14,12},{16,14},{18,16},{20... | collective-permute-start | bytes 10760 | tf_op jit(solution)/shard_map/ppermute | solution.py:184
  14.2 5.6 %collective-permute-start.1 = (bf16[896,256]{1,0:T(8,128)(2,1)}, bf16[896,256]{1,0:T(8,128)(2,1)S(1)}, u32[]{:S(2)}, u32[]{:S(2)}) collective-permute-start(bf16[896,256]{1,0:T(8,128)(2,1)} %param.13), channel_id=1, source_target_pairs={{2,0},{4,2},{6,4},{8,6},{10,8},{12,10},{14,12},{16,14},{18,16},{20... | collective-permute-start | bytes 1376264 | tf_op jit(solution)/shard_map/ppermute | solution.py:184
  21.3 4.3 %all_gather.9 = bf16[896,512]{1,0:T(8,128)(2,1)} all-gather(bf16[896,256]{1,0:T(8,128)(2,1)} %param.13), channel_id=1, replica_groups=mesh['nodes'=16,'heads'=2] {'heads'}, dimensions={1}, use_global_device_ids=true | all-gather | bytes 1376256 | tf_op jit(solution)/shard_map/all_gather | solution.py:270
  26.5 2.9 %collective-permute-done.1 = bf16[896,256]{1,0:T(8,128)(2,1)S(1)} collective-permute-done((bf16[896,256]{1,0:T(8,128)(2,1)}, bf16[896,256]{1,0:T(8,128)(2,1)S(1)}, u32[]{:S(2)}, u32[]{:S(2)}) %collective-permute-start.1) | collective-permute-done | bytes 458784 | tf_op jit(solution)/shard_map/ppermute | solution.py:184
  29.4 5.9 %collective-permute-done = bf16[896,256]{1,0:T(8,128)(2,1)S(1)} collective-permute-done((bf16[896,256]{1,0:T(8,128)(2,1)}, bf16[896,256]{1,0:T(8,128)(2,1)S(1)}, u32[]{:S(2)}, u32[]{:S(2)}) %collective-permute-start) | collective-permute-done | bytes 458784 | tf_op jit(solution)/shard_map/ppermute | solution.py:184
  36.4 2.6 all_gather.11
  40.8 3.4 %fusion.39 = f32[2688,512]{1,0:T(8,128)} fusion(pred[2688,16]{0,1:T(8,128)(4,1)S(1)} %iota_compare_fusion, bf16[16,512]{1,0:T(8,128)(2,1)S(1)} %get-tuple-element.60, bf16[16,512]{1,0:T(8,128)(2,1)S(1)} %get-tuple-element.61, bf16[16,512]{1,0:T(8,128)(2,1)S(1)} %get-tuple-element.66), kind=kOutput, calls=%fused_computation.126 | convolution fusion | flops 132526080 | bytes 5597184 | tf_op jit(solution)/shard_map/dot_general | solution.py:22
  44.2 3.1 %all-gather.2.cloned.1.call-done = bf16[1792,512]{1,0:T(8,128)(2,1)} async-done(((bf16[1792,256]{1,0:T(8,128)(2,1)}), bf16[1792,512]{1,0:T(8,128)(2,1)}) %all-gather.2.cloned.1.call-update) | async-done | bytes 1835024 | tf_op jit(solution)/shard_map/all_gather | solution.py:270
  49.5 6.3 %fusion.2 = f32[2688]{0:T(1024)S(1)} fusion(f32[2688]{0:T(1024)S(1)} %broadcast_multiply_fusion, bf16[896,512]{1,0:T(8,128)(2,1)S(1)} %get-tuple-element.47, bf16[896,512]{1,0:T(8,128)(2,1)S(1)} %copy-done.5, bf16[896,512]{1,0:T(8,128)(2,1)S(1)} %get-tuple-element.46), kind=kLoop, calls=%fused_computation.4 | loop fusion | flops 12383616 | bytes 2774016 | tf_op jit(solution)/shard_map/reduce_sum | solution.py:230
  55.9 5.7 %add_convert_fusion = bf16[2688,512]{1,0:T(8,128)(2,1)S(1)} fusion(f32[2688,512]{1,0:T(8,128)S(1)} %copy-done.16, pred[2688,16]{0,1:T(8,128)(4,1)S(1)} %iota_compare_fusion, bf16[16,512]{1,0:T(8,128)(2,1)S(1)} %get-tuple-element.59, bf16[16,512]{1,0:T(8,128)(2,1)S(1)} %get-tuple-element.62, bf16[16,512]{1,0:T(8,128)(2,1)S(1)} %get-tuple-element.65, ...), kind=kOutput, calls=%fused_computation.5 | convolution fusion | flops 149041152 | bytes 11123712 | tf_op jit(solution)/shard_map/dot_general | solution.py:22
  67.2 2.5 copy.32.k_ref
  69.8 2.6 copy.33.vt_ref
  72.3 16.0 %attend_forward.1 = (bf16[7,1920,256]{2,1,0:T(8,128)(2,1)}, bf16[896,256]{1,0:T(8,128)(2,1)}, f32[7,8,256]{2,1,0:T(8,128)}) custom-call(s32[16,896]{1,0:T(8,128)} %add_select_fusion.nbr_ref, bf16[896,256]{1,0:T(8,128)(2,1)} %convolution_convert_fusion.6.q_ref, bf16[2688,256]{1,0:T(8,128)(2,1)} %copy.32.k_ref, bf16[256,2688]{1,0:T(8,128)(2,1)} %copy.33.vt_ref), custom_call_target="tpu_custom_call" | custom-call | tf_op jit(solution)/shard_map/attend_forward/pallas_call | solution.py:82
  90.0 5.2 %fusion = f32[2688,512]{1,0:T(8,128)S(1)} fusion(f32[2688]{0:T(1024)S(1)} %add_rsqrt_fusion, f32[2688]{0:T(1024)S(1)} %broadcast_multiply_fusion, bf16[896,512]{1,0:T(8,128)(2,1)S(1)} %copy-done.11, bf16[896,512]{1,0:T(8,128)(2,1)S(1)} %copy-done.6, bf16[896,512]{1,0:T(8,128)(2,1)S(1)} %copy-done.9), kind=kLoop, calls=%fused_computation.2 | loop fusion | flops 11010048 | bytes 8279040 | tf_op jit(solution)/shard_map/mul | solution.py:232
  112.9 6.4 %collective-permute-done.26 = bf16[256,1024]{1,0:T(8,128)(2,1)S(1)} collective-permute-done((bf16[256,1024]{1,0:T(8,128)(2,1)S(1)}, bf16[256,1024]{1,0:T(8,128)(2,1)S(1)}, u32[]{:S(2)}, u32[]{:S(2)}) %collective-permute-start.26) | collective-permute-done | bytes 524320 | tf_op jit(solution)/shard_map/ppermute | solution.py:189
  121.5 3.5 %collective-permute-done.34 = bf16[512,512]{1,0:T(8,128)(2,1)S(1)} collective-permute-done((bf16[512,512]{1,0:T(8,128)(2,1)S(1)}, bf16[512,512]{1,0:T(8,128)(2,1)S(1)}, u32[]{:S(2)}, u32[]{:S(2)}) %collective-permute-start.34) | collective-permute-done | bytes 524320 | tf_op jit(solution)/shard_map/ppermute | solution.py:189
  125.5 4.2 %collective-permute-done.27 = bf16[128,1024]{1,0:T(8,128)(2,1)S(1)} collective-permute-done((bf16[128,1024]{1,0:T(8,128)(2,1)S(1)}, bf16[128,1024]{1,0:T(8,128)(2,1)S(1)}, u32[]{:S(2)}, u32[]{:S(2)}) %collective-permute-start.27) | collective-permute-done | bytes 262176 | tf_op jit(solution)/shard_map/ppermute | solution.py:189
  143.6 18.3 %attend_backward.1 = (bf16[896,256]{1,0:T(8,128)(2,1)}, f32[2688,256]{1,0:T(8,128)}, f32[2688,256]{1,0:T(8,128)}) custom-call(bf16[7,1920,256]{2,1,0:T(8,128)(2,1)} %get-tuple-element.28.e_ref, f32[7,8,256]{2,1,0:T(8,128)} %get-tuple-element.29.inv_ref, bf16[896,256]{1,0:T(8,128)(2,1)} %convolution_convert_fusion.6.q_ref, bf16[256,2688]{1,0:T(8,128)(2,1)} %bitcast.72, ...), custom_call_target="tpu_custom_call" | custom-call | tf_op jit(solution)/shard_map/attend_backward/pallas_call | solution.py:151
  173.8 3.0 %collective-permute-done.10 = bf16[512,256]{1,0:T(8,128)(2,1)S(1)} collective-permute-done((bf16[512,256]{1,0:T(8,128)(2,1)S(1)}, bf16[512,256]{1,0:T(8,128)(2,1)S(1)}, u32[]{:S(2)}, u32[]{:S(2)}) %collective-permute-start.10) | collective-permute-done | bytes 262176 | tf_op jit(solution)/shard_map/ppermute | solution.py:189
  178.5 3.5 %collective-permute-done.11 = bf16[256,256]{1,0:T(8,128)(2,1)S(1)} collective-permute-done((bf16[256,256]{1,0:T(8,128)(2,1)S(1)}, bf16[256,256]{1,0:T(8,128)(2,1)S(1)}, u32[]{:S(2)}, u32[]{:S(2)}) %collective-permute-start.11) | collective-permute-done | bytes 131104 | tf_op jit(solution)/shard_map/ppermute | solution.py:189
  184.4 2.5 collective-permute-start.30
  186.9 2.5 collective-permute-start.13
  191.9 2.5 collective-permute-start.14
  204.2 3.2 %collective-permute-done.16 = bf16[256,256]{1,0:T(8,128)(2,1)S(1)} collective-permute-done((bf16[256,256]{1,0:T(8,128)(2,1)S(1)}, bf16[256,256]{1,0:T(8,128)(2,1)S(1)}, u32[]{:S(2)}, u32[]{:S(2)}) %collective-permute-start.16) | collective-permute-done | bytes 131104 | tf_op jit(solution)/shard_map/ppermute | solution.py:189
  215.7 2.7 collective-permute-done.17
  222.5 3.7 %collective-permute-done.19 = bf16[288,256]{1,0:T(8,128)(2,1)S(1)} collective-permute-done((bf16[288,256]{1,0:T(8,128)(2,1)S(1)}, bf16[288,256]{1,0:T(8,128)(2,1)S(1)}, u32[]{:S(2)}, u32[]{:S(2)}) %collective-permute-start.19) | collective-permute-done | bytes 147488 | tf_op jit(solution)/shard_map/ppermute | solution.py:189
  228.2 3.4 %collective-permute-done.20 = bf16[144,256]{1,0:T(8,128)(2,1)S(1)} collective-permute-done((bf16[144,256]{1,0:T(8,128)(2,1)S(1)}, bf16[144,256]{1,0:T(8,128)(2,1)S(1)}, u32[]{:S(2)}, u32[]{:S(2)}) %collective-permute-start.20) | collective-permute-done | bytes 73760 | tf_op jit(solution)/shard_map/ppermute | solution.py:189
  240.8 3.4 %collective-permute-done.22 = bf16[72,256]{1,0:T(8,128)(2,1)S(1)} collective-permute-done((bf16[72,256]{1,0:T(8,128)(2,1)S(1)}, bf16[72,256]{1,0:T(8,128)(2,1)S(1)}, u32[]{:S(2)}, u32[]{:S(2)}) %collective-permute-start.22) | collective-permute-done | bytes 36896 | tf_op jit(solution)/shard_map/ppermute | solution.py:189
  244.3 4.8 %collective-permute-start.23 = (bf16[144,256]{1,0:T(8,128)(2,1)S(1)}, bf16[144,256]{1,0:T(8,128)(2,1)S(1)}, u32[]{:S(2)}, u32[]{:S(2)}) collective-permute-start(bf16[144,256]{1,0:T(8,128)(2,1)S(1)} %maximum_select_fusion.14), channel_id=1, source_target_pairs={{0,8},{2,10},{4,12},{6,14},{8,0},{10,2},{12,4},{14,6},{16,24},{18,... | collective-permute-start | bytes 221192 | tf_op jit(solution)/shard_map/ppermute | solution.py:189
  253.3 5.5 %collective-permute-done.24 = bf16[288,256]{1,0:T(8,128)(2,1)S(1)} collective-permute-done((bf16[288,256]{1,0:T(8,128)(2,1)S(1)}, bf16[288,256]{1,0:T(8,128)(2,1)S(1)}, u32[]{:S(2)}, u32[]{:S(2)}) %collective-permute-start.24) | collective-permute-done | bytes 147488 | tf_op jit(solution)/shard_map/ppermute | solution.py:189
  259.5 2.9 %fusion.21 = f32[896,256]{1,0:T(8,128)} fusion(f32[896,512]{1,0:T(8,128)S(1)} %multiply_add_fusion, f32[896,256]{1,0:T(8,128)} %get-tuple-element.39, f32[2688,256]{1,0:T(8,128)} %slice_select_fusion, f32[896]{0:T(1024)S(1)} %get-tuple-element.37, f32[896]{0:T(1024)S(1)} %broadcast_multiply_fusion.1, f32[896]{0:T(1024)S(1)} %copy-done.28, pred[]{:T(512)S(6)} %eq.15), kind=kLoop, calls=%fused_computation.65 | loop fusion | flops 1605632 | bytes 4598273 | tf_op jit(solution)/shard_map/add | solution.py:381
  262.4 4.8 %collective-permute-done.25 = bf16[576,256]{1,0:T(8,128)(2,1)S(1)} collective-permute-done((bf16[576,256]{1,0:T(8,128)(2,1)S(1)}, bf16[576,256]{1,0:T(8,128)(2,1)S(1)}, u32[]{:S(2)}, u32[]{:S(2)}) %collective-permute-start.25) | collective-permute-done | bytes 294944 | tf_op jit(solution)/shard_map/ppermute | solution.py:189
  (240 shorter events, 107.8 us)
Async XLA Ops:
  7.2 40.1 %all-gather.2.cloned.1.call-start = ((), (), s32[]{:S(2)}) async-start(), calls=%async_computation | async-start | bytes 2752512 | tf_op jit(solution)/shard_map/all_gather | solution.py:270
  7.2 33.5 %collective-permute-start.3 = (s32[896]{0:T(1024)}, s32[896]{0:T(1024)S(1)}, u32[]{:S(2)}, u32[]{:S(2)}) collective-permute-start(s32[896]{0:T(1024)} %param.21), channel_id=1, source_target_pairs={{2,0},{4,2},{6,4},{8,6},{10,8},{12,10},{14,12},{16,14},{18,16},{20... | collective-permute-start | bytes 10760 | tf_op jit(solution)/shard_map/ppermute | solution.py:184
  14.2 26.5 %collective-permute-start.2 = (s32[896]{0:T(1024)}, s32[896]{0:T(1024)S(1)}, u32[]{:S(2)}, u32[]{:S(2)}) collective-permute-start(s32[896]{0:T(1024)} %param.21), channel_id=1, source_target_pairs={{30,0},{0,2},{2,4},{4,6},{6,8},{8,10},{10,12},{12,14},{14,16},{16,... | collective-permute-start | bytes 10760 | tf_op jit(solution)/shard_map/ppermute | solution.py:184
  14.2 15.2 %collective-permute-start.1 = (bf16[896,256]{1,0:T(8,128)(2,1)}, bf16[896,256]{1,0:T(8,128)(2,1)S(1)}, u32[]{:S(2)}, u32[]{:S(2)}) collective-permute-start(bf16[896,256]{1,0:T(8,128)(2,1)} %param.13), channel_id=1, source_target_pairs={{2,0},{4,2},{6,4},{8,6},{10,8},{12,10},{14,12},{16,14},{18,16},{20... | collective-permute-start | bytes 1376264 | tf_op jit(solution)/shard_map/ppermute | solution.py:184
  19.8 15.5 %collective-permute-start = (bf16[896,256]{1,0:T(8,128)(2,1)}, bf16[896,256]{1,0:T(8,128)(2,1)S(1)}, u32[]{:S(2)}, u32[]{:S(2)}) collective-permute-start(bf16[896,256]{1,0:T(8,128)(2,1)} %param.13), channel_id=1, source_target_pairs={{30,0},{0,2},{2,4},{4,6},{6,8},{8,10},{10,12},{12,14},{14,16},{16,... | collective-permute-start | bytes 1376264 | tf_op jit(solution)/shard_map/ppermute | solution.py:184
  89.7 8.1 %collective-permute-start.4 = (bf16[896,512]{1,0:T(8,128)(2,1)S(1)}, bf16[896,512]{1,0:T(8,128)(2,1)S(1)}, u32[]{:S(2)}, u32[]{:S(2)}) collective-permute-start(bf16[896,512]{1,0:T(8,128)(2,1)S(1)} %convolution_convert_fusion.5), channel_id=1, source_target_pairs={{0,1},{1,0},{2,3},{3,2},{4,5},{5,4},{6,7},{7,6},{8,9},{9,8},{10,11... | collective-permute-start | bytes 2752520 | tf_op jit(solution)/shard_map/ppermute | solution.py:189
  105.2 14.2 %collective-permute-start.26 = (bf16[256,1024]{1,0:T(8,128)(2,1)S(1)}, bf16[256,1024]{1,0:T(8,128)(2,1)S(1)}, u32[]{:S(2)}, u32[]{:S(2)}) collective-permute-start(bf16[256,1024]{1,0:T(8,128)(2,1)S(1)} %broadcast_select_fusion.1), channel_id=1, source_target_pairs={{0,2},{2,0},{4,6},{6,4},{8,10},{10,8},{12,14},{14,12},{16,18},{18,... | collective-permute-start | bytes 1572872 | tf_op jit(solution)/shard_map/ppermute | solution.py:189
  107.0 32.0 %collective-permute-start.6 = (bf16[896,512]{1,0:T(8,128)(2,1)S(1)}, bf16[896,512]{1,0:T(8,128)(2,1)S(1)}, u32[]{:S(2)}, u32[]{:S(2)}) collective-permute-start(bf16[896,512]{1,0:T(8,128)(2,1)S(1)} %convolution_convert_fusion.4), channel_id=1, source_target_pairs={{0,1},{1,0},{2,3},{3,2},{4,5},{5,4},{6,7},{7,6},{8,9},{9,8},{10,11... | collective-permute-start | bytes 2752520 | tf_op jit(solution)/shard_map/ppermute | solution.py:189
  110.2 14.8 %collective-permute-start.34 = (bf16[512,512]{1,0:T(8,128)(2,1)S(1)}, bf16[512,512]{1,0:T(8,128)(2,1)S(1)}, u32[]{:S(2)}, u32[]{:S(2)}) collective-permute-start(bf16[512,512]{1,0:T(8,128)(2,1)S(1)} %broadcast_select_fusion), channel_id=1, source_target_pairs={{0,4},{2,6},{4,0},{6,2},{8,12},{10,14},{12,8},{14,10},{16,20},{18,... | collective-permute-start | bytes 1572872 | tf_op jit(solution)/shard_map/ppermute | solution.py:189
  119.7 10.0 %collective-permute-start.27 = (bf16[128,1024]{1,0:T(8,128)(2,1)S(1)}, bf16[128,1024]{1,0:T(8,128)(2,1)S(1)}, u32[]{:S(2)}, u32[]{:S(2)}) collective-permute-start(bf16[128,1024]{1,0:T(8,128)(2,1)S(1)} %broadcast_select_fusion.4), channel_id=1, source_target_pairs={{0,4},{2,6},{4,0},{6,2},{8,12},{10,14},{12,8},{14,10},{16,20},{18,... | collective-permute-start | bytes 786440 | tf_op jit(solution)/shard_map/ppermute | solution.py:189
  125.3 6.5 %collective-permute-start.35 = (bf16[256,512]{1,0:T(8,128)(2,1)S(1)}, bf16[256,512]{1,0:T(8,128)(2,1)S(1)}, u32[]{:S(2)}, u32[]{:S(2)}) collective-permute-start(bf16[256,512]{1,0:T(8,128)(2,1)S(1)} %broadcast_select_fusion.3), channel_id=1, source_target_pairs={{0,2},{2,0},{4,6},{6,4},{8,10},{10,8},{12,14},{14,12},{16,18},{18,... | collective-permute-start | bytes 786440 | tf_op jit(solution)/shard_map/ppermute | solution.py:189
  129.9 6.0 %collective-permute-start.28 = (bf16[64,1024]{1,0:T(8,128)(2,1)S(1)}, bf16[64,1024]{1,0:T(8,128)(2,1)S(1)}, u32[]{:S(2)}, u32[]{:S(2)}) collective-permute-start(bf16[64,1024]{1,0:T(8,128)(2,1)S(1)} %broadcast_select_fusion.8), channel_id=1, source_target_pairs={{0,8},{2,10},{4,12},{6,14},{8,0},{10,2},{12,4},{14,6},{16,24},{18,... | collective-permute-start | bytes 393224 | tf_op jit(solution)/shard_map/ppermute | solution.py:189
  131.9 37.2 %collective-permute-start.36 = (bf16[128,512]{1,0:T(8,128)(2,1)S(1)}, bf16[128,512]{1,0:T(8,128)(2,1)S(1)}, u32[]{:S(2)}, u32[]{:S(2)}) collective-permute-start(bf16[128,512]{1,0:T(8,128)(2,1)S(1)} %broadcast_select_fusion.7), channel_id=1, source_target_pairs={{0,8},{2,10},{4,12},{6,14},{8,0},{10,2},{12,4},{14,6},{16,24},{18,... | collective-permute-start | bytes 393224 | tf_op jit(solution)/shard_map/ppermute | solution.py:189
  136.6 46.9 %collective-permute-start.29 = (bf16[32,1024]{1,0:T(8,128)(2,1)}, bf16[32,1024]{1,0:T(8,128)(2,1)}, u32[]{:S(2)}, u32[]{:S(2)}) collective-permute-start(bf16[32,1024]{1,0:T(8,128)(2,1)} %broadcast_select_fusion.12), channel_id=1, source_target_pairs={{0,16},{2,18},{4,20},{6,22},{8,24},{10,26},{12,28},{14,30},{16,0},... | collective-permute-start | bytes 196616 | tf_op jit(solution)/shard_map/ppermute | solution.py:189
  169.2 20.2 %collective-permute-start.37 = (bf16[64,512]{1,0:T(8,128)(2,1)S(1)}, bf16[64,512]{1,0:T(8,128)(2,1)S(1)}, u32[]{:S(2)}, u32[]{:S(2)}) collective-permute-start(bf16[64,512]{1,0:T(8,128)(2,1)S(1)} %broadcast_select_fusion.11), channel_id=1, source_target_pairs={{0,16},{2,18},{4,20},{6,22},{8,24},{10,26},{12,28},{14,30},{16,0},... | collective-permute-start | bytes 196616 | tf_op jit(solution)/shard_map/ppermute | solution.py:189
  170.3 6.4 %collective-permute-start.10 = (bf16[512,256]{1,0:T(8,128)(2,1)S(1)}, bf16[512,256]{1,0:T(8,128)(2,1)S(1)}, u32[]{:S(2)}, u32[]{:S(2)}) collective-permute-start(bf16[512,256]{1,0:T(8,128)(2,1)S(1)} %get-tuple-element.70), channel_id=1, source_target_pairs={{0,2},{2,0},{4,6},{6,4},{8,10},{10,8},{12,14},{14,12},{16,18},{18,... | collective-permute-start | bytes 786440 | tf_op jit(solution)/shard_map/ppermute | solution.py:189
  171.7 36.5 %collective-permute-start.7 = (bf16[2688,256]{1,0:T(8,128)(2,1)S(1)}, bf16[2688,256]{1,0:T(8,128)(2,1)S(1)}, u32[]{:S(2)}, u32[]{:S(2)}) collective-permute-start(bf16[2688,256]{1,0:T(8,128)(2,1)S(1)} %select_convert_fusion), channel_id=1, source_target_pairs={{0,1},{1,0},{2,3},{3,2},{4,5},{5,4},{6,7},{7,6},{8,9},{9,8},{10,11... | collective-permute-start | bytes 4128776 | tf_op jit(solution)/shard_map/ppermute | solution.py:189
  184.4 9.9 %collective-permute-start.30 = (bf16[32,1024]{1,0:T(8,128)(2,1)S(1)}, bf16[32,1024]{1,0:T(8,128)(2,1)S(1)}, u32[]{:S(2)}, u32[]{:S(2)}) collective-permute-start(bf16[32,1024]{1,0:T(8,128)(2,1)S(1)} %add_convert_fusion.14), channel_id=1, source_target_pairs={{0,16},{2,18},{4,20},{6,22},{8,24},{10,26},{12,28},{14,30},{16,0},... | collective-permute-start | bytes 196616 | tf_op jit(solution)/shard_map/ppermute | solution.py:189
  189.5 8.9 %collective-permute-start.38 = (bf16[64,512]{1,0:T(8,128)(2,1)S(1)}, bf16[64,512]{1,0:T(8,128)(2,1)S(1)}, u32[]{:S(2)}, u32[]{:S(2)}) collective-permute-start(bf16[64,512]{1,0:T(8,128)(2,1)S(1)} %add_convert_fusion.13), channel_id=1, source_target_pairs={{0,16},{2,18},{4,20},{6,22},{8,24},{10,26},{12,28},{14,30},{16,0},... | collective-permute-start | bytes 196616 | tf_op jit(solution)/shard_map/ppermute | solution.py:189
  194.4 8.3 %collective-permute-start.31 = (bf16[64,1024]{1,0:T(8,128)(2,1)S(1)}, bf16[64,1024]{1,0:T(8,128)(2,1)S(1)}, u32[]{:S(2)}, u32[]{:S(2)}) collective-permute-start(bf16[64,1024]{1,0:T(8,128)(2,1)S(1)} %maximum_select_fusion.12), channel_id=1, source_target_pairs={{0,8},{2,10},{4,12},{6,14},{8,0},{10,2},{12,4},{14,6},{16,24},{18,... | collective-permute-start | bytes 393224 | tf_op jit(solution)/shard_map/ppermute | solution.py:189
  201.1 6.3 %collective-permute-start.16 = (bf16[256,256]{1,0:T(8,128)(2,1)S(1)}, bf16[256,256]{1,0:T(8,128)(2,1)S(1)}, u32[]{:S(2)}, u32[]{:S(2)}) collective-permute-start(bf16[256,256]{1,0:T(8,128)(2,1)S(1)} %maximum_select_fusion.11), channel_id=1, source_target_pairs={{0,4},{2,6},{4,0},{6,2},{8,12},{10,14},{12,8},{14,10},{16,20},{18,... | collective-permute-start | bytes 393224 | tf_op jit(solution)/shard_map/ppermute | solution.py:189
  202.7 10.3 %collective-permute-start.32 = (bf16[128,1024]{1,0:T(8,128)(2,1)S(1)}, bf16[128,1024]{1,0:T(8,128)(2,1)S(1)}, u32[]{:S(2)}, u32[]{:S(2)}) collective-permute-start(bf16[128,1024]{1,0:T(8,128)(2,1)S(1)} %maximum_select_fusion.8), channel_id=1, source_target_pairs={{0,4},{2,6},{4,0},{6,2},{8,12},{10,14},{12,8},{14,10},{16,20},{18,... | collective-permute-start | bytes 786440 | tf_op jit(solution)/shard_map/ppermute | solution.py:189
  203.5 10.3 %collective-permute-start.40 = (bf16[256,512]{1,0:T(8,128)(2,1)S(1)}, bf16[256,512]{1,0:T(8,128)(2,1)S(1)}, u32[]{:S(2)}, u32[]{:S(2)}) collective-permute-start(bf16[256,512]{1,0:T(8,128)(2,1)S(1)} %maximum_select_fusion.9), channel_id=1, source_target_pairs={{0,2},{2,0},{4,6},{6,4},{8,10},{10,8},{12,14},{14,12},{16,18},{18,... | collective-permute-start | bytes 786440 | tf_op jit(solution)/shard_map/ppermute | solution.py:189
  207.5 10.8 %collective-permute-start.17 = (bf16[512,256]{1,0:T(8,128)(2,1)S(1)}, bf16[512,256]{1,0:T(8,128)(2,1)S(1)}, u32[]{:S(2)}, u32[]{:S(2)}) collective-permute-start(bf16[512,256]{1,0:T(8,128)(2,1)S(1)} %maximum_select_fusion.7), channel_id=1, source_target_pairs={{0,2},{2,0},{4,6},{6,4},{8,10},{10,8},{12,14},{14,12},{16,18},{18,... | collective-permute-start | bytes 786440 | tf_op jit(solution)/shard_map/ppermute | solution.py:189
  210.4 10.0 %collective-permute-start.18 = (bf16[576,256]{1,0:T(8,128)(2,1)S(1)}, bf16[576,256]{1,0:T(8,128)(2,1)S(1)}, u32[]{:S(2)}, u32[]{:S(2)}) collective-permute-start(bf16[576,256]{1,0:T(8,128)(2,1)S(1)} %broadcast_select_fusion.2), channel_id=1, source_target_pairs={{0,4},{2,6},{4,0},{6,2},{8,12},{10,14},{12,8},{14,10},{16,20},{18,... | collective-permute-start | bytes 884744 | tf_op jit(solution)/shard_map/ppermute | solution.py:189
  213.2 25.9 %collective-permute-start.33 = (bf16[256,1024]{1,0:T(8,128)(2,1)S(1)}, bf16[256,1024]{1,0:T(8,128)(2,1)S(1)}, u32[]{:S(2)}, u32[]{:S(2)}) collective-permute-start(bf16[256,1024]{1,0:T(8,128)(2,1)S(1)} %maximum_select_fusion.4), channel_id=1, source_target_pairs={{0,2},{2,0},{4,6},{6,4},{8,10},{10,8},{12,14},{14,12},{16,18},{18,... | collective-permute-start | bytes 1572872 | tf_op jit(solution)/shard_map/ppermute | solution.py:189
  214.1 12.5 %collective-permute-start.41 = (bf16[512,512]{1,0:T(8,128)(2,1)S(1)}, bf16[512,512]{1,0:T(8,128)(2,1)S(1)}, u32[]{:S(2)}, u32[]{:S(2)}) collective-permute-start(bf16[512,512]{1,0:T(8,128)(2,1)S(1)} %maximum_select_fusion.5), channel_id=1, source_target_pairs={{0,4},{2,6},{4,0},{6,2},{8,12},{10,14},{12,8},{14,10},{16,20},{18,... | collective-permute-start | bytes 1572872 | tf_op jit(solution)/shard_map/ppermute | solution.py:189
  234.0 15.0 %collective-permute-start.8 = (bf16[896,256]{1,0:T(8,128)(2,1)S(1)}, bf16[896,256]{1,0:T(8,128)(2,1)S(1)}, u32[]{:S(2)}, u32[]{:S(2)}) collective-permute-start(bf16[896,256]{1,0:T(8,128)(2,1)S(1)} %get-tuple-element.48), channel_id=1, source_target_pairs={{2,0},{4,2},{6,4},{8,6},{10,8},{12,10},{14,12},{16,14},{18,16},{20... | collective-permute-start | bytes 1376264 | tf_op jit(solution)/shard_map/ppermute | solution.py:184
  235.2 13.8 %collective-permute-start.9 = (bf16[896,256]{1,0:T(8,128)(2,1)S(1)}, bf16[896,256]{1,0:T(8,128)(2,1)S(1)}, u32[]{:S(2)}, u32[]{:S(2)}) collective-permute-start(bf16[896,256]{1,0:T(8,128)(2,1)S(1)} %get-tuple-element.49), channel_id=1, source_target_pairs={{30,0},{0,2},{2,4},{4,6},{6,8},{8,10},{10,12},{12,14},{14,16},{16,... | collective-permute-start | bytes 1376264 | tf_op jit(solution)/shard_map/ppermute | solution.py:184
  236.7 7.6 %collective-permute-start.22 = (bf16[72,256]{1,0:T(8,128)(2,1)S(1)}, bf16[72,256]{1,0:T(8,128)(2,1)S(1)}, u32[]{:S(2)}, u32[]{:S(2)}) collective-permute-start(bf16[72,256]{1,0:T(8,128)(2,1)S(1)} %add_convert_fusion.16), channel_id=1, source_target_pairs={{0,16},{2,18},{4,20},{6,22},{8,24},{10,26},{12,28},{14,30},{16,0},... | collective-permute-start | bytes 110600 | tf_op jit(solution)/shard_map/ppermute | solution.py:189
  244.3 8.4 %collective-permute-start.23 = (bf16[144,256]{1,0:T(8,128)(2,1)S(1)}, bf16[144,256]{1,0:T(8,128)(2,1)S(1)}, u32[]{:S(2)}, u32[]{:S(2)}) collective-permute-start(bf16[144,256]{1,0:T(8,128)(2,1)S(1)} %maximum_select_fusion.14), channel_id=1, source_target_pairs={{0,8},{2,10},{4,12},{6,14},{8,0},{10,2},{12,4},{14,6},{16,24},{18,... | collective-permute-start | bytes 221192 | tf_op jit(solution)/shard_map/ppermute | solution.py:189
  258.9 8.3 %collective-permute-start.25 = (bf16[576,256]{1,0:T(8,128)(2,1)S(1)}, bf16[576,256]{1,0:T(8,128)(2,1)S(1)}, u32[]{:S(2)}, u32[]{:S(2)}) collective-permute-start(bf16[576,256]{1,0:T(8,128)(2,1)S(1)} %maximum_select_fusion.6), channel_id=1, source_target_pairs={{0,4},{2,6},{4,0},{6,2},{8,12},{10,14},{12,8},{14,10},{16,20},{18,... | collective-permute-start | bytes 884744 | tf_op jit(solution)/shard_map/ppermute | solution.py:189
  (43 other events, 479.6 us)
Sparse Core Ops, SparseCore 0:
  36.4 10.8 all-gather.1

commit v3 on v0

v3 whole, which is shorter than its diff:
```python
import math

import jax
import jax.numpy as jnp
from jax import lax
from jax.experimental import pallas as pl
from jax.experimental.pallas import tpu as pltpu
from jax.sharding import PartitionSpec as P

HD = 128
K = 16
SPAN = 896
ROWS = 128
WORD = 64
HUGE = -1e30
MIB = 1024 * 1024
FRONT_MIB = 20
ATTEND_MIB = 24
MLP_MIB = 24
BRANCH_MIB = 20
BACK_MIB = 28
GRADS_MIB = 24
epsilon = 1e-05
bf16 = jnp.bfloat16
f32 = jnp.float32


def dot(left, right, left_dim, right_dim):
    return lax.dot_general(
        left,
        right,
        (((left_dim,), (right_dim,)), ((), ())),
        preferred_element_type=f32,
    )


def two_blocks(first, second):
    zero = jnp.zeros_like(first)
    return jnp.concatenate(
        [jnp.concatenate([first, zero], 1), jnp.concatenate([zero, second], 1)], 0
    )


def ordered(head, mine, theirs):
    return jnp.where(
        head == 0,
        jnp.concatenate([mine, theirs], axis=1),
        jnp.concatenate([theirs, mine], axis=1),
    )


def parted(head, block):
    half = block.shape[1] // 2
    low, high = block[:, :half], block[:, half:]
    return jnp.where(head == 0, low, high), jnp.where(head == 0, high, low)


def onehot_t(ids, levels):
    spots = lax.broadcasted_iota(jnp.int32, (levels, ids.shape[1]), 0)
    return jnp.where(spots == ids, 1.0, 0.0).astype(bf16)


def level_values(ids, table):
    chosen = onehot_t(ids, table.shape[0])
    first = table.astype(bf16)
    rest = table - first.astype(f32)
    second = rest.astype(bf16)
    third = (rest - second.astype(f32)).astype(bf16)
    return dot(
        jnp.concatenate([chosen] * 3, axis=0),
        jnp.concatenate([first, second, third], axis=0),
        0,
        0,
    )


def norm_rows(values):
    centred = values - jnp.mean(values, axis=1, keepdims=True)
    inverse = lax.rsqrt(jnp.mean(centred * centred, axis=1, keepdims=True) + epsilon)
    return centred * inverse, inverse


def cost(microseconds):
    return pl.CostEstimate(
        flops=int(microseconds * 5e8), bytes_accessed=int(microseconds * 2.5e6), transcendentals=0
    )


def call(kernel, name, microseconds, mebibytes, operands, out_shape, scratch=()):
    spaces = [
        pltpu.SMEM if operand.shape == (1,) else pltpu.VMEM for operand in operands
    ]
    return pl.pallas_call(
        kernel,
        in_specs=[pl.BlockSpec(memory_space=space) for space in spaces],
        out_shape=[jax.ShapeDtypeStruct(shape, kind) for shape, kind in out_shape],
        scratch_shapes=list(scratch),
        compiler_params=pltpu.CompilerParams(vmem_limit_bytes=mebibytes * MIB),
        cost_estimate=cost(microseconds),
        name=name,
    )(*operands)


def front_kernel(
    head_ref, ids_ref, mine_ref, theirs_ref, table_ref, key_ref, value_ref, *refs
):
    width = 2 * mine_ref.shape[1]
    more = len(refs) > 4
    normed_ref, unit_ref, k_ref, vt_ref = refs[-4:] if not more else refs[1:5]
    values = ordered(head_ref[0], mine_ref[...], theirs_ref[...]).astype(f32)
    unit, _ = norm_rows(values)
    level = level_values(
        ids_ref[...], jnp.concatenate([table_ref[0], table_ref[1]], axis=1)
    )
    normed = (unit * (1.0 + level[:, :width]) + level[:, width:]).astype(bf16)
    normed_ref[...] = normed
    unit_ref[...] = unit.astype(bf16)
    k_ref[...] = dot(normed, key_ref[...], 1, 0).astype(bf16)
    vt_ref[...] = dot(value_ref[...], normed, 0, 1).astype(bf16)
    if more:
        query_ref, (q_ref, kt_ref, v_ref) = refs[0], refs[5:]
        q_ref[...] = dot(normed, query_ref[...], 1, 0).astype(bf16)
        kt_ref[...] = dot(key_ref[...], normed, 0, 1).astype(bf16)
        v_ref[...] = dot(normed, value_ref[...], 1, 0).astype(bf16)


def front(head, ids, mine, theirs, table, w_key, w_value, *w_query):
    rows = mine.shape[0]
    width = 2 * mine.shape[1]
    wide = 2 * HD
    down, along = ((rows, wide), bf16), ((wide, rows), bf16)
    shapes = [((rows, width), bf16)] * 2 + [down, along]
    if w_query:
        shapes += [down, along, down]
    operands = (head, ids, mine, theirs, table, w_key, w_value, *w_query)
    return call(front_kernel, "front", 3, FRONT_MIB, operands, shapes)


def forward_kernel(
    nbr_ref, k0, k1, k2, vt0, vt1, vt2, q_ref, out_ref,
    e_ref, mixed_ref, inv_ref, part_ref, k_all, vt_all, s_new, s_old, top_old,
):
    blocks, window, _ = e_ref.shape
    rows = k0.shape[0]
    scale = math.log2(math.e) / math.sqrt(HD)
    for i, (k, vt) in enumerate(((k0, vt0), (k1, vt1), (k2, vt2))):
        k_all[i * rows : (i + 1) * rows, :] = k[...]
        vt_all[:, i * rows : (i + 1) * rows] = vt[...]
    s_old[...] = jnp.zeros_like(s_old)
    top_old[...] = jnp.zeros_like(top_old)

    def work(step, carry):
        old_block = jnp.maximum(step - 1, 0)
        start = pl.multiple_of(jnp.minimum(step, blocks - 1) * ROWS, ROWS)
        old_start = pl.multiple_of(old_block * ROWS, ROWS)
        place = nbr_ref[:, pl.ds(start, ROWS)] - start
        bit = jnp.left_shift(1, jnp.right_shift(place, 6))
        low = jnp.bitwise_and(place, WORD - 1)
        lane_low = lax.broadcasted_iota(jnp.int32, (WORD, ROWS), 0)
        words = jnp.zeros((WORD, ROWS), jnp.int32)
        for j in range(K):
            words = words | jnp.where(lane_low == low[j : j + 1, :], bit[j : j + 1, :], 0)
        queries = q_ref[pl.ds(start, ROWS), :]
        both = two_blocks(queries[:, :HD], queries[:, HD:])
        scores = dot(k_all[pl.ds(start, window), :], both, 1, 1)
        old = top_old[:1, :]
        top = None
        total = jnp.zeros((WORD, 2 * ROWS), f32)
        weights = []
        for t in range(window // WORD):
            there = slice(t * WORD, (t + 1) * WORD)
            keep = (words & (1 << t)) != 0
            part = scores[there, :]
            part = jnp.concatenate(
                [jnp.where(keep, part[:, :ROWS], HUGE), jnp.where(keep, part[:, ROWS:], HUGE)], 1
            )
            top = part if top is None else jnp.maximum(top, part)
            s_new[there, :] = part
            weight = jnp.exp2(s_old[there, :] * scale - old)
            total = total + weight
            weights.append(weight.astype(bf16))
        inverse = 1.0 / jnp.sum(total, axis=0, keepdims=True)
        weights = jnp.concatenate(weights, 0)
        e_ref[old_block] = weights
        there = pl.ds(old_start, ROWS)
        inv_ref[0:1, there] = inverse[:, :ROWS]
        inv_ref[1:2, there] = inverse[:, ROWS:]
        mixed = dot(vt_all[:, pl.ds(old_start, window)], weights, 1, 0) * inverse
        mixed = jnp.concatenate([mixed[:HD, :ROWS], mixed[HD:, ROWS:]], axis=0)
        mixed_ref[:, there] = mixed.astype(bf16)
        part_ref[there, :] = dot(mixed.T.astype(bf16), out_ref[...], 1, 0).astype(bf16)
        s_old[...] = s_new[...]
        top_old[...] = jnp.broadcast_to(jnp.max(top, axis=0, keepdims=True) * scale, top_old.shape)
        return carry

    lax.fori_loop(0, blocks + 1, work, 0)


def attend(places, keys, values_t, queries, w_out):
    rows = queries.shape[0]
    wide = 2 * HD
    blocks = rows // ROWS
    window = ROWS + 2 * SPAN
    shapes = [
        ((blocks, window, wide), bf16),
        ((wide, rows), bf16),
        ((8, rows), f32),
        ((rows, w_out.shape[1]), bf16),
    ]
    scratch = [
        pltpu.VMEM((3 * rows, wide), bf16),
        pltpu.VMEM((wide, 3 * rows), bf16),
        pltpu.VMEM((window, wide), f32),
        pltpu.VMEM((window, wide), f32),
        pltpu.VMEM((8, wide), f32),
    ]
    operands = (places, *keys, *values_t, queries, w_out)
    return call(forward_kernel, "attend_forward", 10, ATTEND_MIB, operands, shapes, scratch)


def mlp_kernel(
    head_ref, ids_ref, xm_ref, xt_ref, part_ref, other_ref, grad_ref, table_ref, up_ref, down_ref,
    middle_ref, two_ref, theirs_ref, out_ref, normed_ref, act_ref, pre_ref,
):
    head = head_ref[0]
    width = 2 * xm_ref.shape[1]
    values = ordered(head, xm_ref[...], xt_ref[...]).astype(f32)
    middle = values + (part_ref[...].astype(f32) + other_ref[...].astype(f32))
    middle_ref[...] = middle
    unit, _ = norm_rows(middle)
    level = level_values(
        ids_ref[...], jnp.concatenate([table_ref[2], table_ref[3]], axis=1)
    )
    normed = (unit * (1.0 + level[:, :width]) + level[:, width:]).astype(bf16)
    normed_ref[...] = normed
    pre = dot(normed, up_ref[...], 1, 0)
    sigma = jax.nn.sigmoid(pre)
    act = (pre * sigma).astype(bf16)
    act_ref[...] = act
    grad = grad_ref[...].astype(f32)
    grad = (grad * sigma * (1.0 + pre * (1.0 - sigma))).astype(bf16)
    pre_ref[...] = grad
    two_ref[...] = dot(grad, up_ref[...], 1, 1).astype(bf16)
    mine, theirs = parted(head, dot(act, down_ref[...], 1, 0))
    theirs_ref[...] = theirs.astype(bf16)
    out_ref[...] = parted(head, middle)[0] + mine


def mlp(head, ids, x_mine, x_theirs, part, other, grad_act, table, w_up, w_down):
    rows, half = x_mine.shape
    hidden = w_up.shape[1]
    shapes = [
        (2 * half, f32), (2 * half, bf16), (half, bf16), (half, f32),
        (2 * half, bf16), (hidden, bf16), (hidden, bf16),
    ]
    shapes = [((rows, wide), kind) for wide, kind in shapes]
    operands = (head, ids, x_mine, x_theirs, part, other, grad_act, table, w_up, w_down)
    return call(mlp_kernel, "mlp", 5, MLP_MIB, operands, shapes)


def branch_kernel(
    head_ref, ids_ref, middle_ref, cm_ref, ct_ref, two_ref, other_ref, mixed_ref, inv_ref, table_ref, out_ref,
    mid_ref, gout_ref, tab_ref, grad_ref, cross_ref,
):
    head = head_ref[0]
    ids = ids_ref[...]
    unit, inverse = norm_rows(middle_ref[...])
    gain = 1.0 + level_values(ids, table_ref[2])
    grad_two = two_ref[...].astype(f32) + other_ref[...].astype(f32)
    gained = grad_two * gain
    cot = ordered(head, cm_ref[...], ct_ref[...]).astype(f32)
    grad_mid = cot + inverse * (
        gained
        - jnp.mean(gained, axis=1, keepdims=True)
        - unit * jnp.mean(gained * unit, axis=1, keepdims=True)
    )
    mid_ref[...] = parted(head, grad_mid)[0]
    branch = grad_mid.astype(bf16)
    grad = dot(out_ref[...], branch, 1, 1)
    cross = grad * mixed_ref[...].astype(f32)
    for h in range(grad.shape[0] // HD):
        there = slice(h * HD, (h + 1) * HD)
        total = inv_ref[h : h + 1, :]
        grad_ref[there, :] = (grad[there, :] * total).astype(bf16)
        cross_ref[h : h + 1, :] = jnp.sum(cross[there, :], axis=0, keepdims=True) * total
    gout_ref[...] = dot(mixed_ref[...], branch, 1, 0).astype(bf16)
    tab_ref[...] = dot(
        onehot_t(ids, table_ref.shape[1]),
        jnp.concatenate(
            [parted(head, grad_two * unit)[0], parted(head, grad_two)[0]], 1
        ).astype(bf16),
        1,
        0,
    )


def branch(
    head, ids, middle, cot_mine, cot_theirs, two_part, two_other, mixed_t, inverse,
    table, w_out,
):
    rows, half = cot_mine.shape
    width = 2 * half
    shapes = [
        ((rows, half), f32),
        ((w_out.shape[0], width), bf16),
        ((table.shape[1], width), f32),
        ((2 * HD, rows), bf16),
        ((8, rows), f32),
    ]
    operands = (
        head, ids, middle, cot_mine, cot_theirs, two_part, two_other, mixed_t, inverse,
        table, w_out,
    )
    return call(branch_kernel, "branch", 3, BRANCH_MIB, operands, shapes)


def backward_kernel(
    e_ref, grad_ref, cross_ref, q_ref, v0, v1, v2, kt0, kt1, kt2,
    dkv_ref, dq_ref, dkv_sum, kt_all, v_all, ds_slots,
):
    blocks, window, wide = e_ref.shape
    rows = v0.shape[0]
    factor = 1.0 / math.sqrt(HD)
    dkv_sum[...] = jnp.zeros_like(dkv_sum)
    for i, (v, kt) in enumerate(((v0, kt0), (v1, kt1), (v2, kt2))):
        v_all[i * rows : (i + 1) * rows, :] = v[...]
        kt_all[:, i * rows : (i + 1) * rows] = kt[...]

    def scores_and_values(block):
        start = pl.multiple_of(block * ROWS, ROWS)
        grad = grad_ref[:, pl.ds(start, ROWS)]
        grad_both = two_blocks(grad[:HD, :], grad[HD:, :])
        cross = jnp.concatenate(
            [cross_ref[0:1, pl.ds(start, ROWS)], cross_ref[1:2, pl.ds(start, ROWS)]], axis=1
        )
        weights = e_ref[block]
        spots = pl.ds(start, window)
        grad_probs = dot(v_all[spots, :], grad_both, 1, 0)
        ds_slots[block % 2] = (weights.astype(f32) * (grad_probs - cross)).astype(bf16)
        dkv_sum[spots, wide:] += dot(weights, grad_both, 1, 1)

    def keys_and_queries(block):
        start = pl.multiple_of(block * ROWS, ROWS)
        spots = pl.ds(start, window)
        queries = q_ref[pl.ds(start, ROWS), :]
        both = two_blocks(queries[:, :HD], queries[:, HD:])
        grad_scores = ds_slots[block % 2]
        dkv_sum[spots, :wide] += dot(grad_scores, both, 1, 0)
        grad_query = dot(kt_all[:, spots], grad_scores, 1, 0) * factor
        dq_ref[pl.ds(start, ROWS), :HD] = grad_query[:HD, :ROWS].T.astype(bf16)
        dq_ref[pl.ds(start, ROWS), HD:] = grad_query[HD:, ROWS:].T.astype(bf16)

    def work(block, carry):
        scores_and_values(block)
        keys_and_queries(block - 1)
        return carry

    scores_and_values(0)
    lax.fori_loop(1, blocks, work, 0)
    keys_and_queries(blocks - 1)
    for i in range(3):
        there = slice(i * rows, (i + 1) * rows)
        dkv_ref[there, :wide] = (dkv_sum[there, :wide] * factor).astype(bf16)
        dkv_ref[there, wide:] = dkv_sum[there, wide:].astype(bf16)


def backward(weights, grad_t, cross, queries, values, keys_t):
    rows = queries.shape[0]
    wide = 2 * HD
    window = weights.shape[1]
    shapes = [((3 * rows, 2 * wide), bf16), ((rows, wide), bf16)]
    scratch = [
        pltpu.VMEM((3 * rows, 2 * wide), f32),
        pltpu.VMEM((wide, 3 * rows), bf16),
        pltpu.VMEM((3 * rows, wide), bf16),
        pltpu.VMEM((2, window, wide), bf16),
    ]
    operands = (weights, grad_t, cross, queries, *values, *keys_t)
    return call(backward_kernel, "attend_backward", 12, BACK_MIB, operands, shapes, scratch)


def grads_kernel(
    head_ref, dkv_ref, dq_ref, id0, id1, id2, n0, n1, n2, u0, u1, u2, key_ref, value_ref, query_ref,
    gq_ref, gkv_ref, mine_ref, theirs_ref, tab_mine, tab_theirs,
):
    head = head_ref[0]
    rows, width = n0.shape
    wide = dq_ref.shape[1]
    levels = tab_mine.shape[0]
    w_kv = jnp.concatenate([key_ref[...], value_ref[...]], axis=1)
    grad_kv = jnp.zeros((width, 2 * wide), f32)
    table_sum = jnp.zeros((levels, 2 * width), f32)
    for i, (ids, normed, units) in enumerate(((id0, n0, u0), (id1, n1, u1), (id2, n2, u2))):
        there = slice(i * rows, (i + 1) * rows)
        dkv = dkv_ref[there, :]
        grad_kv = grad_kv + dot(normed[...], dkv, 0, 0)
        part = dot(dkv, w_kv, 1, 1)
        if i == 1:
            part = part + dot(dq_ref[...], query_ref[...], 1, 1)
        mine, theirs = parted(head, part)
        mine_ref[there, :] = mine.astype(bf16)
        theirs_ref[there, :] = theirs.astype(bf16)
        table_sum = table_sum + dot(
            onehot_t(ids[...], levels),
            jnp.concatenate([part * units[...].astype(f32), part], 1).astype(bf16),
            1,
            0,
        )
    gkv_ref[...] = grad_kv.astype(bf16)
    gq_ref[...] = dot(n1[...], dq_ref[...], 0, 0).astype(bf16)
    scale_mine, scale_theirs = parted(head, table_sum[:, :width])
    shift_mine, shift_theirs = parted(head, table_sum[:, width:])
    tab_mine[...] = jnp.concatenate([scale_mine, shift_mine], axis=1)
    tab_theirs[...] = jnp.concatenate([scale_theirs, shift_theirs], axis=1)


def grads(head, dkv, dq, ids, normed, units, w_key, w_value, w_query, levels):
    rows, width = normed[0].shape
    half = width // 2
    wide = dq.shape[1]
    shapes = [
        ((width, wide), bf16),
        ((width, 2 * wide), bf16),
        ((3 * rows, half), bf16),
        ((3 * rows, half), bf16),
        ((levels, width), f32),
        ((levels, width), f32),
    ]
    operands = (head, dkv, dq, *ids, *normed, *units, w_key, w_value, w_query)
    return call(grads_kernel, "grads", 5, GRADS_MIB, operands, shapes)


def passed_along(block, axis, distance):
    devices = range(lax.axis_size(axis))
    route = [((i - distance) % len(devices), i) for i in devices]
    return lax.ppermute(block, axis, route)


def swapped(block, axis, bit):
    devices = range(lax.axis_size(axis))
    return lax.ppermute(block, axis, [(i, i ^ bit) for i in devices])


def held_until(block, *others):
    return lax.optimization_barrier((block, *others))[0]


def two_parts(block, axis, bit):
    half = block.shape[0] // 2
    upper = (lax.axis_index(axis) & bit) != 0
    send = jnp.where(upper, block[:half], block[half:])
    keep = jnp.where(upper, block[half:], block[:half])
    return send, keep


def added(keep, got):
    return (keep.astype(f32) + got.astype(f32)).astype(bf16)


def doubled(block, axis, bit):
    upper = (lax.axis_index(axis) & bit) != 0
    got = swapped(block, axis, bit)
    return jnp.where(upper, jnp.concatenate([got, block]), jnp.concatenate([block, got]))


def far_bits(axis):
    return [1 << k for k in range(2, lax.axis_size(axis).bit_length() - 1)]


def halved(block, axis, bit, *others):
    send, keep = two_parts(block, axis, bit)
    return added(keep, held_until(swapped(send, axis, bit), *others))


def scatter_far(block, axis, *others):
    for bit in far_bits(axis):
        block = halved(block, axis, bit, *others)
    return block


def gather_far(block, axis):
    for bit in reversed(far_bits(axis)):
        block = doubled(block, axis, bit)
    return block


def gather_near(first, second, axis):
    first, second = doubled(first, axis, 2), doubled(second, axis, 1)
    return doubled(first, axis, 1), doubled(second, axis, 2)


def body(
    inputs,
    w_query,
    w_key,
    w_value,
    w_out,
    w_up,
    w_down,
    mod_table,
    level_ids,
    neighbours,
    cotangent,
):
    rows, half = inputs.shape
    width = half * lax.axis_size("heads")
    levels = mod_table.shape[1]
    head = lax.axis_index("heads").astype(jnp.int32).reshape(1)
    first_head = lax.axis_index("heads") == 0
    ids_own = level_ids[None, :]

    before = passed_along(inputs, "nodes", 1)
    after = passed_along(inputs, "nodes", -1)
    in_other = swapped(inputs, "heads", 1)
    cot_other = swapped(cotangent, "heads", 1)
    own = front(head, ids_own, inputs, in_other, mod_table, w_key, w_value, w_query)
    queries, keys_t1, values1 = own[4:]
    ids_late = held_until(ids_own, own[0])
    ids_before = passed_along(ids_late, "nodes", 1)
    ids_after = passed_along(ids_late, "nodes", -1)
    node_count = rows * lax.axis_size("nodes")
    first_node = lax.axis_index("nodes") * rows
    places = jnp.mod(neighbours.T - first_node + SPAN, node_count)
    full_cot = jnp.where(
        first_head,
        jnp.concatenate([cotangent, cot_other], axis=1),
        jnp.concatenate([cot_other, cotangent], axis=1),
    )
    grad_act = dot(full_cot, w_down, 1, 1).astype(bf16)
    before_other = swapped(held_until(before, own[0], grad_act), "heads", 1)
    low = front(head, ids_before, before, before_other, mod_table, w_key, w_value)
    after_other = swapped(after, "heads", 1)
    high = front(head, ids_after, after, after_other, mod_table, w_key, w_value)
    normed, units, keys, values_t = zip(low, own[:4], high)
    weights, mixed_t, inverse, attn_part = attend(places, keys, values_t, queries, w_out)
    attn_other = swapped(attn_part, "heads", 1)
    middle, two_part, mlp_theirs, out_mine, normed_two, activated, grad_pre = mlp(
        head, ids_own, inputs, in_other, attn_part, attn_other, grad_act, mod_table, w_up, w_down
    )
    two_other = swapped(two_part, "heads", 1)
    grad_up = dot(normed_two, grad_pre, 0, 0).astype(bf16)
    grad_down = dot(activated, full_cot, 0, 0).astype(bf16)
    hidden = grad_up.shape[1] // 2
    grad_up = jnp.concatenate([grad_up[:, :hidden], grad_up[:, hidden:]])
    up_send, up_keep = two_parts(grad_up, "nodes", 1)
    down_send, down_keep = two_parts(grad_down, "nodes", 2)
    up_got = swapped(up_send, "nodes", 1)
    down_got = swapped(down_send, "nodes", 2)
    mlp_other = swapped(mlp_theirs, "heads", 1)
    output = (out_mine + mlp_other.astype(f32)).astype(bf16)

    keys_t = [
        dot(w_key, normed[0], 0, 1).astype(bf16),
        keys_t1,
        dot(w_key, normed[2], 0, 1).astype(bf16),
    ]
    values = [
        dot(normed[0], w_value, 1, 0).astype(bf16),
        values1,
        dot(normed[2], w_value, 1, 0).astype(bf16),
    ]
    mid_mine, grad_out, tab_two, grad_t, cross = branch(
        head, ids_own, middle, cotangent, cot_other, two_part, two_other, mixed_t, inverse,
        mod_table, w_out,
    )
    grad_t = held_until(grad_t, up_send, down_send)
    dkv, dq = backward(weights, grad_t, cross, queries, values, keys_t)
    up_send, up_keep = two_parts(added(up_keep, held_until(up_got, dq)), "nodes", 2)
    down_send, down_keep = two_parts(added(down_keep, held_until(down_got, dq)), "nodes", 1)
    up_got = swapped(up_send, "nodes", 2)
    down_got = swapped(down_send, "nodes", 1)
    dq = held_until(dq, up_send, down_send)
    grad_q, grad_kv, one_mine, one_theirs, tab_mine, tab_theirs = grads(
        head, dkv, dq, (ids_before, ids_own, ids_after), normed, units,
        w_key, w_value, w_query, levels,
    )
    tab_other = swapped(tab_theirs, "heads", 1)
    one_other = swapped(one_theirs, "heads", 1)
    one_all = one_mine.astype(f32) + one_other.astype(f32)
    to_before = passed_along(one_all[:rows].astype(bf16), "nodes", -1)
    to_after = passed_along(one_all[2 * rows :].astype(bf16), "nodes", 1)
    wide = grad_q.shape[1]
    out_rows = grad_out.shape[0]
    spare = -(width + 2 * levels) % max(64, lax.axis_size("nodes"))
    table = jnp.concatenate([tab_mine + tab_other, tab_two], axis=0).astype(bf16)
    q_and_k = jnp.concatenate([grad_q, grad_kv[:, :wide]], axis=1)
    v_and_more = jnp.concatenate(
        [
            jnp.concatenate(
                [
                    grad_kv[:, wide:],
                    jnp.concatenate([grad_out[:, :half], grad_out[:, half:]], axis=0),
                ],
                axis=1,
            ),
            table,
            jnp.zeros((spare, width), bf16),
        ],
        axis=0,
    )
    qk_send, qk_keep = two_parts(q_and_k, "nodes", 1)
    qk_got = swapped(qk_send, "nodes", 1)
    up_sum = added(up_keep, held_until(up_got, qk_send))
    down_sum = added(down_keep, held_until(down_got, qk_send))
    mlp_sum = jnp.concatenate([up_sum, down_sum])
    mlp_sum = halved(mlp_sum, "nodes", 4, one_all)
    more_sum = halved(v_and_more, "nodes", 2)
    qk_sum = added(qk_keep, held_until(qk_got, one_all))
    qk_sum, more_sum = halved(qk_sum, "nodes", 2), halved(more_sum, "nodes", 1)
    for bit in far_bits("nodes")[1:]:
        mlp_sum = halved(mlp_sum, "nodes", bit)
    attn_sum = scatter_far(jnp.concatenate([qk_sum, more_sum]), "nodes")
    mlp_sum = held_until(mlp_sum, to_before, to_after)
    mlp_sum = gather_far(mlp_sum, "nodes")
    up_total, down_total = gather_near(
        mlp_sum[: mlp_sum.shape[0] // 2], mlp_sum[mlp_sum.shape[0] // 2 :], "nodes"
    )
    attn_sum = gather_far(attn_sum, "nodes")
    count = qk_sum.shape[0]
    qk_total, more_total = gather_near(attn_sum[:count], attn_sum[count:], "nodes")

    grad_one = one_all[rows : 2 * rows] + to_before.astype(f32) + to_after.astype(f32)
    full_in = jnp.concatenate([inputs, in_other], axis=1).astype(f32)
    unit, inverse = norm_rows(full_in)
    unit = unit[:, :half]
    onehot = (level_ids[:, None] == jnp.arange(levels, dtype=jnp.int32)[None, :]).astype(f32)
    scale_mine = jnp.where(first_head, mod_table[0][:, :half], mod_table[0][:, half:])
    gain = 1.0 + jnp.dot(onehot, scale_mine, precision=lax.Precision.HIGHEST)
    gained = grad_one * gain
    sum_gain, sum_cross = lax.psum(
        (jnp.sum(gained, axis=1), jnp.sum(gained * unit, axis=1)), "heads"
    )
    grad_inputs = mid_mine + inverse * (
        gained - sum_gain[:, None] / width - unit * sum_cross[:, None] / width
    )
    depth = w_query.shape[0]
    table_total = more_total[depth : depth + 2 * levels].astype(f32)
    return (
        output,
        grad_inputs,
        qk_total[:, :wide].astype(f32),
        qk_total[:, wide:].astype(f32),
        more_total[:depth, :wide].astype(f32),
        jnp.concatenate(
            [more_total[:out_rows, wide:], more_total[out_rows:depth, wide:]], axis=1
        ).astype(f32),
        jnp.concatenate([up_total[: width], up_total[width:]], axis=1).astype(f32),
        down_total.astype(f32),
        jnp.stack(
            [
                table_total[:levels, :half],
                table_total[:levels, half:],
                table_total[levels:, :half],
                table_total[levels:, half:],
            ]
        ),
    )


def solution(mesh):
    return jax.shard_map(
        body,
        mesh=mesh,
        in_specs=(
            P("nodes", "heads"),
            P(None, "heads"),
            P(None, "heads"),
            P(None, "heads"),
            P("heads", None),
            P(None, "heads"),
            P("heads", None),
            P(),
            P("nodes"),
            P("nodes", None),
            P("nodes", "heads"),
        ),
        out_specs=(
            P("nodes", "heads"),
            P("nodes", "heads"),
            P(None, "heads"),
            P(None, "heads"),
            P(None, "heads"),
            P("heads", None),
            P(None, "heads"),
            P("heads", None),
            P(None, None, "heads"),
        ),
        check_vma=False,
    )
```

time: 928 us -> 171 us (0.18)
  matrix products: 286 us -> 6.33 us
  waiting for transfers between devices: 297 us -> 47.4 us
  local copies, waits for them, and re-layouts: 159 us -> 6.58 us
  other arithmetic: 105 us -> 15.7 us
  starting transfers between devices: 13 us -> 52.2 us
  Pallas kernels: 0 us -> 38.1 us
  loops' own time: 29.8 us -> 0 us
  between operations: 14.8 us -> 1.28 us
  blocking collectives: 15.9 us -> 2.5 us
    dot_general x82 -> x8, matrix products: 286 us -> 6.33 us  [the longest x7 5.5 us: dot(): lax.dot_general(left, right, (((left_dim,), (right_dim,)), ((), ())), pre...]
    psum x1 -> x0, waiting for transfers between devices: 214 us -> none  [body(): lax.psum((grad_up, grad_down, grad_query, grad_key, grad_value, grad_out,...]
    dynamic_update_slice x21 -> x0, local copies, waits for them, and re-layouts: 83.7 us -> none  [the longest x7 79.2 us: attend_back(): carry = lax.dynamic_update_slice_in_dim(carry, current + spread, start, 0)]
    pallas_call x0 -> x8, Pallas kernels: none -> 38.1 us  [call(): pl.pallas_call(kernel, in_specs=[pl.BlockSpec(memory_space=space) for spa...]
    ppermute x2 -> x6, waiting for transfers between devices: 37.8 us -> 1.54 us  [passed_along(): return lax.ppermute(block, axis, route)]
    ppermute x2 -> x33, starting transfers between devices: 7.05 us -> 37.1 us  [swapped(): return lax.ppermute(block, axis, [(i, i ^ bit) for i in devices])]
    another operation x2 -> x0, loops' own time: 29.8 us -> none  [the longest x1 15.5 us: body(): lax.scan(attend_back, start_pad, (query_blocks, index_blocks, grad_mixed....]
    sub x21 -> x0, other arithmetic: 28.4 us -> none  [the longest x7 19.2 us: attend_back(): grad_probs - jnp.sum(probs * grad_probs, axis=1, keepdims=True)]
  transfers between devices with their start and end apart: 9 -> 39, of which waited for: 7 -> 18; matrix products, arithmetic and copies ran while one was open for 4% -> 13% of each run, Pallas kernels for 0% -> 13%
where the time goes in v3:
time: 171 us; the launch traced here: 170 us
  starting transfers between devices  52.2 us (31%)
  waiting for transfers between devices  47.4 us (28%)
  Pallas kernels  38.1 us (22%)
  other arithmetic  15.7 us (9%)
  local copies, waits for them, and re-layouts  6.58 us (4%)
  matrix products  6.33 us (4%)
  blocking collectives  2.5 us (1%)
    ppermute x33, waiting for transfers between devices, swapped(): return lax.ppermute(block, axis, [(i, i ^ bit) for i in devices])  45.9 us
    pallas_call x8, Pallas kernels, call(): pl.pallas_call(kernel, in_specs=[pl.BlockSpec(memory_space=space) for spa...  38.1 us
    ppermute x33, starting transfers between devices, swapped(): return lax.ppermute(block, axis, [(i, i ^ bit) for i in devices])  37.1 us
    ppermute x6, starting transfers between devices, passed_along(): return lax.ppermute(block, axis, route)  15.1 us
    dot_general x7, matrix products, dot(): lax.dot_general(left, right, (((left_dim,), (right_dim,)), ((), ())), pre...  5.5 us
    unnamed x32, local copies, waits for them, and re-layouts  4.85 us
  transfers between devices with their start and end apart: 39, of which 18 were waited for; matrix products, arithmetic and copies ran while one was open for 13% of the time, Pallas kernels for 13%

profile of v3, /device:TPU:0, one launch (start us, length us, event | category | flops | bytes accessed | tf_op | source)
XLA Modules:
  0.0 170.1 jit_solution(5598128565031727226)
XLA Ops:
  1.2 2.6 %collective-permute-start.2 = (bf16[896,256]{1,0:T(8,128)(2,1)}, bf16[896,256]{1,0:T(8,128)(2,1)S(1)}, u32[]{:S(2)}, u32[]{:S(2)}) collective-permute-start(bf16[896,256]{1,0:T(8,128)(2,1)} %xm_ref.1), channel_id=1, source_target_pairs={{30,0},{0,2},{2,4},{4,6},{6,8},{8,10},{10,12},{12,14},{14,16},{16,... | collective-permute-start | bytes 1376264 | tf_op jit(solution)/shard_map/ppermute | solution.py:436
  3.7 4.1 %collective-permute-start.6 = (bf16[896,256]{1,0:T(8,128)(2,1)}, bf16[896,256]{1,0:T(8,128)(2,1)S(1)}, u32[]{:S(2)}, u32[]{:S(2)}) collective-permute-start(bf16[896,256]{1,0:T(8,128)(2,1)} %xm_ref.1), channel_id=1, source_target_pairs={{2,0},{4,2},{6,4},{8,6},{10,8},{12,10},{14,12},{16,14},{18,16},{20... | collective-permute-start | bytes 1376264 | tf_op jit(solution)/shard_map/ppermute | solution.py:436
  15.0 2.4 %front.3 = (bf16[896,512]{1,0:T(8,128)(2,1)S(1)}, bf16[896,512]{1,0:T(8,128)(2,1)S(1)}, bf16[896,256]{1,0:T(8,128)(2,1)S(1)}, bf16[256,896]{1,0:T(8,128)(2,1)S(1...) custom-call(s32[1]{0:T(128)} %bitcast.head_ref, ...), custom_call_target="tpu_custom_call" | custom-call | flops 1500000000 | bytes 7500000 | tf_op jit(solution)/shard_map/front/pallas_call | solution.py:93
  17.5 5.6 %collective-permute-start.5 = (s32[1,896]{1,0:T(1,128)S(1)}, s32[1,896]{1,0:T(1,128)S(1)}, u32[]{:S(2)}, u32[]{:S(2)}) collective-permute-start(s32[1,896]{1,0:T(1,128)S(1)} %broadcast_in_dim.4.ids_ref.id1), channel_id=1, source_target_pairs={{2,0},{4,2},{6,4},{8,6},{10,8},{12,10},{14,12},{16,14},{18,16},{20... | collective-permute-start | bytes 10760 | tf_op jit(solution)/shard_map/ppermute | solution.py:436
  29.8 10.3 %attend_forward.1 = (bf16[7,1920,256]{2,1,0:T(8,128)(2,1)S(1)}, bf16[256,896]{1,0:T(8,128)(2,1)S(1)}, f32[8,896]{1,0:T(8,128)S(1)}, bf16[896,512]{1,0:T(8,128)(2,1)S(1)}) custom-call(s32[16,896]{1,0:T(8,128)S(1)} %add_select_fusion.nbr_ref, bf16[896,256]{1,0:T(8,128)(2,1)S(1)} %get-tuple-element.62.k0, bf16[896,256]{1,0:T(8,128)(2,1)S(1)} %get-tuple-element.63.k1, ...), custom_call_target="tpu_custom_call" | custom-call | flops 5000000000 | bytes 25000000 | tf_op jit(solution)/shard_map/attend_forward/pallas_call | solution.py:93
  42.7 4.3 %mlp.1 = (f32[896,512]{1,0:T(8,128)S(1)}, bf16[896,512]{1,0:T(8,128)(2,1)S(1)}, bf16[896,256]{1,0:T(8,128)(2,1)S(1)}, f32[896,256]{1,0:T(8,128)S(1)}, bf16[896,5...) custom-call(s32[1]{0:T(128)} %bitcast.head_ref, ...), custom_call_target="tpu_custom_call" | custom-call | flops 2500000000 | bytes 12500000 | tf_op jit(solution)/shard_map/mlp/pallas_call | solution.py:93
  48.9 1.9 %collective-permute-start.12 = (bf16[512,512]{1,0:T(8,128)(2,1)S(1)}, bf16[512,512]{1,0:T(8,128)(2,1)S(1)}, u32[]{:S(2)}, u32[]{:S(2)}) collective-permute-start(bf16[512,512]{1,0:T(8,128)(2,1)S(1)} %broadcast_select_fusion), channel_id=1, source_target_pairs={{0,4},{2,6},{4,0},{6,2},{8,12},{10,14},{12,8},{14,10},{16,20},{18,... | collective-permute-start | bytes 1572872 | tf_op jit(solution)/shard_map/ppermute | solution.py:441
  52.3 2.4 %branch.1 = (f32[896,256]{1,0:T(8,128)S(1)}, bf16[256,512]{1,0:T(8,128)(2,1)S(1)}, f32[16,512]{1,0:T(8,128)S(1)}, bf16[256,896]{1,0:T(8,128)(2,1)S(1)}, f32[8,896]{1,0:T(8,128)S(1)}) custom-call(s32[1]{0:T(128)} %bitcast.head_ref, s32[1,896]{1,0:T(1,128)S(1)} %broadcast_in_dim.4.ids_ref.id1, f32[896,512]{1,0:T(8,128)S(1)} %get-tuple-element.72.middle_ref, ...), custom_call_target="tpu_custom_call" | custom-call | flops 1500000000 | bytes 7500000 | tf_op jit(solution)/shard_map/branch/pallas_call | solution.py:93
  54.7 10.9 %attend_backward.1 = (bf16[2688,512]{1,0:T(8,128)(2,1)S(1)}, bf16[896,256]{1,0:T(8,128)(2,1)S(1)}) custom-call(bf16[7,1920,256]{2,1,0:T(8,128)(2,1)S(1)} %get-tuple-element.77.e_ref, bf16[256,896]{1,0:T(8,128)(2,1)S(1)} %get-tuple-element.82.grad_ref, f32[8,896]{1,0:T(8,128)S(1)} %get-tuple-element.83.cross_ref, ...), custom_call_target="tpu_custom_call" | custom-call | flops 6000000000 | bytes 30000000 | tf_op jit(solution)/shard_map/attend_backward/pallas_call | solution.py:93
  68.3 4.7 %grads.1 = (bf16[512,256]{1,0:T(8,128)(2,1)S(1)}, bf16[512,512]{1,0:T(8,128)(2,1)S(1)}, bf16[2688,256]{1,0:T(8,128)(2,1)S(1)}, bf16[2688,256]{1,0:T(8,128)(2,1)S...) custom-call(s32[1]{0:T(128)} %bitcast.head_ref, bf16[2688,512]{1,0:T(8,128)(2,1)S(1)} %get-tuple-element.88.dkv_ref, ...), custom_call_target="tpu_custom_call" | custom-call | flops 2500000000 | bytes 12500000 | tf_op jit(solution)/shard_map/grads/pallas_call | solution.py:93
  73.7 2.6 %collective-permute-done.16 = f32[16,512]{1,0:T(8,128)S(1)} collective-permute-done((f32[16,512]{1,0:T(8,128)S(1)}, f32[16,512]{1,0:T(8,128)S(1)}, u32[]{:S(2)}, u32[]{:S(2)}) %collective-permute-start.16) | collective-permute-done | bytes 32800 | tf_op jit(solution)/shard_map/ppermute | solution.py:441
  76.5 1.9 %collective-permute-start.17 = (bf16[288,512]{1,0:T(8,128)(2,1)S(1)}, bf16[288,512]{1,0:T(8,128)(2,1)S(1)}, u32[]{:S(2)}, u32[]{:S(2)}) collective-permute-start(bf16[288,512]{1,0:T(8,128)(2,1)S(1)} %broadcast_select_fusion.2), channel_id=1, source_target_pairs={{0,4},{2,6},{4,0},{6,2},{8,12},{10,14},{12,8},{14,10},{16,20},{18,... | collective-permute-start | bytes 884744 | tf_op jit(solution)/shard_map/ppermute | solution.py:441
  79.5 6.1 %collective-permute-done.17 = bf16[288,512]{1,0:T(8,128)(2,1)S(1)} collective-permute-done((bf16[288,512]{1,0:T(8,128)(2,1)S(1)}, bf16[288,512]{1,0:T(8,128)(2,1)S(1)}, u32[]{:S(2)}, u32[]{:S(2)}) %collective-permute-start.17) | collective-permute-done | bytes 294944 | tf_op jit(solution)/shard_map/ppermute | solution.py:441
  89.3 1.8 %collective-permute-done.18 = bf16[144,512]{1,0:T(8,128)(2,1)S(1)} collective-permute-done((bf16[144,512]{1,0:T(8,128)(2,1)S(1)}, bf16[144,512]{1,0:T(8,128)(2,1)S(1)}, u32[]{:S(2)}, u32[]{:S(2)}) %collective-permute-start.18) | collective-permute-done | bytes 147488 | tf_op jit(solution)/shard_map/ppermute | solution.py:441
  91.7 1.8 %collective-permute-start.20 = (bf16[128,512]{1,0:T(8,128)(2,1)S(1)}, bf16[128,512]{1,0:T(8,128)(2,1)S(1)}, u32[]{:S(2)}, u32[]{:S(2)}) collective-permute-start(bf16[128,512]{1,0:T(8,128)(2,1)S(1)} %broadcast_select_fusion.10), channel_id=1, source_target_pairs={{0,4},{2,6},{4,0},{6,2},{8,12},{10,14},{12,8},{14,10},{16,20},{18,... | collective-permute-start | bytes 393224 | tf_op jit(solution)/shard_map/ppermute | solution.py:441
  95.0 1.7 %collective-permute-done.20 = bf16[128,512]{1,0:T(8,128)(2,1)S(1)} collective-permute-done((bf16[128,512]{1,0:T(8,128)(2,1)S(1)}, bf16[128,512]{1,0:T(8,128)(2,1)S(1)}, u32[]{:S(2)}, u32[]{:S(2)}) %collective-permute-start.20) | collective-permute-done | bytes 131104 | tf_op jit(solution)/shard_map/ppermute | solution.py:441
  98.5 2.6 %collective-permute-start.32 = (bf16[128,512]{1,0:T(8,128)(2,1)S(1)}, bf16[128,512]{1,0:T(8,128)(2,1)S(1)}, u32[]{:S(2)}, u32[]{:S(2)}) collective-permute-start(bf16[128,512]{1,0:T(8,128)(2,1)S(1)} %broadcast_select_fusion.9), channel_id=1, source_target_pairs={{0,16},{2,18},{4,20},{6,22},{8,24},{10,26},{12,28},{14,30},{16,0},... | collective-permute-start | bytes 393224 | tf_op jit(solution)/shard_map/ppermute | solution.py:441
  101.1 1.7 %collective-permute-done.21 = bf16[136,512]{1,0:T(8,128)(2,1)S(1)} collective-permute-done((bf16[136,512]{1,0:T(8,128)(2,1)S(1)}, bf16[136,512]{1,0:T(8,128)(2,1)S(1)}, u32[]{:S(2)}, u32[]{:S(2)}) %collective-permute-start.21) | collective-permute-done | bytes 139296 | tf_op jit(solution)/shard_map/ppermute | solution.py:441
  103.0 1.9 %collective-permute-start.22 = (bf16[68,512]{1,0:T(8,128)(2,1)S(1)}, bf16[68,512]{1,0:T(8,128)(2,1)S(1)}, u32[]{:S(2)}, u32[]{:S(2)}) collective-permute-start(bf16[68,512]{1,0:T(8,128)(2,1)S(1)} %broadcast_select_fusion.11), channel_id=1, source_target_pairs={{0,16},{2,18},{4,20},{6,22},{8,24},{10,26},{12,28},{14,30},{16,0},... | collective-permute-start | bytes 208904 | tf_op jit(solution)/shard_map/ppermute | solution.py:441
  104.9 2.8 %collective-permute-start.14 = (bf16[896,256]{1,0:T(8,128)(2,1)S(1)}, bf16[896,256]{1,0:T(8,128)(2,1)S(1)}, u32[]{:S(2)}, u32[]{:S(2)}) collective-permute-start(bf16[896,256]{1,0:T(8,128)(2,1)S(1)} %get-tuple-element.118), channel_id=1, source_target_pairs={{2,0},{4,2},{6,4},{8,6},{10,8},{12,10},{14,12},{16,14},{18,16},{20... | collective-permute-start | bytes 1376264 | tf_op jit(solution)/shard_map/ppermute | solution.py:436
  107.7 2.1 %collective-permute-done.22 = bf16[68,512]{1,0:T(8,128)(2,1)S(1)} collective-permute-done((bf16[68,512]{1,0:T(8,128)(2,1)S(1)}, bf16[68,512]{1,0:T(8,128)(2,1)S(1)}, u32[]{:S(2)}, u32[]{:S(2)}) %collective-permute-start.22) | collective-permute-done | bytes 69664 | tf_op jit(solution)/shard_map/ppermute | solution.py:441
  111.2 8.6 %collective-permute-done.23 = bf16[68,512]{1,0:T(8,128)(2,1)S(1)} collective-permute-done((bf16[68,512]{1,0:T(8,128)(2,1)S(1)}, bf16[68,512]{1,0:T(8,128)(2,1)S(1)}, u32[]{:S(2)}, u32[]{:S(2)}) %collective-permute-start.23) | collective-permute-done | bytes 69664 | tf_op jit(solution)/shard_map/ppermute | solution.py:441
  119.9 6.0 %collective-permute-start.24 = (bf16[136,512]{1,0:T(8,128)(2,1)S(1)}, bf16[136,512]{1,0:T(8,128)(2,1)S(1)}, u32[]{:S(2)}, u32[]{:S(2)}) collective-permute-start(bf16[136,512]{1,0:T(8,128)(2,1)S(1)} %maximum_select_fusion.14), channel_id=1, source_target_pairs={{0,8},{2,10},{4,12},{6,14},{8,0},{10,2},{12,4},{14,6},{16,24},{18,... | collective-permute-start | bytes 417800 | tf_op jit(solution)/shard_map/ppermute | solution.py:441
  125.9 2.9 %collective-permute-start.33 = (bf16[128,512]{1,0:T(8,128)(2,1)S(1)}, bf16[128,512]{1,0:T(8,128)(2,1)S(1)}, u32[]{:S(2)}, u32[]{:S(2)}) collective-permute-start(bf16[128,512]{1,0:T(8,128)(2,1)S(1)} %add_convert_fusion.10), channel_id=1, source_target_pairs={{0,16},{2,18},{4,20},{6,22},{8,24},{10,26},{12,28},{14,30},{16,0},... | collective-permute-start | bytes 393224 | tf_op jit(solution)/shard_map/ppermute | solution.py:441
  129.7 2.5 %all-reduce = (f32[896]{0:T(1024)S(1)}, f32[896]{0:T(1024)S(1)}) all-reduce(f32[896]{0:T(1024)S(1)} %get-tuple-element.110, f32[896]{0:T(1024)S(1)} %get-tuple-element.109), channel_id=1, replica_groups=mesh['nodes'=16,'heads'=2] {'heads'}, use_global_device_ids=true, to_apply=%region_5.6 | all-reduce | flops 1792 | bytes 14336 | tf_op jit(solution)/shard_map/psum | solution.py:630
  133.5 2.5 %multiply_add_fusion = f32[896,256]{1,0:T(8,128)} fusion(f32[896,256]{1,0:T(8,128)S(1)} %get-tuple-element.76, f32[896,256]{1,0:T(8,128)S(1)} %get-tuple-element.138, f32[896,512]{1,0:T(8,128)} %copy-done.14, f32[896]{0:T(1024)S(1)} %get-tuple-element.111, f32[896]{0:T(1024)S(1)} %broadcast_multiply_fusion, f32[896]{0:T(1024)S(1)} %add_rsqrt_fusion), kind=kLoop, calls=%fused_computation.26 | loop fusion | flops 1605632 | bytes 3680768 | tf_op jit(solution)/shard_map/add | solution.py:633
  136.0 2.0 %collective-permute-done.25 = bf16[128,512]{1,0:T(8,128)(2,1)S(1)} collective-permute-done((bf16[128,512]{1,0:T(8,128)(2,1)S(1)}, bf16[128,512]{1,0:T(8,128)(2,1)S(1)}, u32[]{:S(2)}, u32[]{:S(2)}) %collective-permute-start.25) | collective-permute-done | bytes 131104 | tf_op jit(solution)/shard_map/ppermute | solution.py:441
  138.1 1.7 %collective-permute-start.26 = (bf16[256,512]{1,0:T(8,128)(2,1)S(1)}, bf16[256,512]{1,0:T(8,128)(2,1)S(1)}, u32[]{:S(2)}, u32[]{:S(2)}) collective-permute-start(bf16[256,512]{1,0:T(8,128)(2,1)S(1)} %maximum_select_fusion.10), channel_id=1, source_target_pairs={{0,2},{2,0},{4,6},{6,4},{8,10},{10,8},{12,14},{14,12},{16,18},{18,... | collective-permute-start | bytes 786440 | tf_op jit(solution)/shard_map/ppermute | solution.py:441
  142.9 1.7 %collective-permute-start.35 = (bf16[256,512]{1,0:T(8,128)(2,1)S(1)}, bf16[256,512]{1,0:T(8,128)(2,1)S(1)}, u32[]{:S(2)}, u32[]{:S(2)}) collective-permute-start(bf16[256,512]{1,0:T(8,128)(2,1)S(1)} %get-tuple-element.127), channel_id=1, source_target_pairs={{0,4},{2,6},{4,0},{6,2},{8,12},{10,14},{12,8},{14,10},{16,20},{18,... | collective-permute-start | bytes 786440 | tf_op jit(solution)/shard_map/ppermute | solution.py:441
  144.7 2.7 %collective-permute-done.26 = bf16[256,512]{1,0:T(8,128)(2,1)S(1)} collective-permute-done((bf16[256,512]{1,0:T(8,128)(2,1)S(1)}, bf16[256,512]{1,0:T(8,128)(2,1)S(1)}, u32[]{:S(2)}, u32[]{:S(2)}) %collective-permute-start.26) | collective-permute-done | bytes 262176 | tf_op jit(solution)/shard_map/ppermute | solution.py:441
  150.2 3.0 %collective-permute-done.35 = bf16[256,512]{1,0:T(8,128)(2,1)S(1)} collective-permute-done((bf16[256,512]{1,0:T(8,128)(2,1)S(1)}, bf16[256,512]{1,0:T(8,128)(2,1)S(1)}, u32[]{:S(2)}, u32[]{:S(2)}) %collective-permute-start.35) | collective-permute-done | bytes 262176 | tf_op jit(solution)/shard_map/ppermute | solution.py:441
  157.4 7.8 %collective-permute-done.36 = bf16[512,512]{1,0:T(8,128)(2,1)S(1)} collective-permute-done((bf16[512,512]{1,0:T(8,128)(2,1)S(1)}, bf16[512,512]{1,0:T(8,128)(2,1)S(1)}, u32[]{:S(2)}, u32[]{:S(2)}) %collective-permute-start.36) | collective-permute-done | bytes 524320 | tf_op jit(solution)/shard_map/ppermute | solution.py:441
  (159 shorter events, 51.0 us)
Async XLA Ops:
  0.6 9.6 %collective-permute-start = (bf16[896,256]{1,0:T(8,128)(2,1)}, bf16[896,256]{1,0:T(8,128)(2,1)S(1)}, u32[]{:S(2)}, u32[]{:S(2)}) collective-permute-start(bf16[896,256]{1,0:T(8,128)(2,1)} %xm_ref.1), channel_id=1, source_target_pairs={{0,1},{1,0},{2,3},{3,2},{4,5},{5,4},{6,7},{7,6},{8,9},{9,8},{10,11... | collective-permute-start | bytes 1376264 | tf_op jit(solution)/shard_map/ppermute | solution.py:441
  1.2 23.2 %collective-permute-start.2 = (bf16[896,256]{1,0:T(8,128)(2,1)}, bf16[896,256]{1,0:T(8,128)(2,1)S(1)}, u32[]{:S(2)}, u32[]{:S(2)}) collective-permute-start(bf16[896,256]{1,0:T(8,128)(2,1)} %xm_ref.1), channel_id=1, source_target_pairs={{30,0},{0,2},{2,4},{4,6},{6,8},{8,10},{10,12},{12,14},{14,16},{16,... | collective-permute-start | bytes 1376264 | tf_op jit(solution)/shard_map/ppermute | solution.py:436
  3.7 22.4 %collective-permute-start.6 = (bf16[896,256]{1,0:T(8,128)(2,1)}, bf16[896,256]{1,0:T(8,128)(2,1)S(1)}, u32[]{:S(2)}, u32[]{:S(2)}) collective-permute-start(bf16[896,256]{1,0:T(8,128)(2,1)} %xm_ref.1), channel_id=1, source_target_pairs={{2,0},{4,2},{6,4},{8,6},{10,8},{12,10},{14,12},{16,14},{18,16},{20... | collective-permute-start | bytes 1376264 | tf_op jit(solution)/shard_map/ppermute | solution.py:436
  7.8 15.3 %collective-permute-start.3 = (bf16[896,256]{1,0:T(8,128)(2,1)}, bf16[896,256]{1,0:T(8,128)(2,1)S(1)}, u32[]{:S(2)}, u32[]{:S(2)}) collective-permute-start(bf16[896,256]{1,0:T(8,128)(2,1)} %cm_ref.1), channel_id=1, source_target_pairs={{0,1},{1,0},{2,3},{3,2},{4,5},{5,4},{6,7},{7,6},{8,9},{9,8},{10,11... | collective-permute-start | bytes 1376264 | tf_op jit(solution)/shard_map/ppermute | solution.py:441
  17.4 9.2 %collective-permute-start.1 = (s32[1,896]{1,0:T(1,128)S(1)}, s32[1,896]{1,0:T(1,128)S(1)}, u32[]{:S(2)}, u32[]{:S(2)}) collective-permute-start(s32[1,896]{1,0:T(1,128)S(1)} %broadcast_in_dim.4.ids_ref.id1), channel_id=1, source_target_pairs={{30,0},{0,2},{2,4},{4,6},{6,8},{8,10},{10,12},{12,14},{14,16},{16,... | collective-permute-start | bytes 10760 | tf_op jit(solution)/shard_map/ppermute | solution.py:436
  17.5 10.7 %collective-permute-start.5 = (s32[1,896]{1,0:T(1,128)S(1)}, s32[1,896]{1,0:T(1,128)S(1)}, u32[]{:S(2)}, u32[]{:S(2)}) collective-permute-start(s32[1,896]{1,0:T(1,128)S(1)} %broadcast_in_dim.4.ids_ref.id1), channel_id=1, source_target_pairs={{2,0},{4,2},{6,4},{8,6},{10,8},{12,10},{14,12},{16,14},{18,16},{20... | collective-permute-start | bytes 10760 | tf_op jit(solution)/shard_map/ppermute | solution.py:436
  48.9 16.7 %collective-permute-start.12 = (bf16[512,512]{1,0:T(8,128)(2,1)S(1)}, bf16[512,512]{1,0:T(8,128)(2,1)S(1)}, u32[]{:S(2)}, u32[]{:S(2)}) collective-permute-start(bf16[512,512]{1,0:T(8,128)(2,1)S(1)} %broadcast_select_fusion), channel_id=1, source_target_pairs={{0,4},{2,6},{4,0},{6,2},{8,12},{10,14},{12,8},{14,10},{16,20},{18,... | collective-permute-start | bytes 1572872 | tf_op jit(solution)/shard_map/ppermute | solution.py:441
  52.1 13.8 %collective-permute-start.11 = (bf16[512,512]{1,0:T(8,128)(2,1)S(1)}, bf16[512,512]{1,0:T(8,128)(2,1)S(1)}, u32[]{:S(2)}, u32[]{:S(2)}) collective-permute-start(bf16[512,512]{1,0:T(8,128)(2,1)S(1)} %broadcast_select_fusion.1), channel_id=1, source_target_pairs={{0,2},{2,0},{4,6},{6,4},{8,10},{10,8},{12,14},{14,12},{16,18},{18,... | collective-permute-start | bytes 1572872 | tf_op jit(solution)/shard_map/ppermute | solution.py:441
  52.2 26.2 %collective-permute-start.9 = (bf16[896,256]{1,0:T(8,128)(2,1)S(1)}, bf16[896,256]{1,0:T(8,128)(2,1)S(1)}, u32[]{:S(2)}, u32[]{:S(2)}) collective-permute-start(bf16[896,256]{1,0:T(8,128)(2,1)S(1)} %get-tuple-element.71), channel_id=1, source_target_pairs={{0,1},{1,0},{2,3},{3,2},{4,5},{5,4},{6,7},{7,6},{8,9},{9,8},{10,11... | collective-permute-start | bytes 1376264 | tf_op jit(solution)/shard_map/ppermute | solution.py:441
  66.1 13.4 %collective-permute-start.30 = (bf16[256,512]{1,0:T(8,128)(2,1)S(1)}, bf16[256,512]{1,0:T(8,128)(2,1)S(1)}, u32[]{:S(2)}, u32[]{:S(2)}) collective-permute-start(bf16[256,512]{1,0:T(8,128)(2,1)S(1)} %broadcast_select_fusion.6), channel_id=1, source_target_pairs={{0,4},{2,6},{4,0},{6,2},{8,12},{10,14},{12,8},{14,10},{16,20},{18,... | collective-permute-start | bytes 786440 | tf_op jit(solution)/shard_map/ppermute | solution.py:441
  67.8 11.7 %collective-permute-start.29 = (bf16[256,512]{1,0:T(8,128)(2,1)S(1)}, bf16[256,512]{1,0:T(8,128)(2,1)S(1)}, u32[]{:S(2)}, u32[]{:S(2)}) collective-permute-start(bf16[256,512]{1,0:T(8,128)(2,1)S(1)} %broadcast_select_fusion.5), channel_id=1, source_target_pairs={{0,2},{2,0},{4,6},{6,4},{8,10},{10,8},{12,14},{14,12},{16,18},{18,... | collective-permute-start | bytes 786440 | tf_op jit(solution)/shard_map/ppermute | solution.py:441
  73.1 18.1 %collective-permute-start.13 = (bf16[2688,256]{1,0:T(8,128)(2,1)S(1)}, bf16[2688,256]{1,0:T(8,128)(2,1)S(1)}, u32[]{:S(2)}, u32[]{:S(2)}) collective-permute-start(bf16[2688,256]{1,0:T(8,128)(2,1)S(1)} %get-tuple-element.97), channel_id=1, source_target_pairs={{0,1},{1,0},{2,3},{3,2},{4,5},{5,4},{6,7},{7,6},{8,9},{9,8},{10,11... | collective-permute-start | bytes 4128776 | tf_op jit(solution)/shard_map/ppermute | solution.py:441
  76.5 9.2 %collective-permute-start.17 = (bf16[288,512]{1,0:T(8,128)(2,1)S(1)}, bf16[288,512]{1,0:T(8,128)(2,1)S(1)}, u32[]{:S(2)}, u32[]{:S(2)}) collective-permute-start(bf16[288,512]{1,0:T(8,128)(2,1)S(1)} %broadcast_select_fusion.2), channel_id=1, source_target_pairs={{0,4},{2,6},{4,0},{6,2},{8,12},{10,14},{12,8},{14,10},{16,20},{18,... | collective-permute-start | bytes 884744 | tf_op jit(solution)/shard_map/ppermute | solution.py:441
  79.4 12.3 %collective-permute-start.19 = (bf16[256,512]{1,0:T(8,128)(2,1)S(1)}, bf16[256,512]{1,0:T(8,128)(2,1)S(1)}, u32[]{:S(2)}, u32[]{:S(2)}) collective-permute-start(bf16[256,512]{1,0:T(8,128)(2,1)S(1)} %broadcast_select_fusion.4), channel_id=1, source_target_pairs={{0,2},{2,0},{4,6},{6,4},{8,10},{10,8},{12,14},{14,12},{16,18},{18,... | collective-permute-start | bytes 786440 | tf_op jit(solution)/shard_map/ppermute | solution.py:441
  87.6 7.3 %collective-permute-start.31 = (bf16[256,512]{1,0:T(8,128)(2,1)S(1)}, bf16[256,512]{1,0:T(8,128)(2,1)S(1)}, u32[]{:S(2)}, u32[]{:S(2)}) collective-permute-start(bf16[256,512]{1,0:T(8,128)(2,1)S(1)} %get-tuple-element.113), channel_id=1, source_target_pairs={{0,8},{2,10},{4,12},{6,14},{8,0},{10,2},{12,4},{14,6},{16,24},{18,... | collective-permute-start | bytes 786440 | tf_op jit(solution)/shard_map/ppermute | solution.py:441
  96.9 6.0 %collective-permute-start.21 = (bf16[136,512]{1,0:T(8,128)(2,1)S(1)}, bf16[136,512]{1,0:T(8,128)(2,1)S(1)}, u32[]{:S(2)}, u32[]{:S(2)}) collective-permute-start(bf16[136,512]{1,0:T(8,128)(2,1)S(1)} %broadcast_select_fusion.8), channel_id=1, source_target_pairs={{0,8},{2,10},{4,12},{6,14},{8,0},{10,2},{12,4},{14,6},{16,24},{18,... | collective-permute-start | bytes 417800 | tf_op jit(solution)/shard_map/ppermute | solution.py:441
  98.5 9.2 %collective-permute-start.32 = (bf16[128,512]{1,0:T(8,128)(2,1)S(1)}, bf16[128,512]{1,0:T(8,128)(2,1)S(1)}, u32[]{:S(2)}, u32[]{:S(2)}) collective-permute-start(bf16[128,512]{1,0:T(8,128)(2,1)S(1)} %broadcast_select_fusion.9), channel_id=1, source_target_pairs={{0,16},{2,18},{4,20},{6,22},{8,24},{10,26},{12,28},{14,30},{16,0},... | collective-permute-start | bytes 393224 | tf_op jit(solution)/shard_map/ppermute | solution.py:441
  103.0 6.9 %collective-permute-start.22 = (bf16[68,512]{1,0:T(8,128)(2,1)S(1)}, bf16[68,512]{1,0:T(8,128)(2,1)S(1)}, u32[]{:S(2)}, u32[]{:S(2)}) collective-permute-start(bf16[68,512]{1,0:T(8,128)(2,1)S(1)} %broadcast_select_fusion.11), channel_id=1, source_target_pairs={{0,16},{2,18},{4,20},{6,22},{8,24},{10,26},{12,28},{14,30},{16,0},... | collective-permute-start | bytes 208904 | tf_op jit(solution)/shard_map/ppermute | solution.py:441
  104.9 21.0 %collective-permute-start.14 = (bf16[896,256]{1,0:T(8,128)(2,1)S(1)}, bf16[896,256]{1,0:T(8,128)(2,1)S(1)}, u32[]{:S(2)}, u32[]{:S(2)}) collective-permute-start(bf16[896,256]{1,0:T(8,128)(2,1)S(1)} %get-tuple-element.118), channel_id=1, source_target_pairs={{2,0},{4,2},{6,4},{8,6},{10,8},{12,10},{14,12},{16,14},{18,16},{20... | collective-permute-start | bytes 1376264 | tf_op jit(solution)/shard_map/ppermute | solution.py:436
  107.7 18.2 %collective-permute-start.15 = (bf16[896,256]{1,0:T(8,128)(2,1)S(1)}, bf16[896,256]{1,0:T(8,128)(2,1)S(1)}, u32[]{:S(2)}, u32[]{:S(2)}) collective-permute-start(bf16[896,256]{1,0:T(8,128)(2,1)S(1)} %get-tuple-element.119), channel_id=1, source_target_pairs={{30,0},{0,2},{2,4},{4,6},{6,8},{8,10},{10,12},{12,14},{14,16},{16,... | collective-permute-start | bytes 1376264 | tf_op jit(solution)/shard_map/ppermute | solution.py:436
  109.9 9.9 %collective-permute-start.23 = (bf16[68,512]{1,0:T(8,128)(2,1)S(1)}, bf16[68,512]{1,0:T(8,128)(2,1)S(1)}, u32[]{:S(2)}, u32[]{:S(2)}) collective-permute-start(bf16[68,512]{1,0:T(8,128)(2,1)S(1)} %add_convert_fusion.12), channel_id=1, source_target_pairs={{0,16},{2,18},{4,20},{6,22},{8,24},{10,26},{12,28},{14,30},{16,0},... | collective-permute-start | bytes 208904 | tf_op jit(solution)/shard_map/ppermute | solution.py:441
  119.9 12.3 %collective-permute-start.24 = (bf16[136,512]{1,0:T(8,128)(2,1)S(1)}, bf16[136,512]{1,0:T(8,128)(2,1)S(1)}, u32[]{:S(2)}, u32[]{:S(2)}) collective-permute-start(bf16[136,512]{1,0:T(8,128)(2,1)S(1)} %maximum_select_fusion.14), channel_id=1, source_target_pairs={{0,8},{2,10},{4,12},{6,14},{8,0},{10,2},{12,4},{14,6},{16,24},{18,... | collective-permute-start | bytes 417800 | tf_op jit(solution)/shard_map/ppermute | solution.py:441
  125.9 7.3 %collective-permute-start.33 = (bf16[128,512]{1,0:T(8,128)(2,1)S(1)}, bf16[128,512]{1,0:T(8,128)(2,1)S(1)}, u32[]{:S(2)}, u32[]{:S(2)}) collective-permute-start(bf16[128,512]{1,0:T(8,128)(2,1)S(1)} %add_convert_fusion.10), channel_id=1, source_target_pairs={{0,16},{2,18},{4,20},{6,22},{8,24},{10,26},{12,28},{14,30},{16,0},... | collective-permute-start | bytes 393224 | tf_op jit(solution)/shard_map/ppermute | solution.py:441
  132.3 7.5 %collective-permute-start.27 = (bf16[144,512]{1,0:T(8,128)(2,1)S(1)}, bf16[144,512]{1,0:T(8,128)(2,1)S(1)}, u32[]{:S(2)}, u32[]{:S(2)}) collective-permute-start(bf16[144,512]{1,0:T(8,128)(2,1)S(1)} %slice.246), channel_id=1, source_target_pairs={{0,2},{2,0},{4,6},{6,4},{8,10},{10,8},{12,14},{14,12},{16,18},{18,... | collective-permute-start | bytes 442376 | tf_op jit(solution)/shard_map/ppermute | solution.py:441
  132.4 5.6 %collective-permute-start.25 = (bf16[128,512]{1,0:T(8,128)(2,1)S(1)}, bf16[128,512]{1,0:T(8,128)(2,1)S(1)}, u32[]{:S(2)}, u32[]{:S(2)}) collective-permute-start(bf16[128,512]{1,0:T(8,128)(2,1)S(1)} %slice.243), channel_id=1, source_target_pairs={{0,4},{2,6},{4,0},{6,2},{8,12},{10,14},{12,8},{14,10},{16,20},{18,... | collective-permute-start | bytes 393224 | tf_op jit(solution)/shard_map/ppermute | solution.py:441
  133.2 7.7 %collective-permute-start.34 = (bf16[256,512]{1,0:T(8,128)(2,1)S(1)}, bf16[256,512]{1,0:T(8,128)(2,1)S(1)}, u32[]{:S(2)}, u32[]{:S(2)}) collective-permute-start(bf16[256,512]{1,0:T(8,128)(2,1)S(1)} %maximum_select_fusion.11), channel_id=1, source_target_pairs={{0,8},{2,10},{4,12},{6,14},{8,0},{10,2},{12,4},{14,6},{16,24},{18,... | collective-permute-start | bytes 786440 | tf_op jit(solution)/shard_map/ppermute | solution.py:441
  138.1 9.3 %collective-permute-start.26 = (bf16[256,512]{1,0:T(8,128)(2,1)S(1)}, bf16[256,512]{1,0:T(8,128)(2,1)S(1)}, u32[]{:S(2)}, u32[]{:S(2)}) collective-permute-start(bf16[256,512]{1,0:T(8,128)(2,1)S(1)} %maximum_select_fusion.10), channel_id=1, source_target_pairs={{0,2},{2,0},{4,6},{6,4},{8,10},{10,8},{12,14},{14,12},{16,18},{18,... | collective-permute-start | bytes 786440 | tf_op jit(solution)/shard_map/ppermute | solution.py:441
  139.9 10.0 %collective-permute-start.28 = (bf16[288,512]{1,0:T(8,128)(2,1)S(1)}, bf16[288,512]{1,0:T(8,128)(2,1)S(1)}, u32[]{:S(2)}, u32[]{:S(2)}) collective-permute-start(bf16[288,512]{1,0:T(8,128)(2,1)S(1)} %maximum_select_fusion.8), channel_id=1, source_target_pairs={{0,4},{2,6},{4,0},{6,2},{8,12},{10,14},{12,8},{14,10},{16,20},{18,... | collective-permute-start | bytes 884744 | tf_op jit(solution)/shard_map/ppermute | solution.py:441
  141.2 15.3 %collective-permute-start.37 = (bf16[256,512]{1,0:T(8,128)(2,1)S(1)}, bf16[256,512]{1,0:T(8,128)(2,1)S(1)}, u32[]{:S(2)}, u32[]{:S(2)}) collective-permute-start(bf16[256,512]{1,0:T(8,128)(2,1)S(1)} %get-tuple-element.126), channel_id=1, source_target_pairs={{0,2},{2,0},{4,6},{6,4},{8,10},{10,8},{12,14},{14,12},{16,18},{18,... | collective-permute-start | bytes 786440 | tf_op jit(solution)/shard_map/ppermute | solution.py:441
  142.9 10.3 %collective-permute-start.35 = (bf16[256,512]{1,0:T(8,128)(2,1)S(1)}, bf16[256,512]{1,0:T(8,128)(2,1)S(1)}, u32[]{:S(2)}, u32[]{:S(2)}) collective-permute-start(bf16[256,512]{1,0:T(8,128)(2,1)S(1)} %get-tuple-element.127), channel_id=1, source_target_pairs={{0,4},{2,6},{4,0},{6,2},{8,12},{10,14},{12,8},{14,10},{16,20},{18,... | collective-permute-start | bytes 786440 | tf_op jit(solution)/shard_map/ppermute | solution.py:441
  153.4 11.7 %collective-permute-start.36 = (bf16[512,512]{1,0:T(8,128)(2,1)S(1)}, bf16[512,512]{1,0:T(8,128)(2,1)S(1)}, u32[]{:S(2)}, u32[]{:S(2)}) collective-permute-start(bf16[512,512]{1,0:T(8,128)(2,1)S(1)} %maximum_select_fusion.6), channel_id=1, source_target_pairs={{0,2},{2,0},{4,6},{6,4},{8,10},{10,8},{12,14},{14,12},{16,18},{18,... | collective-permute-start | bytes 1572872 | tf_op jit(solution)/shard_map/ppermute | solution.py:441
  156.7 11.7 %collective-permute-start.38 = (bf16[512,512]{1,0:T(8,128)(2,1)S(1)}, bf16[512,512]{1,0:T(8,128)(2,1)S(1)}, u32[]{:S(2)}, u32[]{:S(2)}) collective-permute-start(bf16[512,512]{1,0:T(8,128)(2,1)S(1)} %maximum_select_fusion.7), channel_id=1, source_target_pairs={{0,4},{2,6},{4,0},{6,2},{8,12},{10,14},{12,8},{14,10},{16,20},{18,... | collective-permute-start | bytes 1572872 | tf_op jit(solution)/shard_map/ppermute | solution.py:441
  (23 other events, 198.5 us)

commit v4 on v3

--- a/solution.py
+++ b/solution.py
@@ -16,10 +16,11 @@
 MIB = 1024 * 1024
 FRONT_MIB = 20
 ATTEND_MIB = 24
-MLP_MIB = 24
-BRANCH_MIB = 20
+MLP_MIB = 28
+BRANCH_MIB = 14
 BACK_MIB = 28
 GRADS_MIB = 24
+UNPACK_MIB = 8
 epsilon = 1e-05
 bf16 = jnp.bfloat16
 f32 = jnp.float32
@@ -133,7 +134,7 @@
     if w_query:
         shapes += [down, along, down]
     operands = (head, ids, mine, theirs, table, w_key, w_value, *w_query)
-    return call(front_kernel, "front", 3, FRONT_MIB, operands, shapes)
+    return call(front_kernel, "front", 6.30, FRONT_MIB, operands, shapes)
 
 
 def forward_kernel(
@@ -215,7 +216,7 @@
         pltpu.VMEM((8, wide), f32),
     ]
     operands = (places, *keys, *values_t, queries, w_out)
-    return call(forward_kernel, "attend_forward", 10, ATTEND_MIB, operands, shapes, scratch)
+    return call(forward_kernel, "attend_forward", 30.00, ATTEND_MIB, operands, shapes, scratch)
 
 
 def mlp_kernel(
@@ -255,7 +256,7 @@
     ]
     shapes = [((rows, wide), kind) for wide, kind in shapes]
     operands = (head, ids, x_mine, x_theirs, part, other, grad_act, table, w_up, w_down)
-    return call(mlp_kernel, "mlp", 5, MLP_MIB, operands, shapes)
+    return call(mlp_kernel, "mlp", 15.00, MLP_MIB, operands, shapes)
 
 
 def branch_kernel(
@@ -311,7 +312,7 @@
         head, ids, middle, cot_mine, cot_theirs, two_part, two_other, mixed_t, inverse,
         table, w_out,
     )
-    return call(branch_kernel, "branch", 3, BRANCH_MIB, operands, shapes)
+    return call(branch_kernel, "branch", 6.30, BRANCH_MIB, operands, shapes)
 
 
 def backward_kernel(
@@ -376,7 +377,7 @@
         pltpu.VMEM((2, window, wide), bf16),
     ]
     operands = (weights, grad_t, cross, queries, *values, *keys_t)
-    return call(backward_kernel, "attend_backward", 12, BACK_MIB, operands, shapes, scratch)
+    return call(backward_kernel, "attend_backward", 25.20, BACK_MIB, operands, shapes, scratch)
 
 
 def grads_kernel(
@@ -427,7 +428,80 @@
         ((levels, width), f32),
     ]
     operands = (head, dkv, dq, *ids, *normed, *units, w_key, w_value, w_query)
-    return call(grads_kernel, "grads", 5, GRADS_MIB, operands, shapes)
+    return call(grads_kernel, "grads", 10.50, GRADS_MIB, operands, shapes)
+
+
+def unpack_mlp_kernel(x_ref, y_ref, a, a_near, a_far, b, b_near, b_far, up_ref, down_ref):
+    x, y = x_ref[0], y_ref[0]
+    count, width = a.shape
+
+    def put_up(ref, start, at_x, at_y):
+        spots = pl.ds(pl.multiple_of(at_y * count, count), count)
+        lanes = pl.ds(pl.multiple_of(at_x * width, width), width)
+        up_ref[spots, lanes] = ref[start : start + count, :].astype(f32)
+
+    def put_down(ref, start, at_x, at_y):
+        spots = pl.ds(pl.multiple_of((2 * at_y + at_x) * count, count), count)
+        down_ref[spots, :] = ref[start : start + count, :].astype(f32)
+
+    put_up(a, 0, x, y)
+    put_up(a_near, 0, x, 1 - y)
+    put_up(a_far, 0, 1 - x, y)
+    put_up(a_far, count, 1 - x, 1 - y)
+    put_down(b, 0, x, y)
+    put_down(b_near, 0, 1 - x, y)
+    put_down(b_far, 0, x, 1 - y)
+    put_down(b_far, count, 1 - x, 1 - y)
+
+
+def unpack_mlp(x, y, *pieces):
+    count, width = pieces[0].shape
+    shapes = [((2 * count, 2 * width), f32), ((4 * count, width), f32)]
+    return call(unpack_mlp_kernel, "unpack_mlp", 4.50, UNPACK_MIB, (x, y, *pieces), shapes)
+
+
+def unpack_kernel(
+    x_ref, y_ref, c, c_near, c_far, d, d_near, d_far, tab,
+    q_ref, k_ref, v_ref, out_ref, tab_ref, first, second,
+):
+    x, y = x_ref[0], y_ref[0]
+    count = d.shape[0]
+
+    def put(total, ref, start, low, high):
+        spots = pl.ds(pl.multiple_of((2 * low + high) * count, count), count)
+        total[spots, :] = ref[start : start + count, :].astype(f32)
+
+    put(first, c, 0, x, y)
+    put(first, c_near, 0, x, 1 - y)
+    put(first, c_far, 0, 1 - x, y)
+    put(first, c_far, count, 1 - x, 1 - y)
+    put(second, d, 0, y, x)
+    put(second, d_near, 0, y, 1 - x)
+    put(second, d_far, 0, 1 - y, x)
+    put(second, d_far, count, 1 - y, 1 - x)
+    wide = q_ref.shape[1]
+    out_rows = out_ref.shape[0]
+    levels = tab_ref.shape[1]
+    q_ref[...] = first[:, :wide]
+    k_ref[...] = first[:, wide:]
+    v_ref[...] = second[:, :wide]
+    out_ref[:, :wide] = second[:out_rows, wide:]
+    out_ref[:, wide:] = second[out_rows:, wide:]
+    table = tab[...] + c_far[2 * count :, :].astype(f32)
+    tab_ref[0] = table[:levels, :wide]
+    tab_ref[1] = table[:levels, wide:]
+    tab_ref[2] = table[levels:, :wide]
+    tab_ref[3] = table[levels:, wide:]
+
+
+def unpack(x, y, c, c_near, c_far, d, d_near, d_far, tab, wide, rows):
+    count, width = d.shape
+    depth = 4 * count
+    shapes = [((depth, wide), f32)] * 3
+    shapes += [((rows, width), f32), ((4, tab.shape[0] // 2, wide), f32)]
+    scratch = [pltpu.VMEM((depth, width), f32)] * 2
+    operands = (x, y, c, c_near, c_far, d, d_near, d_far, tab)
+    return call(unpack_kernel, "unpack", 4.50, UNPACK_MIB, operands, shapes, scratch)
 
 
 def passed_along(block, axis, distance):
@@ -439,6 +513,10 @@
 def swapped(block, axis, bit):
     devices = range(lax.axis_size(axis))
     return lax.ppermute(block, axis, [(i, i ^ bit) for i in devices])
+
+
+def together(*blocks):
+    return lax.optimization_barrier(blocks)
 
 
 def held_until(block, *others):
@@ -457,36 +535,39 @@
     return (keep.astype(f32) + got.astype(f32)).astype(bf16)
 
 
-def doubled(block, axis, bit):
-    upper = (lax.axis_index(axis) & bit) != 0
-    got = swapped(block, axis, bit)
-    return jnp.where(upper, jnp.concatenate([got, block]), jnp.concatenate([block, got]))
-
-
-def far_bits(axis):
-    return [1 << k for k in range(2, lax.axis_size(axis).bit_length() - 1)]
-
-
-def halved(block, axis, bit, *others):
-    send, keep = two_parts(block, axis, bit)
-    return added(keep, held_until(swapped(send, axis, bit), *others))
-
-
-def scatter_far(block, axis, *others):
-    for bit in far_bits(axis):
-        block = halved(block, axis, bit, *others)
+def picked(pieces, place, j):
+    return jnp.where(
+        place == 0,
+        pieces[j],
+        jnp.where(
+            place == 1, pieces[1 ^ j], jnp.where(place == 2, pieces[2 ^ j], pieces[3 ^ j])
+        ),
+    )
+
+
+def quarters(block, place):
+    count = block.shape[0] // 4
+    pieces = [block[i * count : (i + 1) * count] for i in range(4)]
+    return [picked(pieces, place, j) for j in range(4)]
+
+
+def to_others(pieces, axis, bit):
+    return [swapped(piece, axis, (j + 1) * bit) for j, piece in enumerate(pieces)]
+
+
+def total(pieces):
+    result = pieces[0].astype(f32)
+    for piece in pieces[1:]:
+        result = result + piece.astype(f32)
+    return result
+
+
+def sum_further(block, axis):
+    size = lax.axis_size(axis)
+    if size > 16:
+        groups = [[j * 16 + i for j in range(size // 16)] for i in range(16)]
+        block = lax.psum(block, axis, axis_index_groups=groups)
     return block
-
-
-def gather_far(block, axis):
-    for bit in reversed(far_bits(axis)):
-        block = doubled(block, axis, bit)
-    return block
-
-
-def gather_near(first, second, axis):
-    first, second = doubled(first, axis, 2), doubled(second, axis, 1)
-    return doubled(first, axis, 1), doubled(second, axis, 2)
 
 
 def body(
@@ -527,7 +608,7 @@
         jnp.concatenate([cot_other, cotangent], axis=1),
     )
     grad_act = dot(full_cot, w_down, 1, 1).astype(bf16)
-    before_other = swapped(held_until(before, own[0], grad_act), "heads", 1)
+    before_other = swapped(held_until(before, own[0], grad_act, ids_before, ids_after), "heads", 1)
     low = front(head, ids_before, before, before_other, mod_table, w_key, w_value)
     after_other = swapped(after, "heads", 1)
     high = front(head, ids_after, after, after_other, mod_table, w_key, w_value)
@@ -544,6 +625,8 @@
     grad_up = jnp.concatenate([grad_up[:, :hidden], grad_up[:, hidden:]])
     up_send, up_keep = two_parts(grad_up, "nodes", 1)
     down_send, down_keep = two_parts(grad_down, "nodes", 2)
+    place = lax.axis_index("nodes").astype(jnp.int32).reshape(1)
+    x, y, z_low, z_high = [jnp.bitwise_and(jnp.right_shift(place, bit), 1) for bit in range(4)]
     up_got = swapped(up_send, "nodes", 1)
     down_got = swapped(down_send, "nodes", 2)
     mlp_other = swapped(mlp_theirs, "heads", 1)
@@ -574,51 +657,63 @@
         head, dkv, dq, (ids_before, ids_own, ids_after), normed, units,
         w_key, w_value, w_query, levels,
     )
+    one_other = swapped(one_theirs, "heads", 1)
     tab_other = swapped(tab_theirs, "heads", 1)
-    one_other = swapped(one_theirs, "heads", 1)
+    up_got, down_got = held_until((up_got, down_got), grad_q)
+    grad_q, grad_kv, grad_out = sum_further((grad_q, grad_kv, grad_out), "nodes")
+    wide = grad_q.shape[1]
+    spot = jnp.bitwise_and(jnp.right_shift(lax.axis_index("nodes"), 2), 3)
+    m = jnp.concatenate([added(up_keep, up_got), added(down_keep, down_got)])
+    m_parts = quarters(m, spot)
+    c = jnp.concatenate([grad_q, grad_kv[:, :wide]], axis=1)
+    d = jnp.concatenate([grad_out[:, :wide], grad_out[:, wide:]], axis=0)
+    d = jnp.concatenate([grad_kv[:, wide:], d], axis=1)
+    c_send, c_keep = two_parts(c, "nodes", 1)
+    d_send, d_keep = two_parts(d, "nodes", 2)
+    c_send, d_send, *m_parts = together(c_send, d_send, *m_parts)
+    c_got, d_got, tab_other, one_other, *m_got = together(
+        swapped(c_send, "nodes", 1),
+        swapped(d_send, "nodes", 2),
+        tab_other,
+        one_other,
+        *to_others(m_parts[1:], "nodes", 4),
+    )
+    c_send, c_keep = two_parts(added(c_keep, c_got), "nodes", 2)
+    d_send, d_keep = two_parts(added(d_keep, d_got), "nodes", 1)
+    m = sum_further(total([m_parts[0], *m_got]).astype(bf16), "nodes")
     one_all = one_mine.astype(f32) + one_other.astype(f32)
-    to_before = passed_along(one_all[:rows].astype(bf16), "nodes", -1)
-    to_after = passed_along(one_all[2 * rows :].astype(bf16), "nodes", 1)
-    wide = grad_q.shape[1]
-    out_rows = grad_out.shape[0]
-    spare = -(width + 2 * levels) % max(64, lax.axis_size("nodes"))
-    table = jnp.concatenate([tab_mine + tab_other, tab_two], axis=0).astype(bf16)
-    q_and_k = jnp.concatenate([grad_q, grad_kv[:, :wide]], axis=1)
-    v_and_more = jnp.concatenate(
-        [
-            jnp.concatenate(
-                [
-                    grad_kv[:, wide:],
-                    jnp.concatenate([grad_out[:, :half], grad_out[:, half:]], axis=0),
-                ],
-                axis=1,
-            ),
-            table,
-            jnp.zeros((spare, width), bf16),
-        ],
-        axis=0,
-    )
-    qk_send, qk_keep = two_parts(q_and_k, "nodes", 1)
-    qk_got = swapped(qk_send, "nodes", 1)
-    up_sum = added(up_keep, held_until(up_got, qk_send))
-    down_sum = added(down_keep, held_until(down_got, qk_send))
-    mlp_sum = jnp.concatenate([up_sum, down_sum])
-    mlp_sum = halved(mlp_sum, "nodes", 4, one_all)
-    more_sum = halved(v_and_more, "nodes", 2)
-    qk_sum = added(qk_keep, held_until(qk_got, one_all))
-    qk_sum, more_sum = halved(qk_sum, "nodes", 2), halved(more_sum, "nodes", 1)
-    for bit in far_bits("nodes")[1:]:
-        mlp_sum = halved(mlp_sum, "nodes", bit)
-    attn_sum = scatter_far(jnp.concatenate([qk_sum, more_sum]), "nodes")
-    mlp_sum = held_until(mlp_sum, to_before, to_after)
-    mlp_sum = gather_far(mlp_sum, "nodes")
-    up_total, down_total = gather_near(
-        mlp_sum[: mlp_sum.shape[0] // 2], mlp_sum[mlp_sum.shape[0] // 2 :], "nodes"
-    )
-    attn_sum = gather_far(attn_sum, "nodes")
-    count = qk_sum.shape[0]
-    qk_total, more_total = gather_near(attn_sum[:count], attn_sum[count:], "nodes")
-
+    to_before, to_after = one_all[:rows].astype(bf16), one_all[2 * rows :].astype(bf16)
+    c_send, d_send, m, to_before, to_after = together(c_send, d_send, m, to_before, to_after)
+    to_before = passed_along(to_before, "nodes", -1)
+    to_after = passed_along(to_after, "nodes", 1)
+    c_got, d_got, *m_got = together(
+        swapped(c_send, "nodes", 2),
+        swapped(d_send, "nodes", 1),
+        *to_others([m] * 3, "nodes", 4),
+    )
+    m_parts = [picked([m, *m_got], spot, i) for i in range(4)]
+    a, b = jnp.concatenate(m_parts[:2]), jnp.concatenate(m_parts[2:])
+    table = sum_further(jnp.concatenate([tab_mine + tab_other, tab_two], axis=0), "nodes")
+    cd = jnp.concatenate(
+        [total([c_keep, c_got]), total([d_keep, d_got]), table], axis=0
+    ).astype(bf16)
+    a, b, *cd_parts = together(a, b, *quarters(cd, spot))
+    cd_got = together(*to_others(cd_parts[1:], "nodes", 4))
+    cd = total([cd_parts[0], *cd_got]).astype(bf16)
+    a, b, cd, to_before, to_after = together(a, b, cd, to_before, to_after)
+    a_near, b_near, *cd_got = together(
+        swapped(a, "nodes", 2),
+        swapped(b, "nodes", 1),
+        *to_others([cd] * 3, "nodes", 4),
+    )
+    cd = jnp.concatenate([picked([cd, *cd_got], spot, i) for i in range(4)])
+    count = cd.shape[0] // 2 - levels
+    a_send, b_send, c, d = together(
+        jnp.concatenate([a, a_near]),
+        jnp.concatenate([b, b_near]),
+        jnp.concatenate([cd[:count], cd[2 * count :]]),
+        cd[count : 2 * count],
+    )
     grad_one = one_all[rows : 2 * rows] + to_before.astype(f32) + to_after.astype(f32)
     full_in = jnp.concatenate([inputs, in_other], axis=1).astype(f32)
     unit, inverse = norm_rows(full_in)
@@ -633,27 +728,32 @@
     grad_inputs = mid_mine + inverse * (
         gained - sum_gain[:, None] / width - unit * sum_cross[:, None] / width
     )
-    depth = w_query.shape[0]
-    table_total = more_total[depth : depth + 2 * levels].astype(f32)
+    a_far, b_far, c_near, d_near, grad_inputs = together(
+        swapped(a_send, "nodes", 1),
+        swapped(b_send, "nodes", 2),
+        swapped(c, "nodes", 2),
+        swapped(d, "nodes", 1),
+        grad_inputs,
+    )
+    tab = total([c[count:], c_near[count:]])
+    c_send = jnp.concatenate([c[:count], c_near[:count], tab.astype(bf16)])
+    c_far = swapped(c_send, "nodes", 1)
+    d_far = swapped(jnp.concatenate([d, d_near]), "nodes", 2)
+    up_total, down_total = unpack_mlp(x, y, a, a_near, a_far, b, b_near, b_far)
+    c_far, d_far = held_until((c_far, d_far), up_total)
+    query_total, key_total, value_total, out_total, table_total = unpack(
+        x, y, c, c_near, c_far, d, d_near, d_far, tab, wide, grad_out.shape[0]
+    )
     return (
         output,
         grad_inputs,
-        qk_total[:, :wide].astype(f32),
-        qk_total[:, wide:].astype(f32),
-        more_total[:depth, :wide].astype(f32),
-        jnp.concatenate(
-            [more_total[:out_rows, wide:], more_total[out_rows:depth, wide:]], axis=1
-        ).astype(f32),
-        jnp.concatenate([up_total[: width], up_total[width:]], axis=1).astype(f32),
-        down_total.astype(f32),
-        jnp.stack(
-            [
-                table_total[:levels, :half],
-                table_total[:levels, half:],
-                table_total[levels:, :half],
-                table_total[levels:, half:],
-            ]
-        ),
+        query_total,
+        key_total,
+        value_total,
+        out_total,
+        up_total,
+        down_total,
+        table_total,
     )
 
 

time: 171 us -> 168 us (0.982)
  starting transfers between devices: 52.2 us -> 62.1 us
  waiting for transfers between devices: 47.4 us -> 37.8 us
  other arithmetic: 15.7 us -> 7.3 us
  Pallas kernels: 38.1 us -> 42 us
    ppermute x33 -> x37, waiting for transfers between devices: 45.9 us -> 36 us  [swapped(): return lax.ppermute(block, axis, [(i, i ^ bit) for i in devices])]
    ppermute x33 -> x37, starting transfers between devices: 37.1 us -> 46.8 us  [swapped(): return lax.ppermute(block, axis, [(i, i ^ bit) for i in devices])]
    convert_element_type x6 -> x2, other arithmetic: 5.98 us -> 0.11 us  [the longest x1 0.07 us: body(): m = sum_further(total([m_parts[0], *m_got]).astype(bf16), 'nodes')]
    pallas_call x8 -> x10, Pallas kernels: 38.1 us -> 42 us  [call(): pl.pallas_call(kernel, in_specs=[pl.BlockSpec(memory_space=space) for spa...]
    unnamed x32 -> x38, local copies, waits for them, and re-layouts: 4.85 us -> 4.85 us
  transfers between devices with their start and end apart: 39 -> 43, of which waited for: 18 -> 16; matrix products, arithmetic and copies ran while one was open for 13% -> 9% of each run, Pallas kernels for 13% -> 15%
where the time goes in v4:
time: 168 us; the launch traced here: 167 us
  starting transfers between devices  62.1 us (37%)
  Pallas kernels  42 us (25%)
  waiting for transfers between devices  37.8 us (22%)
  matrix products  7.68 us (5%)
  other arithmetic  7.3 us (4%)
  local copies, waits for them, and re-layouts  6.44 us (4%)
  blocking collectives  2.46 us (1%)
    ppermute x37, starting transfers between devices, swapped(): return lax.ppermute(block, axis, [(i, i ^ bit) for i in devices])  46.8 us
    pallas_call x10, Pallas kernels, call(): pl.pallas_call(kernel, in_specs=[pl.BlockSpec(memory_space=space) for spa...  42 us
    ppermute x37, waiting for transfers between devices, swapped(): return lax.ppermute(block, axis, [(i, i ^ bit) for i in devices])  36 us
    ppermute x6, starting transfers between devices, passed_along(): return lax.ppermute(block, axis, route)  15.3 us
    dot_general x7, matrix products, dot(): lax.dot_general(left, right, (((left_dim,), (right_dim,)), ((), ())), pre...  5.49 us
    unnamed x38, local copies, waits for them, and re-layouts  4.85 us
  transfers between devices with their start and end apart: 43, of which 16 were waited for; matrix products, arithmetic and copies ran while one was open for 9% of the time, Pallas kernels for 15%

profile of v4, /device:TPU:0, one launch (start us, length us, event | category | flops | bytes accessed | tf_op | source)
XLA Modules:
  0.0 167.1 jit_solution(13255245772436881259)
XLA Ops:
  1.2 2.6 %collective-permute-start.2 = (bf16[896,256]{1,0:T(8,128)(2,1)}, bf16[896,256]{1,0:T(8,128)(2,1)S(1)}, u32[]{:S(2)}, u32[]{:S(2)}) collective-permute-start(bf16[896,256]{1,0:T(8,128)(2,1)} %xm_ref.1), channel_id=1, source_target_pairs={{30,0},{0,2},{2,4},{4,6},{6,8},{8,10},{10,12},{12,14},{14,16},{16,... | collective-permute-start | bytes 1376264 | tf_op jit(solution)/shard_map/ppermute | solution.py:510
  3.7 4.1 %collective-permute-start.6 = (bf16[896,256]{1,0:T(8,128)(2,1)}, bf16[896,256]{1,0:T(8,128)(2,1)S(1)}, u32[]{:S(2)}, u32[]{:S(2)}) collective-permute-start(bf16[896,256]{1,0:T(8,128)(2,1)} %xm_ref.1), channel_id=1, source_target_pairs={{2,0},{4,2},{6,4},{8,6},{10,8},{12,10},{14,12},{16,14},{18,16},{20... | collective-permute-start | bytes 1376264 | tf_op jit(solution)/shard_map/ppermute | solution.py:510
  9.3 2.2 %convolution_add_fusion = f32[896,256]{1,0:T(8,128)} fusion(s32[896]{0:T(1024)} %param.19, f32[16,512]{1,0:T(8,128)S(1)} %slice_bitcast_fusion, pred[]{:T(512)S(6)} %eq.16), kind=kOutput, calls=%fused_computation.7 | convolution fusion | flops 44288000 | bytes 953857 | tf_op jit(solution)/shard_map/dot_general | solution.py:723
  16.3 2.4 %front.3 = (bf16[896,512]{1,0:T(8,128)(2,1)S(1)}, bf16[896,512]{1,0:T(8,128)(2,1)S(1)}, bf16[896,256]{1,0:T(8,128)(2,1)S(1)}, bf16[256,896]{1,0:T(8,128)(2,1)S(1...) custom-call(s32[1]{0:T(128)} %bitcast.head_ref, ...), custom_call_target="tpu_custom_call" | custom-call | flops 3150000128 | bytes 15750000 | tf_op jit(solution)/shard_map/front/pallas_call | solution.py:94
  18.9 5.6 %collective-permute-start.4 = (s32[1,896]{1,0:T(1,128)S(1)}, s32[1,896]{1,0:T(1,128)S(1)}, u32[]{:S(2)}, u32[]{:S(2)}) collective-permute-start(s32[1,896]{1,0:T(1,128)S(1)} %broadcast_in_dim.2.ids_ref.id1), channel_id=1, source_target_pairs={{2,0},{4,2},{6,4},{8,6},{10,8},{12,10},{14,12},{16,14},{18,16},{20... | collective-permute-start | bytes 10760 | tf_op jit(solution)/shard_map/ppermute | solution.py:510
  31.4 10.3 %attend_forward.1 = (bf16[7,1920,256]{2,1,0:T(8,128)(2,1)S(1)}, bf16[256,896]{1,0:T(8,128)(2,1)S(1)}, f32[8,896]{1,0:T(8,128)S(1)}, bf16[896,512]{1,0:T(8,128)(2,1)S(1)}) custom-call(s32[16,896]{1,0:T(8,128)S(1)} %add_select_fusion.nbr_ref, bf16[896,256]{1,0:T(8,128)(2,1)S(1)} %get-tuple-element.119.k0, bf16[896,256]{1,0:T(8,128)(2,1)S(1)} %get-tuple-element.120.k1, ...), custom_call_target="tpu_custom_call" | custom-call | flops 15000000512 | bytes 75000000 | tf_op jit(solution)/shard_map/attend_forward/pallas_call | solution.py:94
  44.2 4.5 %mlp.1 = (f32[896,512]{1,0:T(8,128)S(1)}, bf16[896,512]{1,0:T(8,128)(2,1)S(1)}, bf16[896,256]{1,0:T(8,128)(2,1)S(1)}, f32[896,256]{1,0:T(8,128)S(1)}, bf16[896,5...) custom-call(s32[1]{0:T(128)} %bitcast.head_ref, ...), custom_call_target="tpu_custom_call" | custom-call | flops 7500000256 | bytes 37500000 | tf_op jit(solution)/shard_map/mlp/pallas_call | solution.py:94
  50.2 1.9 %collective-permute-start.12 = (bf16[512,512]{1,0:T(8,128)(2,1)S(1)}, bf16[512,512]{1,0:T(8,128)(2,1)S(1)}, u32[]{:S(2)}, u32[]{:S(2)}) collective-permute-start(bf16[512,512]{1,0:T(8,128)(2,1)S(1)} %broadcast_select_fusion), channel_id=1, source_target_pairs={{0,4},{2,6},{4,0},{6,2},{8,12},{10,14},{12,8},{14,10},{16,20},{18,... | collective-permute-start | bytes 1572872 | tf_op jit(solution)/shard_map/ppermute | solution.py:515
  53.6 2.5 %branch.1 = (f32[896,256]{1,0:T(8,128)S(1)}, bf16[256,512]{1,0:T(8,128)(2,1)S(1)}, f32[16,512]{1,0:T(8,128)S(1)}, bf16[256,896]{1,0:T(8,128)(2,1)S(1)}, f32[8,896]{1,0:T(8,128)S(1)}) custom-call(s32[1]{0:T(128)} %bitcast.head_ref, s32[1,896]{1,0:T(1,128)S(1)} %broadcast_in_dim.2.ids_ref.id1, f32[896,512]{1,0:T(8,128)S(1)} %get-tuple-element.130.middle_ref, ...), custom_call_target="tpu_custom_call" | custom-call | flops 3150000128 | bytes 15750000 | tf_op jit(solution)/shard_map/branch/pallas_call | solution.py:94
  56.0 10.9 %attend_backward.1 = (bf16[2688,512]{1,0:T(8,128)(2,1)S(1)}, bf16[896,256]{1,0:T(8,128)(2,1)S(1)}) custom-call(bf16[7,1920,256]{2,1,0:T(8,128)(2,1)S(1)} %get-tuple-element.129.e_ref, bf16[256,896]{1,0:T(8,128)(2,1)S(1)} %get-tuple-element.138.grad_ref, f32[8,896]{1,0:T(8,128)S(1)} %get-tuple-element.139.cross_ref, ...), custom_call_target="tpu_custom_call" | custom-call | flops 12600000512 | bytes 63000000 | tf_op jit(solution)/shard_map/attend_backward/pallas_call | solution.py:94
  67.7 1.8 %collective-permute-start.14 = (bf16[256,512]{1,0:T(8,128)(2,1)S(1)}, bf16[256,512]{1,0:T(8,128)(2,1)S(1)}, u32[]{:S(2)}, u32[]{:S(2)}) collective-permute-start(bf16[256,512]{1,0:T(8,128)(2,1)S(1)} %broadcast_select_fusion.5), channel_id=1, source_target_pairs={{0,2},{2,0},{4,6},{6,4},{8,10},{10,8},{12,14},{14,12},{16,18},{18,... | collective-permute-start | bytes 786440 | tf_op jit(solution)/shard_map/ppermute | solution.py:515
  69.7 4.7 %grads.1 = (bf16[512,256]{1,0:T(8,128)(2,1)S(1)}, bf16[512,512]{1,0:T(8,128)(2,1)S(1)}, bf16[2688,256]{1,0:T(8,128)(2,1)S(1)}, bf16[2688,256]{1,0:T(8,128)(2,1)S...) custom-call(s32[1]{0:T(128)} %bitcast.head_ref, bf16[2688,512]{1,0:T(8,128)(2,1)S(1)} %get-tuple-element.144.dkv_ref, ...), custom_call_target="tpu_custom_call" | custom-call | flops 5249999872 | bytes 26250000 | tf_op jit(solution)/shard_map/grads/pallas_call | solution.py:94
  79.1 1.7 %collective-permute-start.16 = (bf16[256,512]{1,0:T(8,128)(2,1)S(1)}, bf16[256,512]{1,0:T(8,128)(2,1)S(1)}, u32[]{:S(2)}, u32[]{:S(2)}) collective-permute-start(bf16[256,512]{1,0:T(8,128)(2,1)S(1)} %broadcast_select_fusion.2), channel_id=1, source_target_pairs={{0,4},{2,6},{4,0},{6,2},{8,12},{10,14},{12,8},{14,10},{16,20},{18,... | collective-permute-start | bytes 786440 | tf_op jit(solution)/shard_map/ppermute | solution.py:515
  80.8 2.6 %collective-permute-start.20 = (bf16[128,512]{1,0:T(8,128)(2,1)S(1)}, bf16[128,512]{1,0:T(8,128)(2,1)S(1)}, u32[]{:S(2)}, u32[]{:S(2)}) collective-permute-start(bf16[128,512]{1,0:T(8,128)(2,1)S(1)} %get-tuple-element.162), channel_id=1, source_target_pairs={{0,16},{2,18},{4,20},{6,22},{8,24},{10,26},{12,28},{14,30},{16,0},... | collective-permute-start | bytes 393224 | tf_op jit(solution)/shard_map/ppermute | solution.py:515
  83.4 3.0 %collective-permute-start.21 = (bf16[128,512]{1,0:T(8,128)(2,1)S(1)}, bf16[128,512]{1,0:T(8,128)(2,1)S(1)}, u32[]{:S(2)}, u32[]{:S(2)}) collective-permute-start(bf16[128,512]{1,0:T(8,128)(2,1)S(1)} %get-tuple-element.163), channel_id=1, source_target_pairs={{0,24},{2,26},{4,28},{6,30},{8,16},{10,18},{12,20},{14,22},{16,8},... | collective-permute-start | bytes 393224 | tf_op jit(solution)/shard_map/ppermute | solution.py:515
  86.9 5.0 %collective-permute-done.20 = bf16[128,512]{1,0:T(8,128)(2,1)S(1)} collective-permute-done((bf16[128,512]{1,0:T(8,128)(2,1)S(1)}, bf16[128,512]{1,0:T(8,128)(2,1)S(1)}, u32[]{:S(2)}, u32[]{:S(2)}) %collective-permute-start.20) | collective-permute-done | bytes 131104 | tf_op jit(solution)/shard_map/ppermute | solution.py:515
  92.7 2.0 %collective-permute-start.24 = (bf16[128,512]{1,0:T(8,128)(2,1)S(1)}, bf16[128,512]{1,0:T(8,128)(2,1)S(1)}, u32[]{:S(2)}, u32[]{:S(2)}) collective-permute-start(bf16[128,512]{1,0:T(8,128)(2,1)S(1)} %add_convert_fusion.9), channel_id=1, source_target_pairs={{0,8},{2,10},{4,12},{6,14},{8,0},{10,2},{12,4},{14,6},{16,24},{18,... | collective-permute-start | bytes 393224 | tf_op jit(solution)/shard_map/ppermute | solution.py:515
  99.3 3.3 %collective-permute-done.22 = bf16[128,512]{1,0:T(8,128)(2,1)S(1)} collective-permute-done((bf16[128,512]{1,0:T(8,128)(2,1)S(1)}, bf16[128,512]{1,0:T(8,128)(2,1)S(1)}, u32[]{:S(2)}, u32[]{:S(2)}) %collective-permute-start.22) | collective-permute-done | bytes 131104 | tf_op jit(solution)/shard_map/ppermute | solution.py:515
  102.6 3.0 %collective-permute-start.30 = (bf16[896,256]{1,0:T(8,128)(2,1)S(1)}, bf16[896,256]{1,0:T(8,128)(2,1)S(1)}, u32[]{:S(2)}, u32[]{:S(2)}) collective-permute-start(bf16[896,256]{1,0:T(8,128)(2,1)S(1)} %get-tuple-element.192), channel_id=1, source_target_pairs={{2,0},{4,2},{6,4},{8,6},{10,8},{12,10},{14,12},{16,14},{18,16},{20... | collective-permute-start | bytes 1376264 | tf_op jit(solution)/shard_map/ppermute | solution.py:510
  107.2 10.8 %collective-permute-start.27 = (bf16[72,512]{1,0:T(8,128)(2,1)S(1)}, bf16[72,512]{1,0:T(8,128)(2,1)S(1)}, u32[]{:S(2)}, u32[]{:S(2)}) collective-permute-start(bf16[72,512]{1,0:T(8,128)(2,1)S(1)} %get-tuple-element.186), channel_id=1, source_target_pairs={{0,8},{2,10},{4,12},{6,14},{8,0},{10,2},{12,4},{14,6},{16,24},{18,... | collective-permute-start | bytes 221192 | tf_op jit(solution)/shard_map/ppermute | solution.py:515
  118.0 2.0 %collective-permute-start.28 = (bf16[72,512]{1,0:T(8,128)(2,1)S(1)}, bf16[72,512]{1,0:T(8,128)(2,1)S(1)}, u32[]{:S(2)}, u32[]{:S(2)}) collective-permute-start(bf16[72,512]{1,0:T(8,128)(2,1)S(1)} %get-tuple-element.187), channel_id=1, source_target_pairs={{0,16},{2,18},{4,20},{6,22},{8,24},{10,26},{12,28},{14,30},{16,0},... | collective-permute-start | bytes 221192 | tf_op jit(solution)/shard_map/ppermute | solution.py:515
  121.4 5.1 %collective-permute-done.28 = bf16[72,512]{1,0:T(8,128)(2,1)S(1)} collective-permute-done((bf16[72,512]{1,0:T(8,128)(2,1)S(1)}, bf16[72,512]{1,0:T(8,128)(2,1)S(1)}, u32[]{:S(2)}, u32[]{:S(2)}) %collective-permute-start.28) | collective-permute-done | bytes 73760 | tf_op jit(solution)/shard_map/ppermute | solution.py:515
  128.0 1.8 %collective-permute-start.35 = (bf16[72,512]{1,0:T(8,128)(2,1)S(1)}, bf16[72,512]{1,0:T(8,128)(2,1)}, u32[]{:S(2)}, u32[]{:S(2)}) collective-permute-start(bf16[72,512]{1,0:T(8,128)(2,1)S(1)} %add_convert_fusion.10), channel_id=1, source_target_pairs={{0,16},{2,18},{4,20},{6,22},{8,24},{10,26},{12,28},{14,30},{16,0},... | collective-permute-start | bytes 221192 | tf_op jit(solution)/shard_map/ppermute | solution.py:515
  132.3 2.5 %all-reduce = (f32[896]{0:T(1024)S(1)}, f32[896]{0:T(1024)S(1)}) all-reduce(f32[896]{0:T(1024)S(1)} %get-tuple-element.224, f32[896]{0:T(1024)S(1)} %get-tuple-element.223), channel_id=1, replica_groups=mesh['nodes'=16,'heads'=2] {'heads'}, use_global_device_ids=true, to_apply=%region_5.6 | all-reduce | flops 1792 | bytes 14336 | tf_op jit(solution)/shard_map/psum | solution.py:725
  138.8 2.0 %collective-permute-start.38 = (bf16[512,512]{1,0:T(8,128)(2,1)S(1)}, bf16[512,512]{1,0:T(8,128)(2,1)S(1)}, u32[]{:S(2)}, u32[]{:S(2)}) collective-permute-start(bf16[512,512]{1,0:T(8,128)(2,1)S(1)} %pad_maximum_fusion.2), channel_id=1, source_target_pairs={{0,4},{2,6},{4,0},{6,2},{8,12},{10,14},{12,8},{14,10},{16,20},{18,... | collective-permute-start | bytes 1572872 | tf_op jit(solution)/shard_map/ppermute | solution.py:515
  140.8 1.9 %collective-permute-start.40 = (bf16[128,512]{1,0:T(8,128)(2,1)S(1)}, bf16[128,512]{1,0:T(8,128)(2,1)S(1)}, u32[]{:S(2)}, u32[]{:S(2)}) collective-permute-start(bf16[128,512]{1,0:T(8,128)(2,1)S(1)} %pad_maximum_fusion.8.d), channel_id=1, source_target_pairs={{0,2},{2,0},{4,6},{6,4},{8,10},{10,8},{12,14},{14,12},{16,18},{18,... | collective-permute-start | bytes 393224 | tf_op jit(solution)/shard_map/ppermute | solution.py:515
  144.1 9.6 %collective-permute-done.40.d_near = bf16[128,512]{1,0:T(8,128)(2,1)S(1)} collective-permute-done((bf16[128,512]{1,0:T(8,128)(2,1)S(1)}, bf16[128,512]{1,0:T(8,128)(2,1)S(1)}, u32[]{:S(2)}, u32[]{:S(2)}) %collective-permute-start.40) | collective-permute-done | bytes 131104 | tf_op jit(solution)/shard_map/ppermute | solution.py:515
  153.7 2.4 %collective-permute-done.39.c_near = bf16[160,512]{1,0:T(8,128)(2,1)S(1)} collective-permute-done((bf16[160,512]{1,0:T(8,128)(2,1)S(1)}, bf16[160,512]{1,0:T(8,128)(2,1)S(1)}, u32[]{:S(2)}, u32[]{:S(2)}) %collective-permute-start.39) | collective-permute-done | bytes 163872 | tf_op jit(solution)/shard_map/ppermute | solution.py:515
  156.2 1.8 %collective-permute-start.42 = (bf16[256,512]{1,0:T(8,128)(2,1)S(1)}, bf16[256,512]{1,0:T(8,128)(2,1)S(1)}, u32[]{:S(2)}, u32[]{:S(2)}) collective-permute-start(bf16[256,512]{1,0:T(8,128)(2,1)S(1)} %pad_maximum_fusion.7), channel_id=1, source_target_pairs={{0,4},{2,6},{4,0},{6,2},{8,12},{10,14},{12,8},{14,10},{16,20},{18,... | collective-permute-start | bytes 786440 | tf_op jit(solution)/shard_map/ppermute | solution.py:515
  159.4 2.2 %unpack_mlp.1 = (f32[512,1024]{1,0:T(8,128)}, f32[1024,512]{1,0:T(8,128)}) custom-call(s32[1]{0:T(128)} %bitcast.5.x_ref, s32[1]{0:T(128)} %bitcast.6.y_ref, bf16[256,512]{1,0:T(8,128)(2,1)S(1)} %pad_maximum_fusion.5.a, bf16[256,512]{1,0:T(8,128)(2,1)S(1)} %collective-permute-done.32.a_near, bf16[512,512]{1,0:T(8,128)(2,1)S(1)} %collective-permute-done.37.a_far, ...), custom_call_target="tpu_custom_call" | custom-call | flops 2249999872 | bytes 11250000 | tf_op jit(solution)/shard_map/unpack_mlp/pallas_call | solution.py:94
  161.6 2.0 %collective-permute-done.42.d_far = bf16[256,512]{1,0:T(8,128)(2,1)S(1)} collective-permute-done((bf16[256,512]{1,0:T(8,128)(2,1)S(1)}, bf16[256,512]{1,0:T(8,128)(2,1)S(1)}, u32[]{:S(2)}, u32[]{:S(2)}) %collective-permute-start.42) | collective-permute-done | bytes 262176 | tf_op jit(solution)/shard_map/ppermute | solution.py:515
  163.6 2.0 %collective-permute-done.41.c_far = bf16[288,512]{1,0:T(8,128)(2,1)S(1)} collective-permute-done((bf16[288,512]{1,0:T(8,128)(2,1)S(1)}, bf16[288,512]{1,0:T(8,128)(2,1)S(1)}, u32[]{:S(2)}, u32[]{:S(2)}) %collective-permute-start.41) | collective-permute-done | bytes 294944 | tf_op jit(solution)/shard_map/ppermute | solution.py:515
  (163 shorter events, 45.8 us)
Async XLA Ops:
  0.6 10.9 %collective-permute-start = (bf16[896,256]{1,0:T(8,128)(2,1)}, bf16[896,256]{1,0:T(8,128)(2,1)S(1)}, u32[]{:S(2)}, u32[]{:S(2)}) collective-permute-start(bf16[896,256]{1,0:T(8,128)(2,1)} %xm_ref.1), channel_id=1, source_target_pairs={{0,1},{1,0},{2,3},{3,2},{4,5},{5,4},{6,7},{7,6},{8,9},{9,8},{10,11... | collective-permute-start | bytes 1376264 | tf_op jit(solution)/shard_map/ppermute | solution.py:515
  1.2 26.2 %collective-permute-start.2 = (bf16[896,256]{1,0:T(8,128)(2,1)}, bf16[896,256]{1,0:T(8,128)(2,1)S(1)}, u32[]{:S(2)}, u32[]{:S(2)}) collective-permute-start(bf16[896,256]{1,0:T(8,128)(2,1)} %xm_ref.1), channel_id=1, source_target_pairs={{30,0},{0,2},{2,4},{4,6},{6,8},{8,10},{10,12},{12,14},{14,16},{16,... | collective-permute-start | bytes 1376264 | tf_op jit(solution)/shard_map/ppermute | solution.py:510
  3.7 22.4 %collective-permute-start.6 = (bf16[896,256]{1,0:T(8,128)(2,1)}, bf16[896,256]{1,0:T(8,128)(2,1)S(1)}, u32[]{:S(2)}, u32[]{:S(2)}) collective-permute-start(bf16[896,256]{1,0:T(8,128)(2,1)} %xm_ref.1), channel_id=1, source_target_pairs={{2,0},{4,2},{6,4},{8,6},{10,8},{12,10},{14,12},{16,14},{18,16},{20... | collective-permute-start | bytes 1376264 | tf_op jit(solution)/shard_map/ppermute | solution.py:510
  7.8 18.4 %collective-permute-start.3 = (bf16[896,256]{1,0:T(8,128)(2,1)}, bf16[896,256]{1,0:T(8,128)(2,1)S(1)}, u32[]{:S(2)}, u32[]{:S(2)}) collective-permute-start(bf16[896,256]{1,0:T(8,128)(2,1)} %cm_ref.1), channel_id=1, source_target_pairs={{0,1},{1,0},{2,3},{3,2},{4,5},{5,4},{6,7},{7,6},{8,9},{9,8},{10,11... | collective-permute-start | bytes 1376264 | tf_op jit(solution)/shard_map/ppermute | solution.py:515
  18.8 8.6 %collective-permute-start.1 = (s32[1,896]{1,0:T(1,128)S(1)}, s32[1,896]{1,0:T(1,128)S(1)}, u32[]{:S(2)}, u32[]{:S(2)}) collective-permute-start(s32[1,896]{1,0:T(1,128)S(1)} %broadcast_in_dim.2.ids_ref.id1), channel_id=1, source_target_pairs={{30,0},{0,2},{2,4},{4,6},{6,8},{8,10},{10,12},{12,14},{14,16},{16,... | collective-permute-start | bytes 10760 | tf_op jit(solution)/shard_map/ppermute | solution.py:510
  18.9 8.5 %collective-permute-start.4 = (s32[1,896]{1,0:T(1,128)S(1)}, s32[1,896]{1,0:T(1,128)S(1)}, u32[]{:S(2)}, u32[]{:S(2)}) collective-permute-start(s32[1,896]{1,0:T(1,128)S(1)} %broadcast_in_dim.2.ids_ref.id1), channel_id=1, source_target_pairs={{2,0},{4,2},{6,4},{8,6},{10,8},{12,10},{14,12},{16,14},{18,16},{20... | collective-permute-start | bytes 10760 | tf_op jit(solution)/shard_map/ppermute | solution.py:510
  50.2 16.7 %collective-permute-start.12 = (bf16[512,512]{1,0:T(8,128)(2,1)S(1)}, bf16[512,512]{1,0:T(8,128)(2,1)S(1)}, u32[]{:S(2)}, u32[]{:S(2)}) collective-permute-start(bf16[512,512]{1,0:T(8,128)(2,1)S(1)} %broadcast_select_fusion), channel_id=1, source_target_pairs={{0,4},{2,6},{4,0},{6,2},{8,12},{10,14},{12,8},{14,10},{16,20},{18,... | collective-permute-start | bytes 1572872 | tf_op jit(solution)/shard_map/ppermute | solution.py:515
  53.5 14.0 %collective-permute-start.11 = (bf16[512,512]{1,0:T(8,128)(2,1)S(1)}, bf16[512,512]{1,0:T(8,128)(2,1)S(1)}, u32[]{:S(2)}, u32[]{:S(2)}) collective-permute-start(bf16[512,512]{1,0:T(8,128)(2,1)S(1)} %broadcast_select_fusion.1), channel_id=1, source_target_pairs={{0,2},{2,0},{4,6},{6,4},{8,10},{10,8},{12,14},{14,12},{16,18},{18,... | collective-permute-start | bytes 1572872 | tf_op jit(solution)/shard_map/ppermute | solution.py:515
  67.7 8.1 %collective-permute-start.14 = (bf16[256,512]{1,0:T(8,128)(2,1)S(1)}, bf16[256,512]{1,0:T(8,128)(2,1)S(1)}, u32[]{:S(2)}, u32[]{:S(2)}) collective-permute-start(bf16[256,512]{1,0:T(8,128)(2,1)S(1)} %broadcast_select_fusion.5), channel_id=1, source_target_pairs={{0,2},{2,0},{4,6},{6,4},{8,10},{10,8},{12,14},{14,12},{16,18},{18,... | collective-permute-start | bytes 786440 | tf_op jit(solution)/shard_map/ppermute | solution.py:515
  69.5 7.7 %collective-permute-start.13 = (bf16[256,512]{1,0:T(8,128)(2,1)S(1)}, bf16[256,512]{1,0:T(8,128)(2,1)S(1)}, u32[]{:S(2)}, u32[]{:S(2)}) collective-permute-start(bf16[256,512]{1,0:T(8,128)(2,1)S(1)} %broadcast_select_fusion.3), channel_id=1, source_target_pairs={{0,4},{2,6},{4,0},{6,2},{8,12},{10,14},{12,8},{14,10},{16,20},{18,... | collective-permute-start | bytes 786440 | tf_op jit(solution)/shard_map/ppermute | solution.py:515
  74.5 17.4 %collective-permute-start.18 = (bf16[2688,256]{1,0:T(8,128)(2,1)S(1)}, bf16[2688,256]{1,0:T(8,128)(2,1)S(1)}, u32[]{:S(2)}, u32[]{:S(2)}) collective-permute-start(bf16[2688,256]{1,0:T(8,128)(2,1)S(1)} %get-tuple-element.160), channel_id=1, source_target_pairs={{0,1},{1,0},{2,3},{3,2},{4,5},{5,4},{6,7},{7,6},{8,9},{9,8},{10,11... | collective-permute-start | bytes 4128776 | tf_op jit(solution)/shard_map/ppermute | solution.py:515
  78.8 13.2 %collective-permute-start.15 = (bf16[256,512]{1,0:T(8,128)(2,1)S(1)}, bf16[256,512]{1,0:T(8,128)(2,1)S(1)}, u32[]{:S(2)}, u32[]{:S(2)}) collective-permute-start(bf16[256,512]{1,0:T(8,128)(2,1)S(1)} %broadcast_select_fusion.4), channel_id=1, source_target_pairs={{0,2},{2,0},{4,6},{6,4},{8,10},{10,8},{12,14},{14,12},{16,18},{18,... | collective-permute-start | bytes 786440 | tf_op jit(solution)/shard_map/ppermute | solution.py:515
  79.1 12.8 %collective-permute-start.16 = (bf16[256,512]{1,0:T(8,128)(2,1)S(1)}, bf16[256,512]{1,0:T(8,128)(2,1)S(1)}, u32[]{:S(2)}, u32[]{:S(2)}) collective-permute-start(bf16[256,512]{1,0:T(8,128)(2,1)S(1)} %broadcast_select_fusion.2), channel_id=1, source_target_pairs={{0,4},{2,6},{4,0},{6,2},{8,12},{10,14},{12,8},{14,10},{16,20},{18,... | collective-permute-start | bytes 786440 | tf_op jit(solution)/shard_map/ppermute | solution.py:515
  80.8 11.1 %collective-permute-start.20 = (bf16[128,512]{1,0:T(8,128)(2,1)S(1)}, bf16[128,512]{1,0:T(8,128)(2,1)S(1)}, u32[]{:S(2)}, u32[]{:S(2)}) collective-permute-start(bf16[128,512]{1,0:T(8,128)(2,1)S(1)} %get-tuple-element.162), channel_id=1, source_target_pairs={{0,16},{2,18},{4,20},{6,22},{8,24},{10,26},{12,28},{14,30},{16,0},... | collective-permute-start | bytes 393224 | tf_op jit(solution)/shard_map/ppermute | solution.py:515
  83.4 8.5 %collective-permute-start.21 = (bf16[128,512]{1,0:T(8,128)(2,1)S(1)}, bf16[128,512]{1,0:T(8,128)(2,1)S(1)}, u32[]{:S(2)}, u32[]{:S(2)}) collective-permute-start(bf16[128,512]{1,0:T(8,128)(2,1)S(1)} %get-tuple-element.163), channel_id=1, source_target_pairs={{0,24},{2,26},{4,28},{6,30},{8,16},{10,18},{12,20},{14,22},{16,8},... | collective-permute-start | bytes 393224 | tf_op jit(solution)/shard_map/ppermute | solution.py:515
  92.7 12.9 %collective-permute-start.24 = (bf16[128,512]{1,0:T(8,128)(2,1)S(1)}, bf16[128,512]{1,0:T(8,128)(2,1)S(1)}, u32[]{:S(2)}, u32[]{:S(2)}) collective-permute-start(bf16[128,512]{1,0:T(8,128)(2,1)S(1)} %add_convert_fusion.9), channel_id=1, source_target_pairs={{0,8},{2,10},{4,12},{6,14},{8,0},{10,2},{12,4},{14,6},{16,24},{18,... | collective-permute-start | bytes 393224 | tf_op jit(solution)/shard_map/ppermute | solution.py:515
  94.7 12.1 %collective-permute-start.25 = (bf16[128,512]{1,0:T(8,128)(2,1)S(1)}, bf16[128,512]{1,0:T(8,128)(2,1)S(1)}, u32[]{:S(2)}, u32[]{:S(2)}) collective-permute-start(bf16[128,512]{1,0:T(8,128)(2,1)S(1)} %add_convert_fusion.9), channel_id=1, source_target_pairs={{0,16},{2,18},{4,20},{6,22},{8,24},{10,26},{12,28},{14,30},{16,0},... | collective-permute-start | bytes 393224 | tf_op jit(solution)/shard_map/ppermute | solution.py:515
  96.2 10.7 %collective-permute-start.26 = (bf16[128,512]{1,0:T(8,128)(2,1)S(1)}, bf16[128,512]{1,0:T(8,128)(2,1)S(1)}, u32[]{:S(2)}, u32[]{:S(2)}) collective-permute-start(bf16[128,512]{1,0:T(8,128)(2,1)S(1)} %add_convert_fusion.9), channel_id=1, source_target_pairs={{0,24},{2,26},{4,28},{6,30},{8,16},{10,18},{12,20},{14,22},{16,8},... | collective-permute-start | bytes 393224 | tf_op jit(solution)/shard_map/ppermute | solution.py:515
  99.1 6.5 %collective-permute-start.23 = (bf16[128,512]{1,0:T(8,128)(2,1)S(1)}, bf16[128,512]{1,0:T(8,128)(2,1)S(1)}, u32[]{:S(2)}, u32[]{:S(2)}) collective-permute-start(bf16[128,512]{1,0:T(8,128)(2,1)S(1)} %broadcast_select_fusion.6), channel_id=1, source_target_pairs={{0,2},{2,0},{4,6},{6,4},{8,10},{10,8},{12,14},{14,12},{16,18},{18,... | collective-permute-start | bytes 393224 | tf_op jit(solution)/shard_map/ppermute | solution.py:515
  102.6 24.0 %collective-permute-start.30 = (bf16[896,256]{1,0:T(8,128)(2,1)S(1)}, bf16[896,256]{1,0:T(8,128)(2,1)S(1)}, u32[]{:S(2)}, u32[]{:S(2)}) collective-permute-start(bf16[896,256]{1,0:T(8,128)(2,1)S(1)} %get-tuple-element.192), channel_id=1, source_target_pairs={{2,0},{4,2},{6,4},{8,6},{10,8},{12,10},{14,12},{16,14},{18,16},{20... | collective-permute-start | bytes 1376264 | tf_op jit(solution)/shard_map/ppermute | solution.py:510
  105.6 21.0 %collective-permute-start.31 = (bf16[896,256]{1,0:T(8,128)(2,1)S(1)}, bf16[896,256]{1,0:T(8,128)(2,1)S(1)}, u32[]{:S(2)}, u32[]{:S(2)}) collective-permute-start(bf16[896,256]{1,0:T(8,128)(2,1)S(1)} %get-tuple-element.193), channel_id=1, source_target_pairs={{30,0},{0,2},{2,4},{4,6},{6,8},{8,10},{10,12},{12,14},{14,16},{16,... | collective-permute-start | bytes 1376264 | tf_op jit(solution)/shard_map/ppermute | solution.py:510
  107.2 14.2 %collective-permute-start.27 = (bf16[72,512]{1,0:T(8,128)(2,1)S(1)}, bf16[72,512]{1,0:T(8,128)(2,1)S(1)}, u32[]{:S(2)}, u32[]{:S(2)}) collective-permute-start(bf16[72,512]{1,0:T(8,128)(2,1)S(1)} %get-tuple-element.186), channel_id=1, source_target_pairs={{0,8},{2,10},{4,12},{6,14},{8,0},{10,2},{12,4},{14,6},{16,24},{18,... | collective-permute-start | bytes 221192 | tf_op jit(solution)/shard_map/ppermute | solution.py:515
  118.0 8.5 %collective-permute-start.28 = (bf16[72,512]{1,0:T(8,128)(2,1)S(1)}, bf16[72,512]{1,0:T(8,128)(2,1)S(1)}, u32[]{:S(2)}, u32[]{:S(2)}) collective-permute-start(bf16[72,512]{1,0:T(8,128)(2,1)S(1)} %get-tuple-element.187), channel_id=1, source_target_pairs={{0,16},{2,18},{4,20},{6,22},{8,24},{10,26},{12,28},{14,30},{16,0},... | collective-permute-start | bytes 221192 | tf_op jit(solution)/shard_map/ppermute | solution.py:515
  126.6 8.2 %collective-permute-start.34 = (bf16[72,512]{1,0:T(8,128)(2,1)S(1)}, bf16[72,512]{1,0:T(8,128)(2,1)S(1)}, u32[]{:S(2)}, u32[]{:S(2)}) collective-permute-start(bf16[72,512]{1,0:T(8,128)(2,1)S(1)} %add_convert_fusion.10), channel_id=1, source_target_pairs={{0,8},{2,10},{4,12},{6,14},{8,0},{10,2},{12,4},{14,6},{16,24},{18,... | collective-permute-start | bytes 221192 | tf_op jit(solution)/shard_map/ppermute | solution.py:515
  128.0 7.1 %collective-permute-start.35 = (bf16[72,512]{1,0:T(8,128)(2,1)S(1)}, bf16[72,512]{1,0:T(8,128)(2,1)}, u32[]{:S(2)}, u32[]{:S(2)}) collective-permute-start(bf16[72,512]{1,0:T(8,128)(2,1)S(1)} %add_convert_fusion.10), channel_id=1, source_target_pairs={{0,16},{2,18},{4,20},{6,22},{8,24},{10,26},{12,28},{14,30},{16,0},... | collective-permute-start | bytes 221192 | tf_op jit(solution)/shard_map/ppermute | solution.py:515
  134.8 23.7 %collective-permute-start.9 = (bf16[896,256]{1,0:T(8,128)(2,1)S(1)}, bf16[896,256]{1,0:T(8,128)(2,1)S(1)}, u32[]{:S(2)}, u32[]{:S(2)}) collective-permute-start(bf16[896,256]{1,0:T(8,128)(2,1)S(1)} %get-tuple-element.128), channel_id=1, source_target_pairs={{0,1},{1,0},{2,3},{3,2},{4,5},{5,4},{6,7},{7,6},{8,9},{9,8},{10,11... | collective-permute-start | bytes 1376264 | tf_op jit(solution)/shard_map/ppermute | solution.py:515
  138.6 17.6 %collective-permute-start.37 = (bf16[512,512]{1,0:T(8,128)(2,1)S(1)}, bf16[512,512]{1,0:T(8,128)(2,1)S(1)}, u32[]{:S(2)}, u32[]{:S(2)}) collective-permute-start(bf16[512,512]{1,0:T(8,128)(2,1)S(1)} %pad_maximum_fusion.1), channel_id=1, source_target_pairs={{0,2},{2,0},{4,6},{6,4},{8,10},{10,8},{12,14},{14,12},{16,18},{18,... | collective-permute-start | bytes 1572872 | tf_op jit(solution)/shard_map/ppermute | solution.py:515
  138.8 17.4 %collective-permute-start.38 = (bf16[512,512]{1,0:T(8,128)(2,1)S(1)}, bf16[512,512]{1,0:T(8,128)(2,1)S(1)}, u32[]{:S(2)}, u32[]{:S(2)}) collective-permute-start(bf16[512,512]{1,0:T(8,128)(2,1)S(1)} %pad_maximum_fusion.2), channel_id=1, source_target_pairs={{0,4},{2,6},{4,0},{6,2},{8,12},{10,14},{12,8},{14,10},{16,20},{18,... | collective-permute-start | bytes 1572872 | tf_op jit(solution)/shard_map/ppermute | solution.py:515
  140.8 15.3 %collective-permute-start.39 = (bf16[160,512]{1,0:T(8,128)(2,1)S(1)}, bf16[160,512]{1,0:T(8,128)(2,1)S(1)}, u32[]{:S(2)}, u32[]{:S(2)}) collective-permute-start(bf16[160,512]{1,0:T(8,128)(2,1)S(1)} %fusion.8.c), channel_id=1, source_target_pairs={{0,4},{2,6},{4,0},{6,2},{8,12},{10,14},{12,8},{14,10},{16,20},{18,... | collective-permute-start | bytes 491528 | tf_op jit(solution)/shard_map/ppermute | solution.py:515
  140.8 12.9 %collective-permute-start.40 = (bf16[128,512]{1,0:T(8,128)(2,1)S(1)}, bf16[128,512]{1,0:T(8,128)(2,1)S(1)}, u32[]{:S(2)}, u32[]{:S(2)}) collective-permute-start(bf16[128,512]{1,0:T(8,128)(2,1)S(1)} %pad_maximum_fusion.8.d), channel_id=1, source_target_pairs={{0,2},{2,0},{4,6},{6,4},{8,10},{10,8},{12,14},{14,12},{16,18},{18,... | collective-permute-start | bytes 393224 | tf_op jit(solution)/shard_map/ppermute | solution.py:515
  156.2 7.4 %collective-permute-start.42 = (bf16[256,512]{1,0:T(8,128)(2,1)S(1)}, bf16[256,512]{1,0:T(8,128)(2,1)S(1)}, u32[]{:S(2)}, u32[]{:S(2)}) collective-permute-start(bf16[256,512]{1,0:T(8,128)(2,1)S(1)} %pad_maximum_fusion.7), channel_id=1, source_target_pairs={{0,4},{2,6},{4,0},{6,2},{8,12},{10,14},{12,8},{14,10},{16,20},{18,... | collective-permute-start | bytes 786440 | tf_op jit(solution)/shard_map/ppermute | solution.py:515
  158.0 7.6 %collective-permute-start.41 = (bf16[288,512]{1,0:T(8,128)(2,1)S(1)}, bf16[288,512]{1,0:T(8,128)(2,1)S(1)}, u32[]{:S(2)}, u32[]{:S(2)}) collective-permute-start(bf16[288,512]{1,0:T(8,128)(2,1)S(1)} %pad_maximum_fusion.3), channel_id=1, source_target_pairs={{0,2},{2,0},{4,6},{6,4},{8,10},{10,8},{12,14},{14,12},{16,18},{18,... | collective-permute-start | bytes 884744 | tf_op jit(solution)/shard_map/ppermute | solution.py:515
  (30 other events, 216.2 us)

commit v5 on v4

--- a/solution.py
+++ b/solution.py
@@ -15,11 +15,11 @@
 HUGE = -1e30
 MIB = 1024 * 1024
 FRONT_MIB = 20
-ATTEND_MIB = 24
-MLP_MIB = 28
+ATTEND_MIB = 20
+MLP_MIB = 24
 BRANCH_MIB = 14
-BACK_MIB = 28
-GRADS_MIB = 24
+BACK_MIB = 32
+GRADS_MIB = 20
 UNPACK_MIB = 8
 epsilon = 1e-05
 bf16 = jnp.bfloat16
@@ -134,7 +134,7 @@
     if w_query:
         shapes += [down, along, down]
     operands = (head, ids, mine, theirs, table, w_key, w_value, *w_query)
-    return call(front_kernel, "front", 6.30, FRONT_MIB, operands, shapes)
+    return call(front_kernel, "front", 10.50, FRONT_MIB, operands, shapes)
 
 
 def forward_kernel(
@@ -216,7 +216,7 @@
         pltpu.VMEM((8, wide), f32),
     ]
     operands = (places, *keys, *values_t, queries, w_out)
-    return call(forward_kernel, "attend_forward", 30.00, ATTEND_MIB, operands, shapes, scratch)
+    return call(forward_kernel, "attend_forward", 35.00, ATTEND_MIB, operands, shapes, scratch)
 
 
 def mlp_kernel(
@@ -256,7 +256,7 @@
     ]
     shapes = [((rows, wide), kind) for wide, kind in shapes]
     operands = (head, ids, x_mine, x_theirs, part, other, grad_act, table, w_up, w_down)
-    return call(mlp_kernel, "mlp", 15.00, MLP_MIB, operands, shapes)
+    return call(mlp_kernel, "mlp", 10.50, MLP_MIB, operands, shapes)
 
 
 def branch_kernel(
@@ -377,7 +377,7 @@
         pltpu.VMEM((2, window, wide), bf16),
     ]
     operands = (weights, grad_t, cross, queries, *values, *keys_t)
-    return call(backward_kernel, "attend_backward", 25.20, BACK_MIB, operands, shapes, scratch)
+    return call(backward_kernel, "attend_backward", 67.20, BACK_MIB, operands, shapes, scratch)
 
 
 def grads_kernel(
@@ -428,7 +428,7 @@
         ((levels, width), f32),
     ]
     operands = (head, dkv, dq, *ids, *normed, *units, w_key, w_value, w_query)
-    return call(grads_kernel, "grads", 10.50, GRADS_MIB, operands, shapes)
+    return call(grads_kernel, "grads", 17.50, GRADS_MIB, operands, shapes)
 
 
 def unpack_mlp_kernel(x_ref, y_ref, a, a_near, a_far, b, b_near, b_far, up_ref, down_ref):
@@ -457,7 +457,7 @@
 def unpack_mlp(x, y, *pieces):
     count, width = pieces[0].shape
     shapes = [((2 * count, 2 * width), f32), ((4 * count, width), f32)]
-    return call(unpack_mlp_kernel, "unpack_mlp", 4.50, UNPACK_MIB, (x, y, *pieces), shapes)
+    return call(unpack_mlp_kernel, "unpack_mlp", 2.10, UNPACK_MIB, (x, y, *pieces), shapes)
 
 
 def unpack_kernel(
@@ -501,7 +501,7 @@
     shapes += [((rows, width), f32), ((4, tab.shape[0] // 2, wide), f32)]
     scratch = [pltpu.VMEM((depth, width), f32)] * 2
     operands = (x, y, c, c_near, c_far, d, d_near, d_far, tab)
-    return call(unpack_kernel, "unpack", 4.50, UNPACK_MIB, operands, shapes, scratch)
+    return call(unpack_kernel, "unpack", 5.60, UNPACK_MIB, operands, shapes, scratch)
 
 
 def passed_along(block, axis, distance):
@@ -608,7 +608,8 @@
         jnp.concatenate([cot_other, cotangent], axis=1),
     )
     grad_act = dot(full_cot, w_down, 1, 1).astype(bf16)
-    before_other = swapped(held_until(before, own[0], grad_act, ids_before, ids_after), "heads", 1)
+    before, after = held_until((before, after), own[0], grad_act, ids_before, ids_after)
+    before_other = swapped(before, "heads", 1)
     low = front(head, ids_before, before, before_other, mod_table, w_key, w_value)
     after_other = swapped(after, "heads", 1)
     high = front(head, ids_after, after, after_other, mod_table, w_key, w_value)

time: 168 us -> 167 us (level)
    unnamed x38 -> x36, local copies, waits for them, and re-layouts: 4.85 us -> 4.84 us
  transfers between devices with their start and end apart: 43 -> 43, of which waited for: 16 -> 19; matrix products, arithmetic and copies ran while one was open for 9% -> 8% of each run, Pallas kernels for 15% -> 15%
where the time goes in v5:
time: 167 us
  starting transfers between devices  63.1 us (38%)
  Pallas kernels  41.8 us (25%)
  waiting for transfers between devices  38.2 us (23%)
  other arithmetic  8.17 us (5%)
  matrix products  6.08 us (4%)
  local copies, waits for them, and re-layouts  5.67 us (3%)
  blocking collectives  2.46 us (1%)
    ppermute x37, starting transfers between devices, swapped(): return lax.ppermute(block, axis, [(i, i ^ bit) for i in devices])  47.5 us
    pallas_call x10, Pallas kernels, call(): pl.pallas_call(kernel, in_specs=[pl.BlockSpec(memory_space=space) for spa...  41.8 us
    ppermute x37, waiting for transfers between devices, swapped(): return lax.ppermute(block, axis, [(i, i ^ bit) for i in devices])  35.5 us
    ppermute x6, starting transfers between devices, passed_along(): return lax.ppermute(block, axis, route)  15.6 us
    dot_general x7, matrix products, dot(): lax.dot_general(left, right, (((left_dim,), (right_dim,)), ((), ())), pre...  5.5 us
    unnamed x36, local copies, waits for them, and re-layouts  4.84 us
  transfers between devices with their start and end apart: 43, of which 19 were waited for; matrix products, arithmetic and copies ran while one was open for 8% of the time, Pallas kernels for 15%

profile of v5, /device:TPU:0, one launch (start us, length us, event | category | flops | bytes accessed | tf_op | source)
XLA Modules:
  0.0 166.7 jit_solution(4140177040236770569)
XLA Ops:
  1.2 2.6 %collective-permute-start.2 = (bf16[896,256]{1,0:T(8,128)(2,1)}, bf16[896,256]{1,0:T(8,128)(2,1)S(1)}, u32[]{:S(2)}, u32[]{:S(2)}) collective-permute-start(bf16[896,256]{1,0:T(8,128)(2,1)} %xm_ref.1), channel_id=1, source_target_pairs={{30,0},{0,2},{2,4},{4,6},{6,8},{8,10},{10,12},{12,14},{14,16},{16,... | collective-permute-start | bytes 1376264 | tf_op jit(solution)/shard_map/ppermute | solution.py:510
  3.7 4.1 %collective-permute-start.3 = (bf16[896,256]{1,0:T(8,128)(2,1)}, bf16[896,256]{1,0:T(8,128)(2,1)S(1)}, u32[]{:S(2)}, u32[]{:S(2)}) collective-permute-start(bf16[896,256]{1,0:T(8,128)(2,1)} %xm_ref.1), channel_id=1, source_target_pairs={{2,0},{4,2},{6,4},{8,6},{10,8},{12,10},{14,12},{16,14},{18,16},{20... | collective-permute-start | bytes 1376264 | tf_op jit(solution)/shard_map/ppermute | solution.py:510
  14.2 2.4 %front.3 = (bf16[896,512]{1,0:T(8,128)(2,1)S(1)}, bf16[896,512]{1,0:T(8,128)(2,1)S(1)}, bf16[896,256]{1,0:T(8,128)(2,1)S(1)}, bf16[256,896]{1,0:T(8,128)(2,1)S(1...) custom-call(s32[1]{0:T(128)} %bitcast.head_ref, ...), custom_call_target="tpu_custom_call" | custom-call | flops 5249999872 | bytes 26250000 | tf_op jit(solution)/shard_map/front/pallas_call | solution.py:94
  16.8 5.6 %collective-permute-start.5 = (s32[1,896]{1,0:T(1,128)S(1)}, s32[1,896]{1,0:T(1,128)S(1)}, u32[]{:S(2)}, u32[]{:S(2)}) collective-permute-start(s32[1,896]{1,0:T(1,128)S(1)} %broadcast_in_dim.2.ids_ref.id1), channel_id=1, source_target_pairs={{2,0},{4,2},{6,4},{8,6},{10,8},{12,10},{14,12},{16,14},{18,16},{20... | collective-permute-start | bytes 10760 | tf_op jit(solution)/shard_map/ppermute | solution.py:510
  24.4 1.8 %collective-permute-done.3.mine_ref = bf16[896,256]{1,0:T(8,128)(2,1)S(1)} collective-permute-done((bf16[896,256]{1,0:T(8,128)(2,1)}, bf16[896,256]{1,0:T(8,128)(2,1)S(1)}, u32[]{:S(2)}, u32[]{:S(2)}) %collective-permute-start.3) | collective-permute-done | bytes 458784 | tf_op jit(solution)/shard_map/ppermute | solution.py:510
  29.6 1.5 front.4
  31.1 10.3 %attend_forward.1 = (bf16[7,1920,256]{2,1,0:T(8,128)(2,1)S(1)}, bf16[256,896]{1,0:T(8,128)(2,1)S(1)}, f32[8,896]{1,0:T(8,128)S(1)}, bf16[896,512]{1,0:T(8,128)(2,1)S(1)}) custom-call(s32[16,896]{1,0:T(8,128)S(1)} %add_select_fusion.nbr_ref, bf16[896,256]{1,0:T(8,128)(2,1)S(1)} %get-tuple-element.120.k0, bf16[896,256]{1,0:T(8,128)(2,1)S(1)} %get-tuple-element.121.k1, ...), custom_call_target="tpu_custom_call" | custom-call | flops 17500000256 | bytes 87500000 | tf_op jit(solution)/shard_map/attend_forward/pallas_call | solution.py:94
  43.9 4.4 %mlp.1 = (f32[896,512]{1,0:T(8,128)S(1)}, bf16[896,512]{1,0:T(8,128)(2,1)S(1)}, bf16[896,256]{1,0:T(8,128)(2,1)S(1)}, f32[896,256]{1,0:T(8,128)S(1)}, bf16[896,5...) custom-call(s32[1]{0:T(128)} %bitcast.head_ref, ...), custom_call_target="tpu_custom_call" | custom-call | flops 5249999872 | bytes 26250000 | tf_op jit(solution)/shard_map/mlp/pallas_call | solution.py:94
  50.0 1.8 %collective-permute-start.12 = (bf16[512,512]{1,0:T(8,128)(2,1)S(1)}, bf16[512,512]{1,0:T(8,128)(2,1)S(1)}, u32[]{:S(2)}, u32[]{:S(2)}) collective-permute-start(bf16[512,512]{1,0:T(8,128)(2,1)S(1)} %broadcast_select_fusion), channel_id=1, source_target_pairs={{0,4},{2,6},{4,0},{6,2},{8,12},{10,14},{12,8},{14,10},{16,20},{18,... | collective-permute-start | bytes 1572872 | tf_op jit(solution)/shard_map/ppermute | solution.py:515
  53.5 2.5 %branch.1 = (f32[896,256]{1,0:T(8,128)S(1)}, bf16[256,512]{1,0:T(8,128)(2,1)S(1)}, f32[16,512]{1,0:T(8,128)S(1)}, bf16[256,896]{1,0:T(8,128)(2,1)S(1)}, f32[8,896]{1,0:T(8,128)S(1)}) custom-call(s32[1]{0:T(128)} %bitcast.head_ref, s32[1,896]{1,0:T(1,128)S(1)} %broadcast_in_dim.2.ids_ref.id1, f32[896,512]{1,0:T(8,128)S(1)} %get-tuple-element.132.middle_ref, ...), custom_call_target="tpu_custom_call" | custom-call | flops 3150000128 | bytes 15750000 | tf_op jit(solution)/shard_map/branch/pallas_call | solution.py:94
  55.9 10.8 %attend_backward.1 = (bf16[2688,512]{1,0:T(8,128)(2,1)S(1)}, bf16[896,256]{1,0:T(8,128)(2,1)S(1)}) custom-call(bf16[7,1920,256]{2,1,0:T(8,128)(2,1)S(1)} %get-tuple-element.131.e_ref, bf16[256,896]{1,0:T(8,128)(2,1)S(1)} %get-tuple-element.140.grad_ref, f32[8,896]{1,0:T(8,128)S(1)} %get-tuple-element.141.cross_ref, ...), custom_call_target="tpu_custom_call" | custom-call | flops 33600000000 | bytes 168000000 | tf_op jit(solution)/shard_map/attend_backward/pallas_call | solution.py:94
  67.3 1.7 %collective-permute-start.14 = (bf16[256,512]{1,0:T(8,128)(2,1)S(1)}, bf16[256,512]{1,0:T(8,128)(2,1)S(1)}, u32[]{:S(2)}, u32[]{:S(2)}) collective-permute-start(bf16[256,512]{1,0:T(8,128)(2,1)S(1)} %broadcast_select_fusion.5), channel_id=1, source_target_pairs={{0,2},{2,0},{4,6},{6,4},{8,10},{10,8},{12,14},{14,12},{16,18},{18,... | collective-permute-start | bytes 786440 | tf_op jit(solution)/shard_map/ppermute | solution.py:515
  69.3 4.7 %grads.1 = (bf16[512,256]{1,0:T(8,128)(2,1)S(1)}, bf16[512,512]{1,0:T(8,128)(2,1)S(1)}, bf16[2688,256]{1,0:T(8,128)(2,1)S(1)}, bf16[2688,256]{1,0:T(8,128)(2,1)S...) custom-call(s32[1]{0:T(128)} %bitcast.head_ref, bf16[2688,512]{1,0:T(8,128)(2,1)S(1)} %get-tuple-element.146.dkv_ref, ...), custom_call_target="tpu_custom_call" | custom-call | flops 8750000128 | bytes 43750000 | tf_op jit(solution)/shard_map/grads/pallas_call | solution.py:94
  80.5 2.6 %collective-permute-start.20 = (bf16[128,512]{1,0:T(8,128)(2,1)S(1)}, bf16[128,512]{1,0:T(8,128)(2,1)S(1)}, u32[]{:S(2)}, u32[]{:S(2)}) collective-permute-start(bf16[128,512]{1,0:T(8,128)(2,1)S(1)} %get-tuple-element.164), channel_id=1, source_target_pairs={{0,16},{2,18},{4,20},{6,22},{8,24},{10,26},{12,28},{14,30},{16,0},... | collective-permute-start | bytes 393224 | tf_op jit(solution)/shard_map/ppermute | solution.py:515
  83.1 3.0 %collective-permute-start.21 = (bf16[128,512]{1,0:T(8,128)(2,1)S(1)}, bf16[128,512]{1,0:T(8,128)(2,1)S(1)}, u32[]{:S(2)}, u32[]{:S(2)}) collective-permute-start(bf16[128,512]{1,0:T(8,128)(2,1)S(1)} %get-tuple-element.165), channel_id=1, source_target_pairs={{0,24},{2,26},{4,28},{6,30},{8,16},{10,18},{12,20},{14,22},{16,8},... | collective-permute-start | bytes 393224 | tf_op jit(solution)/shard_map/ppermute | solution.py:515
  86.6 5.0 %collective-permute-done.20 = bf16[128,512]{1,0:T(8,128)(2,1)S(1)} collective-permute-done((bf16[128,512]{1,0:T(8,128)(2,1)S(1)}, bf16[128,512]{1,0:T(8,128)(2,1)S(1)}, u32[]{:S(2)}, u32[]{:S(2)}) %collective-permute-start.20) | collective-permute-done | bytes 131104 | tf_op jit(solution)/shard_map/ppermute | solution.py:515
  92.4 2.0 %collective-permute-start.24 = (bf16[128,512]{1,0:T(8,128)(2,1)S(1)}, bf16[128,512]{1,0:T(8,128)(2,1)S(1)}, u32[]{:S(2)}, u32[]{:S(2)}) collective-permute-start(bf16[128,512]{1,0:T(8,128)(2,1)S(1)} %add_convert_fusion.9), channel_id=1, source_target_pairs={{0,8},{2,10},{4,12},{6,14},{8,0},{10,2},{12,4},{14,6},{16,24},{18,... | collective-permute-start | bytes 393224 | tf_op jit(solution)/shard_map/ppermute | solution.py:515
  99.3 2.9 %collective-permute-done.22 = bf16[128,512]{1,0:T(8,128)(2,1)S(1)} collective-permute-done((bf16[128,512]{1,0:T(8,128)(2,1)S(1)}, bf16[128,512]{1,0:T(8,128)(2,1)S(1)}, u32[]{:S(2)}, u32[]{:S(2)}) %collective-permute-start.22) | collective-permute-done | bytes 131104 | tf_op jit(solution)/shard_map/ppermute | solution.py:515
  102.3 3.3 %collective-permute-start.30 = (bf16[896,256]{1,0:T(8,128)(2,1)S(1)}, bf16[896,256]{1,0:T(8,128)(2,1)S(1)}, u32[]{:S(2)}, u32[]{:S(2)}) collective-permute-start(bf16[896,256]{1,0:T(8,128)(2,1)S(1)} %get-tuple-element.194), channel_id=1, source_target_pairs={{2,0},{4,2},{6,4},{8,6},{10,8},{12,10},{14,12},{16,14},{18,16},{20... | collective-permute-start | bytes 1376264 | tf_op jit(solution)/shard_map/ppermute | solution.py:510
  106.9 10.8 %collective-permute-start.27 = (bf16[72,512]{1,0:T(8,128)(2,1)S(1)}, bf16[72,512]{1,0:T(8,128)(2,1)S(1)}, u32[]{:S(2)}, u32[]{:S(2)}) collective-permute-start(bf16[72,512]{1,0:T(8,128)(2,1)S(1)} %get-tuple-element.188), channel_id=1, source_target_pairs={{0,8},{2,10},{4,12},{6,14},{8,0},{10,2},{12,4},{14,6},{16,24},{18,... | collective-permute-start | bytes 221192 | tf_op jit(solution)/shard_map/ppermute | solution.py:515
  117.7 2.0 %collective-permute-start.28 = (bf16[72,512]{1,0:T(8,128)(2,1)S(1)}, bf16[72,512]{1,0:T(8,128)(2,1)S(1)}, u32[]{:S(2)}, u32[]{:S(2)}) collective-permute-start(bf16[72,512]{1,0:T(8,128)(2,1)S(1)} %get-tuple-element.189), channel_id=1, source_target_pairs={{0,16},{2,18},{4,20},{6,22},{8,24},{10,26},{12,28},{14,30},{16,0},... | collective-permute-start | bytes 221192 | tf_op jit(solution)/shard_map/ppermute | solution.py:515
  121.1 5.1 %collective-permute-done.28 = bf16[72,512]{1,0:T(8,128)(2,1)S(1)} collective-permute-done((bf16[72,512]{1,0:T(8,128)(2,1)S(1)}, bf16[72,512]{1,0:T(8,128)(2,1)S(1)}, u32[]{:S(2)}, u32[]{:S(2)}) %collective-permute-start.28) | collective-permute-done | bytes 73760 | tf_op jit(solution)/shard_map/ppermute | solution.py:515
  127.7 1.7 %collective-permute-start.35 = (bf16[72,512]{1,0:T(8,128)(2,1)S(1)}, bf16[72,512]{1,0:T(8,128)(2,1)}, u32[]{:S(2)}, u32[]{:S(2)}) collective-permute-start(bf16[72,512]{1,0:T(8,128)(2,1)S(1)} %add_convert_fusion.10), channel_id=1, source_target_pairs={{0,16},{2,18},{4,20},{6,22},{8,24},{10,26},{12,28},{14,30},{16,0},... | collective-permute-start | bytes 221192 | tf_op jit(solution)/shard_map/ppermute | solution.py:515
  132.0 2.5 %all-reduce = (f32[896]{0:T(1024)S(1)}, f32[896]{0:T(1024)S(1)}) all-reduce(f32[896]{0:T(1024)S(1)} %get-tuple-element.226, f32[896]{0:T(1024)S(1)} %get-tuple-element.225), channel_id=1, replica_groups=mesh['nodes'=16,'heads'=2] {'heads'}, use_global_device_ids=true, to_apply=%region_5.6 | all-reduce | flops 1792 | bytes 14336 | tf_op jit(solution)/shard_map/psum | solution.py:726
  138.7 1.8 %collective-permute-start.38 = (bf16[512,512]{1,0:T(8,128)(2,1)S(1)}, bf16[512,512]{1,0:T(8,128)(2,1)S(1)}, u32[]{:S(2)}, u32[]{:S(2)}) collective-permute-start(bf16[512,512]{1,0:T(8,128)(2,1)S(1)} %pad_maximum_fusion.2), channel_id=1, source_target_pairs={{0,4},{2,6},{4,0},{6,2},{8,12},{10,14},{12,8},{14,10},{16,20},{18,... | collective-permute-start | bytes 1572872 | tf_op jit(solution)/shard_map/ppermute | solution.py:515
  140.7 1.7 %collective-permute-start.40 = (bf16[128,512]{1,0:T(8,128)(2,1)S(1)}, bf16[128,512]{1,0:T(8,128)(2,1)S(1)}, u32[]{:S(2)}, u32[]{:S(2)}) collective-permute-start(bf16[128,512]{1,0:T(8,128)(2,1)S(1)} %pad_maximum_fusion.8.d), channel_id=1, source_target_pairs={{0,2},{2,0},{4,6},{6,4},{8,10},{10,8},{12,14},{14,12},{16,18},{18,... | collective-permute-start | bytes 393224 | tf_op jit(solution)/shard_map/ppermute | solution.py:515
  143.9 9.5 %collective-permute-done.40.d_near = bf16[128,512]{1,0:T(8,128)(2,1)S(1)} collective-permute-done((bf16[128,512]{1,0:T(8,128)(2,1)S(1)}, bf16[128,512]{1,0:T(8,128)(2,1)S(1)}, u32[]{:S(2)}, u32[]{:S(2)}) %collective-permute-start.40) | collective-permute-done | bytes 131104 | tf_op jit(solution)/shard_map/ppermute | solution.py:515
  153.4 2.4 %collective-permute-done.39.c_near = bf16[160,512]{1,0:T(8,128)(2,1)S(1)} collective-permute-done((bf16[160,512]{1,0:T(8,128)(2,1)S(1)}, bf16[160,512]{1,0:T(8,128)(2,1)S(1)}, u32[]{:S(2)}, u32[]{:S(2)}) %collective-permute-start.39) | collective-permute-done | bytes 163872 | tf_op jit(solution)/shard_map/ppermute | solution.py:515
  155.9 1.8 %collective-permute-start.42 = (bf16[256,512]{1,0:T(8,128)(2,1)S(1)}, bf16[256,512]{1,0:T(8,128)(2,1)S(1)}, u32[]{:S(2)}, u32[]{:S(2)}) collective-permute-start(bf16[256,512]{1,0:T(8,128)(2,1)S(1)} %pad_maximum_fusion.7), channel_id=1, source_target_pairs={{0,4},{2,6},{4,0},{6,2},{8,12},{10,14},{12,8},{14,10},{16,20},{18,... | collective-permute-start | bytes 786440 | tf_op jit(solution)/shard_map/ppermute | solution.py:515
  159.0 2.2 %unpack_mlp.1 = (f32[512,1024]{1,0:T(8,128)}, f32[1024,512]{1,0:T(8,128)}) custom-call(s32[1]{0:T(128)} %bitcast.5.x_ref, s32[1]{0:T(128)} %bitcast.6.y_ref, bf16[256,512]{1,0:T(8,128)(2,1)S(1)} %pad_maximum_fusion.5.a, bf16[256,512]{1,0:T(8,128)(2,1)S(1)} %collective-permute-done.32.a_near, bf16[512,512]{1,0:T(8,128)(2,1)S(1)} %collective-permute-done.37.a_far, ...), custom_call_target="tpu_custom_call" | custom-call | flops 1050000000 | bytes 5250000 | tf_op jit(solution)/shard_map/unpack_mlp/pallas_call | solution.py:94
  161.3 1.7 %collective-permute-done.42.d_far = bf16[256,512]{1,0:T(8,128)(2,1)S(1)} collective-permute-done((bf16[256,512]{1,0:T(8,128)(2,1)S(1)}, bf16[256,512]{1,0:T(8,128)(2,1)S(1)}, u32[]{:S(2)}, u32[]{:S(2)}) %collective-permute-start.42) | collective-permute-done | bytes 262176 | tf_op jit(solution)/shard_map/ppermute | solution.py:515
  163.0 2.3 %collective-permute-done.41.c_far = bf16[288,512]{1,0:T(8,128)(2,1)S(1)} collective-permute-done((bf16[288,512]{1,0:T(8,128)(2,1)S(1)}, bf16[288,512]{1,0:T(8,128)(2,1)S(1)}, u32[]{:S(2)}, u32[]{:S(2)}) %collective-permute-start.41) | collective-permute-done | bytes 294944 | tf_op jit(solution)/shard_map/ppermute | solution.py:515
  (161 shorter events, 46.7 us)
Async XLA Ops:
  0.6 8.8 %collective-permute-start = (bf16[896,256]{1,0:T(8,128)(2,1)}, bf16[896,256]{1,0:T(8,128)(2,1)S(1)}, u32[]{:S(2)}, u32[]{:S(2)}) collective-permute-start(bf16[896,256]{1,0:T(8,128)(2,1)} %xm_ref.1), channel_id=1, source_target_pairs={{0,1},{1,0},{2,3},{3,2},{4,5},{5,4},{6,7},{7,6},{8,9},{9,8},{10,11... | collective-permute-start | bytes 1376264 | tf_op jit(solution)/shard_map/ppermute | solution.py:515
  1.2 23.2 %collective-permute-start.2 = (bf16[896,256]{1,0:T(8,128)(2,1)}, bf16[896,256]{1,0:T(8,128)(2,1)S(1)}, u32[]{:S(2)}, u32[]{:S(2)}) collective-permute-start(bf16[896,256]{1,0:T(8,128)(2,1)} %xm_ref.1), channel_id=1, source_target_pairs={{30,0},{0,2},{2,4},{4,6},{6,8},{8,10},{10,12},{12,14},{14,16},{16,... | collective-permute-start | bytes 1376264 | tf_op jit(solution)/shard_map/ppermute | solution.py:510
  3.7 22.4 %collective-permute-start.3 = (bf16[896,256]{1,0:T(8,128)(2,1)}, bf16[896,256]{1,0:T(8,128)(2,1)S(1)}, u32[]{:S(2)}, u32[]{:S(2)}) collective-permute-start(bf16[896,256]{1,0:T(8,128)(2,1)} %xm_ref.1), channel_id=1, source_target_pairs={{2,0},{4,2},{6,4},{8,6},{10,8},{12,10},{14,12},{16,14},{18,16},{20... | collective-permute-start | bytes 1376264 | tf_op jit(solution)/shard_map/ppermute | solution.py:510
  7.8 14.6 %collective-permute-start.4 = (bf16[896,256]{1,0:T(8,128)(2,1)}, bf16[896,256]{1,0:T(8,128)(2,1)S(1)}, u32[]{:S(2)}, u32[]{:S(2)}) collective-permute-start(bf16[896,256]{1,0:T(8,128)(2,1)} %cm_ref.1), channel_id=1, source_target_pairs={{0,1},{1,0},{2,3},{3,2},{4,5},{5,4},{6,7},{7,6},{8,9},{9,8},{10,11... | collective-permute-start | bytes 1376264 | tf_op jit(solution)/shard_map/ppermute | solution.py:515
  16.7 9.5 %collective-permute-start.1 = (s32[1,896]{1,0:T(1,128)S(1)}, s32[1,896]{1,0:T(1,128)S(1)}, u32[]{:S(2)}, u32[]{:S(2)}) collective-permute-start(s32[1,896]{1,0:T(1,128)S(1)} %broadcast_in_dim.2.ids_ref.id1), channel_id=1, source_target_pairs={{30,0},{0,2},{2,4},{4,6},{6,8},{8,10},{10,12},{12,14},{14,16},{16,... | collective-permute-start | bytes 10760 | tf_op jit(solution)/shard_map/ppermute | solution.py:510
  16.8 9.5 %collective-permute-start.5 = (s32[1,896]{1,0:T(1,128)S(1)}, s32[1,896]{1,0:T(1,128)S(1)}, u32[]{:S(2)}, u32[]{:S(2)}) collective-permute-start(s32[1,896]{1,0:T(1,128)S(1)} %broadcast_in_dim.2.ids_ref.id1), channel_id=1, source_target_pairs={{2,0},{4,2},{6,4},{8,6},{10,8},{12,10},{14,12},{16,14},{18,16},{20... | collective-permute-start | bytes 10760 | tf_op jit(solution)/shard_map/ppermute | solution.py:510
  50.0 16.7 %collective-permute-start.12 = (bf16[512,512]{1,0:T(8,128)(2,1)S(1)}, bf16[512,512]{1,0:T(8,128)(2,1)S(1)}, u32[]{:S(2)}, u32[]{:S(2)}) collective-permute-start(bf16[512,512]{1,0:T(8,128)(2,1)S(1)} %broadcast_select_fusion), channel_id=1, source_target_pairs={{0,4},{2,6},{4,0},{6,2},{8,12},{10,14},{12,8},{14,10},{16,20},{18,... | collective-permute-start | bytes 1572872 | tf_op jit(solution)/shard_map/ppermute | solution.py:515
  53.1 14.0 %collective-permute-start.11 = (bf16[512,512]{1,0:T(8,128)(2,1)S(1)}, bf16[512,512]{1,0:T(8,128)(2,1)S(1)}, u32[]{:S(2)}, u32[]{:S(2)}) collective-permute-start(bf16[512,512]{1,0:T(8,128)(2,1)S(1)} %broadcast_select_fusion.1), channel_id=1, source_target_pairs={{0,2},{2,0},{4,6},{6,4},{8,10},{10,8},{12,14},{14,12},{16,18},{18,... | collective-permute-start | bytes 1572872 | tf_op jit(solution)/shard_map/ppermute | solution.py:515
  67.3 8.0 %collective-permute-start.14 = (bf16[256,512]{1,0:T(8,128)(2,1)S(1)}, bf16[256,512]{1,0:T(8,128)(2,1)S(1)}, u32[]{:S(2)}, u32[]{:S(2)}) collective-permute-start(bf16[256,512]{1,0:T(8,128)(2,1)S(1)} %broadcast_select_fusion.5), channel_id=1, source_target_pairs={{0,2},{2,0},{4,6},{6,4},{8,10},{10,8},{12,14},{14,12},{16,18},{18,... | collective-permute-start | bytes 786440 | tf_op jit(solution)/shard_map/ppermute | solution.py:515
  69.1 7.7 %collective-permute-start.13 = (bf16[256,512]{1,0:T(8,128)(2,1)S(1)}, bf16[256,512]{1,0:T(8,128)(2,1)S(1)}, u32[]{:S(2)}, u32[]{:S(2)}) collective-permute-start(bf16[256,512]{1,0:T(8,128)(2,1)S(1)} %broadcast_select_fusion.3), channel_id=1, source_target_pairs={{0,4},{2,6},{4,0},{6,2},{8,12},{10,14},{12,8},{14,10},{16,20},{18,... | collective-permute-start | bytes 786440 | tf_op jit(solution)/shard_map/ppermute | solution.py:515
  74.2 17.4 %collective-permute-start.18 = (bf16[2688,256]{1,0:T(8,128)(2,1)S(1)}, bf16[2688,256]{1,0:T(8,128)(2,1)S(1)}, u32[]{:S(2)}, u32[]{:S(2)}) collective-permute-start(bf16[2688,256]{1,0:T(8,128)(2,1)S(1)} %get-tuple-element.162), channel_id=1, source_target_pairs={{0,1},{1,0},{2,3},{3,2},{4,5},{5,4},{6,7},{7,6},{8,9},{9,8},{10,11... | collective-permute-start | bytes 4128776 | tf_op jit(solution)/shard_map/ppermute | solution.py:515
  78.4 13.2 %collective-permute-start.15 = (bf16[256,512]{1,0:T(8,128)(2,1)S(1)}, bf16[256,512]{1,0:T(8,128)(2,1)S(1)}, u32[]{:S(2)}, u32[]{:S(2)}) collective-permute-start(bf16[256,512]{1,0:T(8,128)(2,1)S(1)} %broadcast_select_fusion.4), channel_id=1, source_target_pairs={{0,2},{2,0},{4,6},{6,4},{8,10},{10,8},{12,14},{14,12},{16,18},{18,... | collective-permute-start | bytes 786440 | tf_op jit(solution)/shard_map/ppermute | solution.py:515
  79.0 12.6 %collective-permute-start.16 = (bf16[256,512]{1,0:T(8,128)(2,1)S(1)}, bf16[256,512]{1,0:T(8,128)(2,1)S(1)}, u32[]{:S(2)}, u32[]{:S(2)}) collective-permute-start(bf16[256,512]{1,0:T(8,128)(2,1)S(1)} %broadcast_select_fusion.2), channel_id=1, source_target_pairs={{0,4},{2,6},{4,0},{6,2},{8,12},{10,14},{12,8},{14,10},{16,20},{18,... | collective-permute-start | bytes 786440 | tf_op jit(solution)/shard_map/ppermute | solution.py:515
  80.5 11.1 %collective-permute-start.20 = (bf16[128,512]{1,0:T(8,128)(2,1)S(1)}, bf16[128,512]{1,0:T(8,128)(2,1)S(1)}, u32[]{:S(2)}, u32[]{:S(2)}) collective-permute-start(bf16[128,512]{1,0:T(8,128)(2,1)S(1)} %get-tuple-element.164), channel_id=1, source_target_pairs={{0,16},{2,18},{4,20},{6,22},{8,24},{10,26},{12,28},{14,30},{16,0},... | collective-permute-start | bytes 393224 | tf_op jit(solution)/shard_map/ppermute | solution.py:515
  83.1 8.5 %collective-permute-start.21 = (bf16[128,512]{1,0:T(8,128)(2,1)S(1)}, bf16[128,512]{1,0:T(8,128)(2,1)S(1)}, u32[]{:S(2)}, u32[]{:S(2)}) collective-permute-start(bf16[128,512]{1,0:T(8,128)(2,1)S(1)} %get-tuple-element.165), channel_id=1, source_target_pairs={{0,24},{2,26},{4,28},{6,30},{8,16},{10,18},{12,20},{14,22},{16,8},... | collective-permute-start | bytes 393224 | tf_op jit(solution)/shard_map/ppermute | solution.py:515
  92.4 13.2 %collective-permute-start.24 = (bf16[128,512]{1,0:T(8,128)(2,1)S(1)}, bf16[128,512]{1,0:T(8,128)(2,1)S(1)}, u32[]{:S(2)}, u32[]{:S(2)}) collective-permute-start(bf16[128,512]{1,0:T(8,128)(2,1)S(1)} %add_convert_fusion.9), channel_id=1, source_target_pairs={{0,8},{2,10},{4,12},{6,14},{8,0},{10,2},{12,4},{14,6},{16,24},{18,... | collective-permute-start | bytes 393224 | tf_op jit(solution)/shard_map/ppermute | solution.py:515
  94.4 12.1 %collective-permute-start.25 = (bf16[128,512]{1,0:T(8,128)(2,1)S(1)}, bf16[128,512]{1,0:T(8,128)(2,1)S(1)}, u32[]{:S(2)}, u32[]{:S(2)}) collective-permute-start(bf16[128,512]{1,0:T(8,128)(2,1)S(1)} %add_convert_fusion.9), channel_id=1, source_target_pairs={{0,16},{2,18},{4,20},{6,22},{8,24},{10,26},{12,28},{14,30},{16,0},... | collective-permute-start | bytes 393224 | tf_op jit(solution)/shard_map/ppermute | solution.py:515
  95.9 10.6 %collective-permute-start.26 = (bf16[128,512]{1,0:T(8,128)(2,1)S(1)}, bf16[128,512]{1,0:T(8,128)(2,1)S(1)}, u32[]{:S(2)}, u32[]{:S(2)}) collective-permute-start(bf16[128,512]{1,0:T(8,128)(2,1)S(1)} %add_convert_fusion.9), channel_id=1, source_target_pairs={{0,24},{2,26},{4,28},{6,30},{8,16},{10,18},{12,20},{14,22},{16,8},... | collective-permute-start | bytes 393224 | tf_op jit(solution)/shard_map/ppermute | solution.py:515
  98.7 6.9 %collective-permute-start.23 = (bf16[128,512]{1,0:T(8,128)(2,1)S(1)}, bf16[128,512]{1,0:T(8,128)(2,1)S(1)}, u32[]{:S(2)}, u32[]{:S(2)}) collective-permute-start(bf16[128,512]{1,0:T(8,128)(2,1)S(1)} %broadcast_select_fusion.6), channel_id=1, source_target_pairs={{0,2},{2,0},{4,6},{6,4},{8,10},{10,8},{12,14},{14,12},{16,18},{18,... | collective-permute-start | bytes 393224 | tf_op jit(solution)/shard_map/ppermute | solution.py:515
  102.3 24.0 %collective-permute-start.30 = (bf16[896,256]{1,0:T(8,128)(2,1)S(1)}, bf16[896,256]{1,0:T(8,128)(2,1)S(1)}, u32[]{:S(2)}, u32[]{:S(2)}) collective-permute-start(bf16[896,256]{1,0:T(8,128)(2,1)S(1)} %get-tuple-element.194), channel_id=1, source_target_pairs={{2,0},{4,2},{6,4},{8,6},{10,8},{12,10},{14,12},{16,14},{18,16},{20... | collective-permute-start | bytes 1376264 | tf_op jit(solution)/shard_map/ppermute | solution.py:510
  105.6 20.7 %collective-permute-start.31 = (bf16[896,256]{1,0:T(8,128)(2,1)S(1)}, bf16[896,256]{1,0:T(8,128)(2,1)S(1)}, u32[]{:S(2)}, u32[]{:S(2)}) collective-permute-start(bf16[896,256]{1,0:T(8,128)(2,1)S(1)} %get-tuple-element.195), channel_id=1, source_target_pairs={{30,0},{0,2},{2,4},{4,6},{6,8},{8,10},{10,12},{12,14},{14,16},{16,... | collective-permute-start | bytes 1376264 | tf_op jit(solution)/shard_map/ppermute | solution.py:510
  106.9 14.2 %collective-permute-start.27 = (bf16[72,512]{1,0:T(8,128)(2,1)S(1)}, bf16[72,512]{1,0:T(8,128)(2,1)S(1)}, u32[]{:S(2)}, u32[]{:S(2)}) collective-permute-start(bf16[72,512]{1,0:T(8,128)(2,1)S(1)} %get-tuple-element.188), channel_id=1, source_target_pairs={{0,8},{2,10},{4,12},{6,14},{8,0},{10,2},{12,4},{14,6},{16,24},{18,... | collective-permute-start | bytes 221192 | tf_op jit(solution)/shard_map/ppermute | solution.py:515
  117.7 8.5 %collective-permute-start.28 = (bf16[72,512]{1,0:T(8,128)(2,1)S(1)}, bf16[72,512]{1,0:T(8,128)(2,1)S(1)}, u32[]{:S(2)}, u32[]{:S(2)}) collective-permute-start(bf16[72,512]{1,0:T(8,128)(2,1)S(1)} %get-tuple-element.189), channel_id=1, source_target_pairs={{0,16},{2,18},{4,20},{6,22},{8,24},{10,26},{12,28},{14,30},{16,0},... | collective-permute-start | bytes 221192 | tf_op jit(solution)/shard_map/ppermute | solution.py:515
  126.3 8.2 %collective-permute-start.34 = (bf16[72,512]{1,0:T(8,128)(2,1)S(1)}, bf16[72,512]{1,0:T(8,128)(2,1)S(1)}, u32[]{:S(2)}, u32[]{:S(2)}) collective-permute-start(bf16[72,512]{1,0:T(8,128)(2,1)S(1)} %add_convert_fusion.10), channel_id=1, source_target_pairs={{0,8},{2,10},{4,12},{6,14},{8,0},{10,2},{12,4},{14,6},{16,24},{18,... | collective-permute-start | bytes 221192 | tf_op jit(solution)/shard_map/ppermute | solution.py:515
  127.7 7.3 %collective-permute-start.35 = (bf16[72,512]{1,0:T(8,128)(2,1)S(1)}, bf16[72,512]{1,0:T(8,128)(2,1)}, u32[]{:S(2)}, u32[]{:S(2)}) collective-permute-start(bf16[72,512]{1,0:T(8,128)(2,1)S(1)} %add_convert_fusion.10), channel_id=1, source_target_pairs={{0,16},{2,18},{4,20},{6,22},{8,24},{10,26},{12,28},{14,30},{16,0},... | collective-permute-start | bytes 221192 | tf_op jit(solution)/shard_map/ppermute | solution.py:515
  134.5 23.7 %collective-permute-start.9 = (bf16[896,256]{1,0:T(8,128)(2,1)S(1)}, bf16[896,256]{1,0:T(8,128)(2,1)S(1)}, u32[]{:S(2)}, u32[]{:S(2)}) collective-permute-start(bf16[896,256]{1,0:T(8,128)(2,1)S(1)} %get-tuple-element.130), channel_id=1, source_target_pairs={{0,1},{1,0},{2,3},{3,2},{4,5},{5,4},{6,7},{7,6},{8,9},{9,8},{10,11... | collective-permute-start | bytes 1376264 | tf_op jit(solution)/shard_map/ppermute | solution.py:515
  138.4 17.5 %collective-permute-start.37 = (bf16[512,512]{1,0:T(8,128)(2,1)S(1)}, bf16[512,512]{1,0:T(8,128)(2,1)S(1)}, u32[]{:S(2)}, u32[]{:S(2)}) collective-permute-start(bf16[512,512]{1,0:T(8,128)(2,1)S(1)} %pad_maximum_fusion.1), channel_id=1, source_target_pairs={{0,2},{2,0},{4,6},{6,4},{8,10},{10,8},{12,14},{14,12},{16,18},{18,... | collective-permute-start | bytes 1572872 | tf_op jit(solution)/shard_map/ppermute | solution.py:515
  138.7 17.1 %collective-permute-start.38 = (bf16[512,512]{1,0:T(8,128)(2,1)S(1)}, bf16[512,512]{1,0:T(8,128)(2,1)S(1)}, u32[]{:S(2)}, u32[]{:S(2)}) collective-permute-start(bf16[512,512]{1,0:T(8,128)(2,1)S(1)} %pad_maximum_fusion.2), channel_id=1, source_target_pairs={{0,4},{2,6},{4,0},{6,2},{8,12},{10,14},{12,8},{14,10},{16,20},{18,... | collective-permute-start | bytes 1572872 | tf_op jit(solution)/shard_map/ppermute | solution.py:515
  140.5 15.3 %collective-permute-start.39 = (bf16[160,512]{1,0:T(8,128)(2,1)S(1)}, bf16[160,512]{1,0:T(8,128)(2,1)S(1)}, u32[]{:S(2)}, u32[]{:S(2)}) collective-permute-start(bf16[160,512]{1,0:T(8,128)(2,1)S(1)} %fusion.8.c), channel_id=1, source_target_pairs={{0,4},{2,6},{4,0},{6,2},{8,12},{10,14},{12,8},{14,10},{16,20},{18,... | collective-permute-start | bytes 491528 | tf_op jit(solution)/shard_map/ppermute | solution.py:515
  140.7 12.6 %collective-permute-start.40 = (bf16[128,512]{1,0:T(8,128)(2,1)S(1)}, bf16[128,512]{1,0:T(8,128)(2,1)S(1)}, u32[]{:S(2)}, u32[]{:S(2)}) collective-permute-start(bf16[128,512]{1,0:T(8,128)(2,1)S(1)} %pad_maximum_fusion.8.d), channel_id=1, source_target_pairs={{0,2},{2,0},{4,6},{6,4},{8,10},{10,8},{12,14},{14,12},{16,18},{18,... | collective-permute-start | bytes 393224 | tf_op jit(solution)/shard_map/ppermute | solution.py:515
  155.9 7.2 %collective-permute-start.42 = (bf16[256,512]{1,0:T(8,128)(2,1)S(1)}, bf16[256,512]{1,0:T(8,128)(2,1)S(1)}, u32[]{:S(2)}, u32[]{:S(2)}) collective-permute-start(bf16[256,512]{1,0:T(8,128)(2,1)S(1)} %pad_maximum_fusion.7), channel_id=1, source_target_pairs={{0,4},{2,6},{4,0},{6,2},{8,12},{10,14},{12,8},{14,10},{16,20},{18,... | collective-permute-start | bytes 786440 | tf_op jit(solution)/shard_map/ppermute | solution.py:515
  157.7 7.5 %collective-permute-start.41 = (bf16[288,512]{1,0:T(8,128)(2,1)S(1)}, bf16[288,512]{1,0:T(8,128)(2,1)S(1)}, u32[]{:S(2)}, u32[]{:S(2)}) collective-permute-start(bf16[288,512]{1,0:T(8,128)(2,1)S(1)} %pad_maximum_fusion.3), channel_id=1, source_target_pairs={{0,2},{2,0},{4,6},{6,4},{8,10},{10,8},{12,14},{14,12},{16,18},{18,... | collective-permute-start | bytes 884744 | tf_op jit(solution)/shard_map/ppermute | solution.py:515
  (29 other events, 180.2 us)

commit v6 on v5

--- a/solution.py
+++ b/solution.py
@@ -166,7 +166,6 @@
         scores = dot(k_all[pl.ds(start, window), :], both, 1, 1)
         old = top_old[:1, :]
         top = None
-        total = jnp.zeros((WORD, 2 * ROWS), f32)
         weights = []
         for t in range(window // WORD):
             there = slice(t * WORD, (t + 1) * WORD)
@@ -178,10 +177,9 @@
             top = part if top is None else jnp.maximum(top, part)
             s_new[there, :] = part
             weight = jnp.exp2(s_old[there, :] * scale - old)
-            total = total + weight
             weights.append(weight.astype(bf16))
-        inverse = 1.0 / jnp.sum(total, axis=0, keepdims=True)
         weights = jnp.concatenate(weights, 0)
+        inverse = 1.0 / dot(jnp.ones((16, window), bf16), weights, 1, 0)[:1, :]
         e_ref[old_block] = weights
         there = pl.ds(old_start, ROWS)
         inv_ref[0:1, there] = inverse[:, :ROWS]

time: 167 us -> 167 us (level)
  no operation moved by 1% of the time
where the time goes in v6:
time: 167 us
  starting transfers between devices  63.2 us (38%)
  Pallas kernels  41.7 us (25%)
  waiting for transfers between devices  38 us (23%)
  other arithmetic  8.17 us (5%)
  matrix products  6.08 us (4%)
  local copies, waits for them, and re-layouts  5.67 us (3%)
  blocking collectives  2.46 us (1%)
    ppermute x37, starting transfers between devices, swapped(): return lax.ppermute(block, axis, [(i, i ^ bit) for i in devices])  47.6 us
    pallas_call x10, Pallas kernels, call(): pl.pallas_call(kernel, in_specs=[pl.BlockSpec(memory_space=space) for spa...  41.7 us
    ppermute x37, waiting for transfers between devices, swapped(): return lax.ppermute(block, axis, [(i, i ^ bit) for i in devices])  35.4 us
    ppermute x6, starting transfers between devices, passed_along(): return lax.ppermute(block, axis, route)  15.6 us
    dot_general x7, matrix products, dot(): lax.dot_general(left, right, (((left_dim,), (right_dim,)), ((), ())), pre...  5.5 us
    unnamed x36, local copies, waits for them, and re-layouts  4.84 us
  transfers between devices with their start and end apart: 43, of which 19 were waited for; matrix products, arithmetic and copies ran while one was open for 8% of the time, Pallas kernels for 15%

profile of v6, /device:TPU:0, one launch (start us, length us, event | category | flops | bytes accessed | tf_op | source)
XLA Modules:
  0.0 166.6 jit_solution(2303825021080287150)
XLA Ops:
  1.2 2.6 %collective-permute-start.2 = (bf16[896,256]{1,0:T(8,128)(2,1)}, bf16[896,256]{1,0:T(8,128)(2,1)S(1)}, u32[]{:S(2)}, u32[]{:S(2)}) collective-permute-start(bf16[896,256]{1,0:T(8,128)(2,1)} %xm_ref.1), channel_id=1, source_target_pairs={{30,0},{0,2},{2,4},{4,6},{6,8},{8,10},{10,12},{12,14},{14,16},{16,... | collective-permute-start | bytes 1376264 | tf_op jit(solution)/shard_map/ppermute | solution.py:508
  3.7 4.1 %collective-permute-start.3 = (bf16[896,256]{1,0:T(8,128)(2,1)}, bf16[896,256]{1,0:T(8,128)(2,1)S(1)}, u32[]{:S(2)}, u32[]{:S(2)}) collective-permute-start(bf16[896,256]{1,0:T(8,128)(2,1)} %xm_ref.1), channel_id=1, source_target_pairs={{2,0},{4,2},{6,4},{8,6},{10,8},{12,10},{14,12},{16,14},{18,16},{20... | collective-permute-start | bytes 1376264 | tf_op jit(solution)/shard_map/ppermute | solution.py:508
  14.2 2.4 %front.3 = (bf16[896,512]{1,0:T(8,128)(2,1)S(1)}, bf16[896,512]{1,0:T(8,128)(2,1)S(1)}, bf16[896,256]{1,0:T(8,128)(2,1)S(1)}, bf16[256,896]{1,0:T(8,128)(2,1)S(1...) custom-call(s32[1]{0:T(128)} %bitcast.head_ref, ...), custom_call_target="tpu_custom_call" | custom-call | flops 5249999872 | bytes 26250000 | tf_op jit(solution)/shard_map/front/pallas_call | solution.py:94
  16.8 5.6 %collective-permute-start.5 = (s32[1,896]{1,0:T(1,128)S(1)}, s32[1,896]{1,0:T(1,128)S(1)}, u32[]{:S(2)}, u32[]{:S(2)}) collective-permute-start(s32[1,896]{1,0:T(1,128)S(1)} %broadcast_in_dim.2.ids_ref.id1), channel_id=1, source_target_pairs={{2,0},{4,2},{6,4},{8,6},{10,8},{12,10},{14,12},{16,14},{18,16},{20... | collective-permute-start | bytes 10760 | tf_op jit(solution)/shard_map/ppermute | solution.py:508
  24.4 1.8 %collective-permute-done.3.mine_ref = bf16[896,256]{1,0:T(8,128)(2,1)S(1)} collective-permute-done((bf16[896,256]{1,0:T(8,128)(2,1)}, bf16[896,256]{1,0:T(8,128)(2,1)S(1)}, u32[]{:S(2)}, u32[]{:S(2)}) %collective-permute-start.3) | collective-permute-done | bytes 458784 | tf_op jit(solution)/shard_map/ppermute | solution.py:508
  31.1 10.1 %attend_forward.1 = (bf16[7,1920,256]{2,1,0:T(8,128)(2,1)S(1)}, bf16[256,896]{1,0:T(8,128)(2,1)S(1)}, f32[8,896]{1,0:T(8,128)S(1)}, bf16[896,512]{1,0:T(8,128)(2,1)S(1)}) custom-call(s32[16,896]{1,0:T(8,128)S(1)} %add_select_fusion.nbr_ref, bf16[896,256]{1,0:T(8,128)(2,1)S(1)} %get-tuple-element.120.k0, bf16[896,256]{1,0:T(8,128)(2,1)S(1)} %get-tuple-element.121.k1, ...), custom_call_target="tpu_custom_call" | custom-call | flops 17500000256 | bytes 87500000 | tf_op jit(solution)/shard_map/attend_forward/pallas_call | solution.py:94
  43.8 4.4 %mlp.1 = (f32[896,512]{1,0:T(8,128)S(1)}, bf16[896,512]{1,0:T(8,128)(2,1)S(1)}, bf16[896,256]{1,0:T(8,128)(2,1)S(1)}, f32[896,256]{1,0:T(8,128)S(1)}, bf16[896,5...) custom-call(s32[1]{0:T(128)} %bitcast.head_ref, ...), custom_call_target="tpu_custom_call" | custom-call | flops 5249999872 | bytes 26250000 | tf_op jit(solution)/shard_map/mlp/pallas_call | solution.py:94
  49.8 1.8 %collective-permute-start.12 = (bf16[512,512]{1,0:T(8,128)(2,1)S(1)}, bf16[512,512]{1,0:T(8,128)(2,1)S(1)}, u32[]{:S(2)}, u32[]{:S(2)}) collective-permute-start(bf16[512,512]{1,0:T(8,128)(2,1)S(1)} %broadcast_select_fusion), channel_id=1, source_target_pairs={{0,4},{2,6},{4,0},{6,2},{8,12},{10,14},{12,8},{14,10},{16,20},{18,... | collective-permute-start | bytes 1572872 | tf_op jit(solution)/shard_map/ppermute | solution.py:513
  53.3 2.5 %branch.1 = (f32[896,256]{1,0:T(8,128)S(1)}, bf16[256,512]{1,0:T(8,128)(2,1)S(1)}, f32[16,512]{1,0:T(8,128)S(1)}, bf16[256,896]{1,0:T(8,128)(2,1)S(1)}, f32[8,896]{1,0:T(8,128)S(1)}) custom-call(s32[1]{0:T(128)} %bitcast.head_ref, s32[1,896]{1,0:T(1,128)S(1)} %broadcast_in_dim.2.ids_ref.id1, f32[896,512]{1,0:T(8,128)S(1)} %get-tuple-element.132.middle_ref, ...), custom_call_target="tpu_custom_call" | custom-call | flops 3150000128 | bytes 15750000 | tf_op jit(solution)/shard_map/branch/pallas_call | solution.py:94
  55.8 10.8 %attend_backward.1 = (bf16[2688,512]{1,0:T(8,128)(2,1)S(1)}, bf16[896,256]{1,0:T(8,128)(2,1)S(1)}) custom-call(bf16[7,1920,256]{2,1,0:T(8,128)(2,1)S(1)} %get-tuple-element.131.e_ref, bf16[256,896]{1,0:T(8,128)(2,1)S(1)} %get-tuple-element.140.grad_ref, f32[8,896]{1,0:T(8,128)S(1)} %get-tuple-element.141.cross_ref, ...), custom_call_target="tpu_custom_call" | custom-call | flops 33600000000 | bytes 168000000 | tf_op jit(solution)/shard_map/attend_backward/pallas_call | solution.py:94
  67.2 1.7 %collective-permute-start.14 = (bf16[256,512]{1,0:T(8,128)(2,1)S(1)}, bf16[256,512]{1,0:T(8,128)(2,1)S(1)}, u32[]{:S(2)}, u32[]{:S(2)}) collective-permute-start(bf16[256,512]{1,0:T(8,128)(2,1)S(1)} %broadcast_select_fusion.5), channel_id=1, source_target_pairs={{0,2},{2,0},{4,6},{6,4},{8,10},{10,8},{12,14},{14,12},{16,18},{18,... | collective-permute-start | bytes 786440 | tf_op jit(solution)/shard_map/ppermute | solution.py:513
  69.2 4.7 %grads.1 = (bf16[512,256]{1,0:T(8,128)(2,1)S(1)}, bf16[512,512]{1,0:T(8,128)(2,1)S(1)}, bf16[2688,256]{1,0:T(8,128)(2,1)S(1)}, bf16[2688,256]{1,0:T(8,128)(2,1)S...) custom-call(s32[1]{0:T(128)} %bitcast.head_ref, bf16[2688,512]{1,0:T(8,128)(2,1)S(1)} %get-tuple-element.146.dkv_ref, ...), custom_call_target="tpu_custom_call" | custom-call | flops 8750000128 | bytes 43750000 | tf_op jit(solution)/shard_map/grads/pallas_call | solution.py:94
  80.3 2.6 %collective-permute-start.20 = (bf16[128,512]{1,0:T(8,128)(2,1)S(1)}, bf16[128,512]{1,0:T(8,128)(2,1)S(1)}, u32[]{:S(2)}, u32[]{:S(2)}) collective-permute-start(bf16[128,512]{1,0:T(8,128)(2,1)S(1)} %get-tuple-element.164), channel_id=1, source_target_pairs={{0,16},{2,18},{4,20},{6,22},{8,24},{10,26},{12,28},{14,30},{16,0},... | collective-permute-start | bytes 393224 | tf_op jit(solution)/shard_map/ppermute | solution.py:513
  83.0 3.0 %collective-permute-start.21 = (bf16[128,512]{1,0:T(8,128)(2,1)S(1)}, bf16[128,512]{1,0:T(8,128)(2,1)S(1)}, u32[]{:S(2)}, u32[]{:S(2)}) collective-permute-start(bf16[128,512]{1,0:T(8,128)(2,1)S(1)} %get-tuple-element.165), channel_id=1, source_target_pairs={{0,24},{2,26},{4,28},{6,30},{8,16},{10,18},{12,20},{14,22},{16,8},... | collective-permute-start | bytes 393224 | tf_op jit(solution)/shard_map/ppermute | solution.py:513
  86.5 5.0 %collective-permute-done.20 = bf16[128,512]{1,0:T(8,128)(2,1)S(1)} collective-permute-done((bf16[128,512]{1,0:T(8,128)(2,1)S(1)}, bf16[128,512]{1,0:T(8,128)(2,1)S(1)}, u32[]{:S(2)}, u32[]{:S(2)}) %collective-permute-start.20) | collective-permute-done | bytes 131104 | tf_op jit(solution)/shard_map/ppermute | solution.py:513
  92.2 2.0 %collective-permute-start.24 = (bf16[128,512]{1,0:T(8,128)(2,1)S(1)}, bf16[128,512]{1,0:T(8,128)(2,1)S(1)}, u32[]{:S(2)}, u32[]{:S(2)}) collective-permute-start(bf16[128,512]{1,0:T(8,128)(2,1)S(1)} %add_convert_fusion.9), channel_id=1, source_target_pairs={{0,8},{2,10},{4,12},{6,14},{8,0},{10,2},{12,4},{14,6},{16,24},{18,... | collective-permute-start | bytes 393224 | tf_op jit(solution)/shard_map/ppermute | solution.py:513
  94.3 1.5 collective-permute-start.25
  99.2 2.9 %collective-permute-done.22 = bf16[128,512]{1,0:T(8,128)(2,1)S(1)} collective-permute-done((bf16[128,512]{1,0:T(8,128)(2,1)S(1)}, bf16[128,512]{1,0:T(8,128)(2,1)S(1)}, u32[]{:S(2)}, u32[]{:S(2)}) %collective-permute-start.22) | collective-permute-done | bytes 131104 | tf_op jit(solution)/shard_map/ppermute | solution.py:513
  102.1 3.3 %collective-permute-start.30 = (bf16[896,256]{1,0:T(8,128)(2,1)S(1)}, bf16[896,256]{1,0:T(8,128)(2,1)S(1)}, u32[]{:S(2)}, u32[]{:S(2)}) collective-permute-start(bf16[896,256]{1,0:T(8,128)(2,1)S(1)} %get-tuple-element.194), channel_id=1, source_target_pairs={{2,0},{4,2},{6,4},{8,6},{10,8},{12,10},{14,12},{16,14},{18,16},{20... | collective-permute-start | bytes 1376264 | tf_op jit(solution)/shard_map/ppermute | solution.py:508
  106.7 10.9 %collective-permute-start.27 = (bf16[72,512]{1,0:T(8,128)(2,1)S(1)}, bf16[72,512]{1,0:T(8,128)(2,1)S(1)}, u32[]{:S(2)}, u32[]{:S(2)}) collective-permute-start(bf16[72,512]{1,0:T(8,128)(2,1)S(1)} %get-tuple-element.188), channel_id=1, source_target_pairs={{0,8},{2,10},{4,12},{6,14},{8,0},{10,2},{12,4},{14,6},{16,24},{18,... | collective-permute-start | bytes 221192 | tf_op jit(solution)/shard_map/ppermute | solution.py:513
  117.6 2.0 %collective-permute-start.28 = (bf16[72,512]{1,0:T(8,128)(2,1)S(1)}, bf16[72,512]{1,0:T(8,128)(2,1)S(1)}, u32[]{:S(2)}, u32[]{:S(2)}) collective-permute-start(bf16[72,512]{1,0:T(8,128)(2,1)S(1)} %get-tuple-element.189), channel_id=1, source_target_pairs={{0,16},{2,18},{4,20},{6,22},{8,24},{10,26},{12,28},{14,30},{16,0},... | collective-permute-start | bytes 221192 | tf_op jit(solution)/shard_map/ppermute | solution.py:513
  121.0 5.1 %collective-permute-done.28 = bf16[72,512]{1,0:T(8,128)(2,1)S(1)} collective-permute-done((bf16[72,512]{1,0:T(8,128)(2,1)S(1)}, bf16[72,512]{1,0:T(8,128)(2,1)S(1)}, u32[]{:S(2)}, u32[]{:S(2)}) %collective-permute-start.28) | collective-permute-done | bytes 73760 | tf_op jit(solution)/shard_map/ppermute | solution.py:513
  127.6 1.8 %collective-permute-start.35 = (bf16[72,512]{1,0:T(8,128)(2,1)S(1)}, bf16[72,512]{1,0:T(8,128)(2,1)}, u32[]{:S(2)}, u32[]{:S(2)}) collective-permute-start(bf16[72,512]{1,0:T(8,128)(2,1)S(1)} %add_convert_fusion.10), channel_id=1, source_target_pairs={{0,16},{2,18},{4,20},{6,22},{8,24},{10,26},{12,28},{14,30},{16,0},... | collective-permute-start | bytes 221192 | tf_op jit(solution)/shard_map/ppermute | solution.py:513
  131.8 2.5 %all-reduce = (f32[896]{0:T(1024)S(1)}, f32[896]{0:T(1024)S(1)}) all-reduce(f32[896]{0:T(1024)S(1)} %get-tuple-element.226, f32[896]{0:T(1024)S(1)} %get-tuple-element.225), channel_id=1, replica_groups=mesh['nodes'=16,'heads'=2] {'heads'}, use_global_device_ids=true, to_apply=%region_5.6 | all-reduce | flops 1792 | bytes 14336 | tf_op jit(solution)/shard_map/psum | solution.py:724
  138.3 2.0 %collective-permute-start.38 = (bf16[512,512]{1,0:T(8,128)(2,1)S(1)}, bf16[512,512]{1,0:T(8,128)(2,1)S(1)}, u32[]{:S(2)}, u32[]{:S(2)}) collective-permute-start(bf16[512,512]{1,0:T(8,128)(2,1)S(1)} %pad_maximum_fusion.2), channel_id=1, source_target_pairs={{0,4},{2,6},{4,0},{6,2},{8,12},{10,14},{12,8},{14,10},{16,20},{18,... | collective-permute-start | bytes 1572872 | tf_op jit(solution)/shard_map/ppermute | solution.py:513
  140.4 1.9 %collective-permute-start.40 = (bf16[128,512]{1,0:T(8,128)(2,1)S(1)}, bf16[128,512]{1,0:T(8,128)(2,1)S(1)}, u32[]{:S(2)}, u32[]{:S(2)}) collective-permute-start(bf16[128,512]{1,0:T(8,128)(2,1)S(1)} %pad_maximum_fusion.8.d), channel_id=1, source_target_pairs={{0,2},{2,0},{4,6},{6,4},{8,10},{10,8},{12,14},{14,12},{16,18},{18,... | collective-permute-start | bytes 393224 | tf_op jit(solution)/shard_map/ppermute | solution.py:513
  143.6 9.6 %collective-permute-done.40.d_near = bf16[128,512]{1,0:T(8,128)(2,1)S(1)} collective-permute-done((bf16[128,512]{1,0:T(8,128)(2,1)S(1)}, bf16[128,512]{1,0:T(8,128)(2,1)S(1)}, u32[]{:S(2)}, u32[]{:S(2)}) %collective-permute-start.40) | collective-permute-done | bytes 131104 | tf_op jit(solution)/shard_map/ppermute | solution.py:513
  153.2 2.4 %collective-permute-done.39.c_near = bf16[160,512]{1,0:T(8,128)(2,1)S(1)} collective-permute-done((bf16[160,512]{1,0:T(8,128)(2,1)S(1)}, bf16[160,512]{1,0:T(8,128)(2,1)S(1)}, u32[]{:S(2)}, u32[]{:S(2)}) %collective-permute-start.39) | collective-permute-done | bytes 163872 | tf_op jit(solution)/shard_map/ppermute | solution.py:513
  155.7 1.8 %collective-permute-start.42 = (bf16[256,512]{1,0:T(8,128)(2,1)S(1)}, bf16[256,512]{1,0:T(8,128)(2,1)S(1)}, u32[]{:S(2)}, u32[]{:S(2)}) collective-permute-start(bf16[256,512]{1,0:T(8,128)(2,1)S(1)} %pad_maximum_fusion.7), channel_id=1, source_target_pairs={{0,4},{2,6},{4,0},{6,2},{8,12},{10,14},{12,8},{14,10},{16,20},{18,... | collective-permute-start | bytes 786440 | tf_op jit(solution)/shard_map/ppermute | solution.py:513
  158.9 2.2 %unpack_mlp.1 = (f32[512,1024]{1,0:T(8,128)}, f32[1024,512]{1,0:T(8,128)}) custom-call(s32[1]{0:T(128)} %bitcast.5.x_ref, s32[1]{0:T(128)} %bitcast.6.y_ref, bf16[256,512]{1,0:T(8,128)(2,1)S(1)} %pad_maximum_fusion.5.a, bf16[256,512]{1,0:T(8,128)(2,1)S(1)} %collective-permute-done.32.a_near, bf16[512,512]{1,0:T(8,128)(2,1)S(1)} %collective-permute-done.37.a_far, ...), custom_call_target="tpu_custom_call" | custom-call | flops 1050000000 | bytes 5250000 | tf_op jit(solution)/shard_map/unpack_mlp/pallas_call | solution.py:94
  161.1 2.0 %collective-permute-done.42.d_far = bf16[256,512]{1,0:T(8,128)(2,1)S(1)} collective-permute-done((bf16[256,512]{1,0:T(8,128)(2,1)S(1)}, bf16[256,512]{1,0:T(8,128)(2,1)S(1)}, u32[]{:S(2)}, u32[]{:S(2)}) %collective-permute-start.42) | collective-permute-done | bytes 262176 | tf_op jit(solution)/shard_map/ppermute | solution.py:513
  163.1 2.0 %collective-permute-done.41.c_far = bf16[288,512]{1,0:T(8,128)(2,1)S(1)} collective-permute-done((bf16[288,512]{1,0:T(8,128)(2,1)S(1)}, bf16[288,512]{1,0:T(8,128)(2,1)S(1)}, u32[]{:S(2)}, u32[]{:S(2)}) %collective-permute-start.41) | collective-permute-done | bytes 294944 | tf_op jit(solution)/shard_map/ppermute | solution.py:513
  (161 shorter events, 46.2 us)
Async XLA Ops:
  0.6 8.8 %collective-permute-start = (bf16[896,256]{1,0:T(8,128)(2,1)}, bf16[896,256]{1,0:T(8,128)(2,1)S(1)}, u32[]{:S(2)}, u32[]{:S(2)}) collective-permute-start(bf16[896,256]{1,0:T(8,128)(2,1)} %xm_ref.1), channel_id=1, source_target_pairs={{0,1},{1,0},{2,3},{3,2},{4,5},{5,4},{6,7},{7,6},{8,9},{9,8},{10,11... | collective-permute-start | bytes 1376264 | tf_op jit(solution)/shard_map/ppermute | solution.py:513
  1.2 23.2 %collective-permute-start.2 = (bf16[896,256]{1,0:T(8,128)(2,1)}, bf16[896,256]{1,0:T(8,128)(2,1)S(1)}, u32[]{:S(2)}, u32[]{:S(2)}) collective-permute-start(bf16[896,256]{1,0:T(8,128)(2,1)} %xm_ref.1), channel_id=1, source_target_pairs={{30,0},{0,2},{2,4},{4,6},{6,8},{8,10},{10,12},{12,14},{14,16},{16,... | collective-permute-start | bytes 1376264 | tf_op jit(solution)/shard_map/ppermute | solution.py:508
  3.7 22.4 %collective-permute-start.3 = (bf16[896,256]{1,0:T(8,128)(2,1)}, bf16[896,256]{1,0:T(8,128)(2,1)S(1)}, u32[]{:S(2)}, u32[]{:S(2)}) collective-permute-start(bf16[896,256]{1,0:T(8,128)(2,1)} %xm_ref.1), channel_id=1, source_target_pairs={{2,0},{4,2},{6,4},{8,6},{10,8},{12,10},{14,12},{16,14},{18,16},{20... | collective-permute-start | bytes 1376264 | tf_op jit(solution)/shard_map/ppermute | solution.py:508
  7.8 14.6 %collective-permute-start.4 = (bf16[896,256]{1,0:T(8,128)(2,1)}, bf16[896,256]{1,0:T(8,128)(2,1)S(1)}, u32[]{:S(2)}, u32[]{:S(2)}) collective-permute-start(bf16[896,256]{1,0:T(8,128)(2,1)} %cm_ref.1), channel_id=1, source_target_pairs={{0,1},{1,0},{2,3},{3,2},{4,5},{5,4},{6,7},{7,6},{8,9},{9,8},{10,11... | collective-permute-start | bytes 1376264 | tf_op jit(solution)/shard_map/ppermute | solution.py:513
  16.7 9.5 %collective-permute-start.1 = (s32[1,896]{1,0:T(1,128)S(1)}, s32[1,896]{1,0:T(1,128)S(1)}, u32[]{:S(2)}, u32[]{:S(2)}) collective-permute-start(s32[1,896]{1,0:T(1,128)S(1)} %broadcast_in_dim.2.ids_ref.id1), channel_id=1, source_target_pairs={{30,0},{0,2},{2,4},{4,6},{6,8},{8,10},{10,12},{12,14},{14,16},{16,... | collective-permute-start | bytes 10760 | tf_op jit(solution)/shard_map/ppermute | solution.py:508
  16.8 9.5 %collective-permute-start.5 = (s32[1,896]{1,0:T(1,128)S(1)}, s32[1,896]{1,0:T(1,128)S(1)}, u32[]{:S(2)}, u32[]{:S(2)}) collective-permute-start(s32[1,896]{1,0:T(1,128)S(1)} %broadcast_in_dim.2.ids_ref.id1), channel_id=1, source_target_pairs={{2,0},{4,2},{6,4},{8,6},{10,8},{12,10},{14,12},{16,14},{18,16},{20... | collective-permute-start | bytes 10760 | tf_op jit(solution)/shard_map/ppermute | solution.py:508
  49.8 16.7 %collective-permute-start.12 = (bf16[512,512]{1,0:T(8,128)(2,1)S(1)}, bf16[512,512]{1,0:T(8,128)(2,1)S(1)}, u32[]{:S(2)}, u32[]{:S(2)}) collective-permute-start(bf16[512,512]{1,0:T(8,128)(2,1)S(1)} %broadcast_select_fusion), channel_id=1, source_target_pairs={{0,4},{2,6},{4,0},{6,2},{8,12},{10,14},{12,8},{14,10},{16,20},{18,... | collective-permute-start | bytes 1572872 | tf_op jit(solution)/shard_map/ppermute | solution.py:513
  53.0 14.0 %collective-permute-start.11 = (bf16[512,512]{1,0:T(8,128)(2,1)S(1)}, bf16[512,512]{1,0:T(8,128)(2,1)S(1)}, u32[]{:S(2)}, u32[]{:S(2)}) collective-permute-start(bf16[512,512]{1,0:T(8,128)(2,1)S(1)} %broadcast_select_fusion.1), channel_id=1, source_target_pairs={{0,2},{2,0},{4,6},{6,4},{8,10},{10,8},{12,14},{14,12},{16,18},{18,... | collective-permute-start | bytes 1572872 | tf_op jit(solution)/shard_map/ppermute | solution.py:513
  67.2 8.0 %collective-permute-start.14 = (bf16[256,512]{1,0:T(8,128)(2,1)S(1)}, bf16[256,512]{1,0:T(8,128)(2,1)S(1)}, u32[]{:S(2)}, u32[]{:S(2)}) collective-permute-start(bf16[256,512]{1,0:T(8,128)(2,1)S(1)} %broadcast_select_fusion.5), channel_id=1, source_target_pairs={{0,2},{2,0},{4,6},{6,4},{8,10},{10,8},{12,14},{14,12},{16,18},{18,... | collective-permute-start | bytes 786440 | tf_op jit(solution)/shard_map/ppermute | solution.py:513
  68.9 7.7 %collective-permute-start.13 = (bf16[256,512]{1,0:T(8,128)(2,1)S(1)}, bf16[256,512]{1,0:T(8,128)(2,1)S(1)}, u32[]{:S(2)}, u32[]{:S(2)}) collective-permute-start(bf16[256,512]{1,0:T(8,128)(2,1)S(1)} %broadcast_select_fusion.3), channel_id=1, source_target_pairs={{0,4},{2,6},{4,0},{6,2},{8,12},{10,14},{12,8},{14,10},{16,20},{18,... | collective-permute-start | bytes 786440 | tf_op jit(solution)/shard_map/ppermute | solution.py:513
  74.0 17.4 %collective-permute-start.18 = (bf16[2688,256]{1,0:T(8,128)(2,1)S(1)}, bf16[2688,256]{1,0:T(8,128)(2,1)S(1)}, u32[]{:S(2)}, u32[]{:S(2)}) collective-permute-start(bf16[2688,256]{1,0:T(8,128)(2,1)S(1)} %get-tuple-element.162), channel_id=1, source_target_pairs={{0,1},{1,0},{2,3},{3,2},{4,5},{5,4},{6,7},{7,6},{8,9},{9,8},{10,11... | collective-permute-start | bytes 4128776 | tf_op jit(solution)/shard_map/ppermute | solution.py:513
  78.2 13.2 %collective-permute-start.15 = (bf16[256,512]{1,0:T(8,128)(2,1)S(1)}, bf16[256,512]{1,0:T(8,128)(2,1)S(1)}, u32[]{:S(2)}, u32[]{:S(2)}) collective-permute-start(bf16[256,512]{1,0:T(8,128)(2,1)S(1)} %broadcast_select_fusion.4), channel_id=1, source_target_pairs={{0,2},{2,0},{4,6},{6,4},{8,10},{10,8},{12,14},{14,12},{16,18},{18,... | collective-permute-start | bytes 786440 | tf_op jit(solution)/shard_map/ppermute | solution.py:513
  78.8 12.6 %collective-permute-start.16 = (bf16[256,512]{1,0:T(8,128)(2,1)S(1)}, bf16[256,512]{1,0:T(8,128)(2,1)S(1)}, u32[]{:S(2)}, u32[]{:S(2)}) collective-permute-start(bf16[256,512]{1,0:T(8,128)(2,1)S(1)} %broadcast_select_fusion.2), channel_id=1, source_target_pairs={{0,4},{2,6},{4,0},{6,2},{8,12},{10,14},{12,8},{14,10},{16,20},{18,... | collective-permute-start | bytes 786440 | tf_op jit(solution)/shard_map/ppermute | solution.py:513
  80.3 11.1 %collective-permute-start.20 = (bf16[128,512]{1,0:T(8,128)(2,1)S(1)}, bf16[128,512]{1,0:T(8,128)(2,1)S(1)}, u32[]{:S(2)}, u32[]{:S(2)}) collective-permute-start(bf16[128,512]{1,0:T(8,128)(2,1)S(1)} %get-tuple-element.164), channel_id=1, source_target_pairs={{0,16},{2,18},{4,20},{6,22},{8,24},{10,26},{12,28},{14,30},{16,0},... | collective-permute-start | bytes 393224 | tf_op jit(solution)/shard_map/ppermute | solution.py:513
  83.0 8.5 %collective-permute-start.21 = (bf16[128,512]{1,0:T(8,128)(2,1)S(1)}, bf16[128,512]{1,0:T(8,128)(2,1)S(1)}, u32[]{:S(2)}, u32[]{:S(2)}) collective-permute-start(bf16[128,512]{1,0:T(8,128)(2,1)S(1)} %get-tuple-element.165), channel_id=1, source_target_pairs={{0,24},{2,26},{4,28},{6,30},{8,16},{10,18},{12,20},{14,22},{16,8},... | collective-permute-start | bytes 393224 | tf_op jit(solution)/shard_map/ppermute | solution.py:513
  92.2 13.3 %collective-permute-start.24 = (bf16[128,512]{1,0:T(8,128)(2,1)S(1)}, bf16[128,512]{1,0:T(8,128)(2,1)S(1)}, u32[]{:S(2)}, u32[]{:S(2)}) collective-permute-start(bf16[128,512]{1,0:T(8,128)(2,1)S(1)} %add_convert_fusion.9), channel_id=1, source_target_pairs={{0,8},{2,10},{4,12},{6,14},{8,0},{10,2},{12,4},{14,6},{16,24},{18,... | collective-permute-start | bytes 393224 | tf_op jit(solution)/shard_map/ppermute | solution.py:513
  94.3 12.1 %collective-permute-start.25 = (bf16[128,512]{1,0:T(8,128)(2,1)S(1)}, bf16[128,512]{1,0:T(8,128)(2,1)S(1)}, u32[]{:S(2)}, u32[]{:S(2)}) collective-permute-start(bf16[128,512]{1,0:T(8,128)(2,1)S(1)} %add_convert_fusion.9), channel_id=1, source_target_pairs={{0,16},{2,18},{4,20},{6,22},{8,24},{10,26},{12,28},{14,30},{16,0},... | collective-permute-start | bytes 393224 | tf_op jit(solution)/shard_map/ppermute | solution.py:513
  95.8 10.6 %collective-permute-start.26 = (bf16[128,512]{1,0:T(8,128)(2,1)S(1)}, bf16[128,512]{1,0:T(8,128)(2,1)S(1)}, u32[]{:S(2)}, u32[]{:S(2)}) collective-permute-start(bf16[128,512]{1,0:T(8,128)(2,1)S(1)} %add_convert_fusion.9), channel_id=1, source_target_pairs={{0,24},{2,26},{4,28},{6,30},{8,16},{10,18},{12,20},{14,22},{16,8},... | collective-permute-start | bytes 393224 | tf_op jit(solution)/shard_map/ppermute | solution.py:513
  98.6 6.9 %collective-permute-start.23 = (bf16[128,512]{1,0:T(8,128)(2,1)S(1)}, bf16[128,512]{1,0:T(8,128)(2,1)S(1)}, u32[]{:S(2)}, u32[]{:S(2)}) collective-permute-start(bf16[128,512]{1,0:T(8,128)(2,1)S(1)} %broadcast_select_fusion.6), channel_id=1, source_target_pairs={{0,2},{2,0},{4,6},{6,4},{8,10},{10,8},{12,14},{14,12},{16,18},{18,... | collective-permute-start | bytes 393224 | tf_op jit(solution)/shard_map/ppermute | solution.py:513
  102.1 24.0 %collective-permute-start.30 = (bf16[896,256]{1,0:T(8,128)(2,1)S(1)}, bf16[896,256]{1,0:T(8,128)(2,1)S(1)}, u32[]{:S(2)}, u32[]{:S(2)}) collective-permute-start(bf16[896,256]{1,0:T(8,128)(2,1)S(1)} %get-tuple-element.194), channel_id=1, source_target_pairs={{2,0},{4,2},{6,4},{8,6},{10,8},{12,10},{14,12},{16,14},{18,16},{20... | collective-permute-start | bytes 1376264 | tf_op jit(solution)/shard_map/ppermute | solution.py:508
  105.5 20.7 %collective-permute-start.31 = (bf16[896,256]{1,0:T(8,128)(2,1)S(1)}, bf16[896,256]{1,0:T(8,128)(2,1)S(1)}, u32[]{:S(2)}, u32[]{:S(2)}) collective-permute-start(bf16[896,256]{1,0:T(8,128)(2,1)S(1)} %get-tuple-element.195), channel_id=1, source_target_pairs={{30,0},{0,2},{2,4},{4,6},{6,8},{8,10},{10,12},{12,14},{14,16},{16,... | collective-permute-start | bytes 1376264 | tf_op jit(solution)/shard_map/ppermute | solution.py:508
  106.7 14.2 %collective-permute-start.27 = (bf16[72,512]{1,0:T(8,128)(2,1)S(1)}, bf16[72,512]{1,0:T(8,128)(2,1)S(1)}, u32[]{:S(2)}, u32[]{:S(2)}) collective-permute-start(bf16[72,512]{1,0:T(8,128)(2,1)S(1)} %get-tuple-element.188), channel_id=1, source_target_pairs={{0,8},{2,10},{4,12},{6,14},{8,0},{10,2},{12,4},{14,6},{16,24},{18,... | collective-permute-start | bytes 221192 | tf_op jit(solution)/shard_map/ppermute | solution.py:513
  117.6 8.5 %collective-permute-start.28 = (bf16[72,512]{1,0:T(8,128)(2,1)S(1)}, bf16[72,512]{1,0:T(8,128)(2,1)S(1)}, u32[]{:S(2)}, u32[]{:S(2)}) collective-permute-start(bf16[72,512]{1,0:T(8,128)(2,1)S(1)} %get-tuple-element.189), channel_id=1, source_target_pairs={{0,16},{2,18},{4,20},{6,22},{8,24},{10,26},{12,28},{14,30},{16,0},... | collective-permute-start | bytes 221192 | tf_op jit(solution)/shard_map/ppermute | solution.py:513
  126.1 8.2 %collective-permute-start.34 = (bf16[72,512]{1,0:T(8,128)(2,1)S(1)}, bf16[72,512]{1,0:T(8,128)(2,1)S(1)}, u32[]{:S(2)}, u32[]{:S(2)}) collective-permute-start(bf16[72,512]{1,0:T(8,128)(2,1)S(1)} %add_convert_fusion.10), channel_id=1, source_target_pairs={{0,8},{2,10},{4,12},{6,14},{8,0},{10,2},{12,4},{14,6},{16,24},{18,... | collective-permute-start | bytes 221192 | tf_op jit(solution)/shard_map/ppermute | solution.py:513
  127.6 7.1 %collective-permute-start.35 = (bf16[72,512]{1,0:T(8,128)(2,1)S(1)}, bf16[72,512]{1,0:T(8,128)(2,1)}, u32[]{:S(2)}, u32[]{:S(2)}) collective-permute-start(bf16[72,512]{1,0:T(8,128)(2,1)S(1)} %add_convert_fusion.10), channel_id=1, source_target_pairs={{0,16},{2,18},{4,20},{6,22},{8,24},{10,26},{12,28},{14,30},{16,0},... | collective-permute-start | bytes 221192 | tf_op jit(solution)/shard_map/ppermute | solution.py:513
  134.3 23.7 %collective-permute-start.9 = (bf16[896,256]{1,0:T(8,128)(2,1)S(1)}, bf16[896,256]{1,0:T(8,128)(2,1)S(1)}, u32[]{:S(2)}, u32[]{:S(2)}) collective-permute-start(bf16[896,256]{1,0:T(8,128)(2,1)S(1)} %get-tuple-element.130), channel_id=1, source_target_pairs={{0,1},{1,0},{2,3},{3,2},{4,5},{5,4},{6,7},{7,6},{8,9},{9,8},{10,11... | collective-permute-start | bytes 1376264 | tf_op jit(solution)/shard_map/ppermute | solution.py:513
  138.1 17.6 %collective-permute-start.37 = (bf16[512,512]{1,0:T(8,128)(2,1)S(1)}, bf16[512,512]{1,0:T(8,128)(2,1)S(1)}, u32[]{:S(2)}, u32[]{:S(2)}) collective-permute-start(bf16[512,512]{1,0:T(8,128)(2,1)S(1)} %pad_maximum_fusion.1), channel_id=1, source_target_pairs={{0,2},{2,0},{4,6},{6,4},{8,10},{10,8},{12,14},{14,12},{16,18},{18,... | collective-permute-start | bytes 1572872 | tf_op jit(solution)/shard_map/ppermute | solution.py:513
  138.3 17.4 %collective-permute-start.38 = (bf16[512,512]{1,0:T(8,128)(2,1)S(1)}, bf16[512,512]{1,0:T(8,128)(2,1)S(1)}, u32[]{:S(2)}, u32[]{:S(2)}) collective-permute-start(bf16[512,512]{1,0:T(8,128)(2,1)S(1)} %pad_maximum_fusion.2), channel_id=1, source_target_pairs={{0,4},{2,6},{4,0},{6,2},{8,12},{10,14},{12,8},{14,10},{16,20},{18,... | collective-permute-start | bytes 1572872 | tf_op jit(solution)/shard_map/ppermute | solution.py:513
  140.3 15.3 %collective-permute-start.39 = (bf16[160,512]{1,0:T(8,128)(2,1)S(1)}, bf16[160,512]{1,0:T(8,128)(2,1)S(1)}, u32[]{:S(2)}, u32[]{:S(2)}) collective-permute-start(bf16[160,512]{1,0:T(8,128)(2,1)S(1)} %fusion.8.c), channel_id=1, source_target_pairs={{0,4},{2,6},{4,0},{6,2},{8,12},{10,14},{12,8},{14,10},{16,20},{18,... | collective-permute-start | bytes 491528 | tf_op jit(solution)/shard_map/ppermute | solution.py:513
  140.4 12.9 %collective-permute-start.40 = (bf16[128,512]{1,0:T(8,128)(2,1)S(1)}, bf16[128,512]{1,0:T(8,128)(2,1)S(1)}, u32[]{:S(2)}, u32[]{:S(2)}) collective-permute-start(bf16[128,512]{1,0:T(8,128)(2,1)S(1)} %pad_maximum_fusion.8.d), channel_id=1, source_target_pairs={{0,2},{2,0},{4,6},{6,4},{8,10},{10,8},{12,14},{14,12},{16,18},{18,... | collective-permute-start | bytes 393224 | tf_op jit(solution)/shard_map/ppermute | solution.py:513
  155.7 7.4 %collective-permute-start.42 = (bf16[256,512]{1,0:T(8,128)(2,1)S(1)}, bf16[256,512]{1,0:T(8,128)(2,1)S(1)}, u32[]{:S(2)}, u32[]{:S(2)}) collective-permute-start(bf16[256,512]{1,0:T(8,128)(2,1)S(1)} %pad_maximum_fusion.7), channel_id=1, source_target_pairs={{0,4},{2,6},{4,0},{6,2},{8,12},{10,14},{12,8},{14,10},{16,20},{18,... | collective-permute-start | bytes 786440 | tf_op jit(solution)/shard_map/ppermute | solution.py:513
  157.6 7.6 %collective-permute-start.41 = (bf16[288,512]{1,0:T(8,128)(2,1)S(1)}, bf16[288,512]{1,0:T(8,128)(2,1)S(1)}, u32[]{:S(2)}, u32[]{:S(2)}) collective-permute-start(bf16[288,512]{1,0:T(8,128)(2,1)S(1)} %pad_maximum_fusion.3), channel_id=1, source_target_pairs={{0,2},{2,0},{4,6},{6,4},{8,10},{10,8},{12,14},{14,12},{16,18},{18,... | collective-permute-start | bytes 884744 | tf_op jit(solution)/shard_map/ppermute | solution.py:513
  (29 other events, 179.7 us)
